TPU v7x, 32 devices: a whole 2x2x4 slice. The times are simulated.
32 devices in a mesh: cases: 2 (over x), tx: 8 (over z, y), ty: 2 (over core).
Axes of the slice: x: 2, y: 2, z: 4, core: 2. Of those that a mesh axis runs over, the one named last changes fastest.
Arguments:
- tiles: bfloat16 [16, 2, 1024, 128], P(('cases', 'tx'), 'ty'), parts along dimension 0, may hold values from -6 to 6
- sources: int32 [16, 2, 1024, 8], P(('cases', 'tx'), 'ty'), parts along dimension 0, may hold values from 0 to 2047
- parents: int32 [16, 2, 1024], P(('cases', 'tx'), 'ty'), parts along dimension 0, may hold values from 0 to 1023, as said below
- restrict_w: bfloat16 [16, 2, 1024], P(('cases', 'tx'), 'ty'), parts along dimension 0, may hold values from 0.29882812 to 3
- coarse_state: bfloat16 [2048, 128], P(('cases', 'tx', 'ty')), parts along dimension 0, may hold values from -6 to 6
- edge_in: bfloat16 [2, 128, 128], replicated, may hold values from -0.5 to 0.5
- edge_bias: float32 [128], replicated, may hold values from -3 to 3
- edge_out: bfloat16 [128, 128], replicated, may hold values from -0.5 to 0.5
- node_in: bfloat16 [2, 128, 128], replicated, may hold values from -0.5 to 0.5
- node_bias: float32 [128], replicated, may hold values from -3 to 3
- node_out: bfloat16 [128, 128], replicated, may hold values from -0.5 to 0.5
- node_gain: float32 [128], replicated, may hold values from 0.1 to 1.9
- coarse_gain: float32 [128], replicated, may hold values from 0.1 to 1.9
- coarse_w: bfloat16 [2, 128, 128], replicated, may hold values from -0.5 to 0.5
- prolong_in: bfloat16 [2, 128, 128], replicated, may hold values from -0.5 to 0.5
- prolong_out: bfloat16 [128, 128], replicated, may hold values from -0.5 to 0.5
Outputs:
- fine_out: bfloat16 [16, 2, 1024, 128], P(('cases', 'tx'), 'ty'), parts along dimension 0
- coarse_out: bfloat16 [2048, 128], P(('cases', 'tx', 'ty')), parts along dimension 0
There are 2 independent parts, one for each index of `cases`. A program takes and returns all parts, laid end to end along the dimension named above; an argument that names none is the same for every part. Nothing has to cross between parts.
Inputs may be any that keep to these rules, and one draw needn't show every extreme that they name: `parents`: tile (i, j) owns the coarse nodes (i * 2 + j) * 64 to (i * 2 + j + 1) * 64 - 1; the parent of each of its fine nodes lies in its own block or in the block of one of the tiles (i-1, j), (i+1, j), (i, j-1), (i, j+1) of the grid.
All inputs are finite; a program needn't handle non-finite values.
Results may differ from a plain program's by a relative error of at most 0.0047.
The roundings to bfloat16 on the way count: a program that leaves them out, or rounds other values in their place, can miss the bound.
Values may be sent and summed in bfloat16 or wider, within the bound.
No kernel may reach another device: no remote copies, remote signals or barrier semaphores. Data moves between devices by JAX's collectives and lax.ppermute only.
A program may use at most 64 MiB of HBM per device.

v0:
```python
import jax
import jax.numpy as jnp
from jax import lax
from jax.sharding import PartitionSpec as P


def padded_2(value, sides, width):
    for axis, dim in sides:
        peers, length = (lax.axis_size(axis), value.shape[dim])
        up = [(i, (i + 1) % peers) for i in range(peers - 1)]
        down = [(j, i) for i, j in up]
        last = lax.slice_in_dim(value, length - width, length, axis=dim)
        first = lax.slice_in_dim(value, 0, width, axis=dim)
        before = lax.ppermute(last, axis, up)
        after = lax.ppermute(first, axis, down)
        value = jnp.concatenate([before, value, after], axis=dim)
    return value


def layer_norm(values, gain):
    center = values - jnp.mean(values, axis=-1, keepdims=True)
    spread = jnp.mean(center * center, axis=-1, keepdims=True)
    return center * lax.rsqrt(spread + 1e-05) * gain


def tile_update(
    latents,
    beside_all,
    sources,
    edge_in,
    edge_bias,
    edge_out,
    node_in,
    node_bias,
    node_out,
    node_gain,
):
    extended = jnp.concatenate([latents, beside_all], axis=0)
    node_rows = latents.shape[0]
    degree = sources.shape[1]
    width = latents.shape[1]
    ext_rows = extended.shape[0]
    block = min(64, node_rows)
    steps = node_rows // block
    dst_proj = jnp.dot(latents, edge_in[0], preferred_element_type=jnp.float32)
    dst_blocks = dst_proj.reshape(steps, block, width)
    src_blocks = sources.reshape(steps, block * degree)
    slots = jnp.arange(ext_rows, dtype=jnp.int32)

    def tile_one_block(items):
        dst_part, src_part = items
        incidence = (src_part[:, None] == slots[None, :]).astype(jnp.bfloat16)
        rows = jnp.dot(incidence, extended, preferred_element_type=jnp.float32).astype(jnp.bfloat16)
        picked = jnp.dot(rows, edge_in[1], preferred_element_type=jnp.float32).reshape(
            block, degree, width
        )
        edge_hidden = jax.nn.silu(dst_part[:, None, :] + picked + edge_bias).astype(jnp.bfloat16)
        messages = jnp.dot(
            edge_hidden.reshape(-1, width), edge_out, preferred_element_type=jnp.float32
        )
        return jnp.sum(messages.reshape(block, degree, width), axis=1)

    aggregate = (
        lax.map(tile_one_block, (dst_blocks, src_blocks))
        .reshape(node_rows, width)
        .astype(jnp.bfloat16)
    )
    node_pre = (
        jnp.dot(latents, node_in[0], preferred_element_type=jnp.float32)
        + jnp.dot(aggregate, node_in[1], preferred_element_type=jnp.float32)
        + node_bias
    )
    node_hidden = jax.nn.silu(node_pre).astype(jnp.bfloat16)
    update = jnp.dot(node_hidden, node_out, preferred_element_type=jnp.float32)
    return (latents.astype(jnp.float32) + layer_norm(update, node_gain)).astype(jnp.bfloat16)


def coarse_update(coarse_in, coarse_gain, coarse_w):
    normed = layer_norm(coarse_in, coarse_gain).astype(jnp.bfloat16)
    hidden = jax.nn.silu(jnp.dot(normed, coarse_w[0], preferred_element_type=jnp.float32)).astype(
        jnp.bfloat16
    )
    return (coarse_in + jnp.dot(hidden, coarse_w[1], preferred_element_type=jnp.float32)).astype(
        jnp.bfloat16
    )


def prolong(fine_mid, lifted, prolong_in, prolong_out):
    pre = jnp.dot(fine_mid, prolong_in[0], preferred_element_type=jnp.float32) + jnp.dot(
        lifted, prolong_in[1], preferred_element_type=jnp.float32
    )
    hidden = jax.nn.silu(pre).astype(jnp.bfloat16)
    return (
        fine_mid.astype(jnp.float32)
        + jnp.dot(hidden, prolong_out, preferred_element_type=jnp.float32)
    ).astype(jnp.bfloat16)


def pool_rows(parent_ids, weighted, start, count):
    block = min(count, 512)
    steps = count // block

    def pool_one_block(index):
        first = start + index * block
        ones = (parent_ids[None, :] == first + jnp.arange(block, dtype=jnp.int32)[:, None]).astype(
            jnp.bfloat16
        )
        return jnp.dot(ones, weighted, preferred_element_type=jnp.float32)

    pieces = lax.map(pool_one_block, jnp.arange(steps, dtype=jnp.int32))
    return pieces.reshape(count, weighted.shape[1])


def lookup_rows(parent_ids, total, piece, start):
    ones = (
        parent_ids[:, None] == start + jnp.arange(piece.shape[0], dtype=jnp.int32)[None, :]
    ).astype(jnp.bfloat16)
    return total + jnp.dot(ones, piece, preferred_element_type=jnp.float32)


def body(
    tiles,
    sources,
    parents,
    restrict_w,
    coarse_state,
    edge_in,
    edge_bias,
    edge_out,
    node_in,
    node_bias,
    node_out,
    node_gain,
    coarse_gain,
    coarse_w,
    prolong_in,
    prolong_out,
):
    latents = tiles[0, 0]
    node_rows = latents.shape[0]
    rim_rows = node_rows // 4
    rim = tiles[:, :, :rim_rows]
    padded = padded_2(rim, (("tx", 0), ("ty", 1)), 1)
    beside_all = jnp.concatenate([padded[0, 1], padded[2, 1], padded[1, 0], padded[1, 2]], axis=0)
    fine_mid = tile_update(
        latents,
        beside_all,
        sources[0, 0],
        edge_in,
        edge_bias,
        edge_out,
        node_in,
        node_bias,
        node_out,
        node_gain,
    )
    weighted = (
        fine_mid.astype(jnp.float32) * restrict_w[0, 0][:, None].astype(jnp.float32)
    ).astype(jnp.bfloat16)
    parent_ids = parents[0, 0]
    co_rows = coarse_state.shape[0]
    col_count = lax.axis_size("ty")
    own_start = lax.axis_index(("tx", "ty")) * co_rows
    empty = jnp.zeros((node_rows, latents.shape[1]), jnp.float32)
    row_step = col_count * co_rows
    own_term = pool_rows(parent_ids, weighted, own_start, co_rows)
    terms_x = jnp.stack(
        [
            pool_rows(parent_ids, weighted, own_start - row_step, co_rows),
            pool_rows(parent_ids, weighted, own_start + row_step, co_rows),
        ],
        axis=0,
    )
    terms_y = jnp.stack(
        [
            pool_rows(parent_ids, weighted, own_start - co_rows, co_rows),
            pool_rows(parent_ids, weighted, own_start + co_rows, co_rows),
        ],
        axis=0,
    )
    got_x = padded_2(terms_x, (("tx", 0),), 1)
    got_y = padded_2(terms_y, (("ty", 0),), 1)
    coarse_in = (
        coarse_state.astype(jnp.float32) + own_term + got_x[0] + got_x[3] + got_y[0] + got_y[3]
    )
    coarse_out = coarse_update(coarse_in, coarse_gain, coarse_w)
    near = padded_2(coarse_out[None, None], (("tx", 0), ("ty", 1)), 1)
    lifted = lookup_rows(parent_ids, empty, coarse_out, own_start)
    lifted = lookup_rows(parent_ids, lifted, near[0, 1], own_start - row_step)
    lifted = lookup_rows(parent_ids, lifted, near[2, 1], own_start + row_step)
    lifted = lookup_rows(parent_ids, lifted, near[1, 0], own_start - co_rows)
    lifted = lookup_rows(parent_ids, lifted, near[1, 2], own_start + co_rows).astype(jnp.bfloat16)
    fine_out = prolong(fine_mid, lifted, prolong_in, prolong_out)
    return (fine_out[None, None], coarse_out)


def solution(mesh):
    return jax.shard_map(
        body,
        mesh=mesh,
        in_specs=(
            P(("cases", "tx"), "ty", None, None),
            P(("cases", "tx"), "ty", None, None),
            P(("cases", "tx"), "ty", None),
            P(("cases", "tx"), "ty", None),
            P(("cases", "tx", "ty"), None),
            P(),
            P(),
            P(),
            P(),
            P(),
            P(),
            P(),
            P(),
            P(),
            P(),
            P(),
        ),
        out_specs=(P(("cases", "tx"), "ty", None, None), P(("cases", "tx", "ty"), None)),
        check_vma=False,
    )
```

profile of v0, /device:TPU:25, one launch (start us, length us, event | category | flops | bytes accessed | tf_op | source)
XLA Modules:
  0.0 73.7 jit_solution(14889855994278742456)
XLA Ops:
  0.7 1.1 %copy.24 = bf16[1,1,1024,128]{2,3,1,0:T(8,128)(2,1)S(1)} copy(bf16[1,1,1024,128]{3,2,1,0:T(8,128)(2,1)} %param.18) | data formatting | bytes 524288 | tf_op args[0]
  1.8 3.0 %collective-permute-start.1 = (bf16[1,1,256,128]{2,3,1,0:T(8,128)(2,1)S(1)}, bf16[1,1,256,128]{2,3,1,0:T(8,128)(2,1)S(1)}, u32[]{:S(2)}, u32[]{:S(2)}) collective-permute-start(bf16[1,1,256,128]{2,3,1,0:T(8,128)(2,1)S(1)} %slice.52), channel_id=1, source_target_pairs={{2,0},{4,2},{6,4},{8,6},{10,8},{12,10},{14,12},{3,1},{5,3},{7,5},{... | collective-permute-start | bytes 196616 | tf_op jit(solution)/shard_map/ppermute | solution.py:15
  4.8 2.2 %collective-permute-start = (bf16[1,1,256,128]{2,3,1,0:T(8,128)(2,1)S(1)}, bf16[1,1,256,128]{2,3,1,0:T(8,128)(2,1)S(1)}, u32[]{:S(2)}, u32[]{:S(2)}) collective-permute-start(bf16[1,1,256,128]{2,3,1,0:T(8,128)(2,1)S(1)} %slice.52), channel_id=1, source_target_pairs={{0,2},{2,4},{4,6},{6,8},{8,10},{10,12},{12,14},{1,3},{3,5},{5,7},{... | collective-permute-start | bytes 196616 | tf_op jit(solution)/shard_map/ppermute | solution.py:14
  9.2 1.5 %collective-permute-done = bf16[1,1,256,128]{2,3,1,0:T(8,128)(2,1)S(1)} collective-permute-done((bf16[1,1,256,128]{2,3,1,0:T(8,128)(2,1)S(1)}, bf16[1,1,256,128]{2,3,1,0:T(8,128)(2,1)S(1)}, u32[]{:S(2)}, u32[]{:S(2)}) %collective-permute-start) | collective-permute-done | bytes 65568 | tf_op jit(solution)/shard_map/ppermute | solution.py:14
  10.8 4.0 %collective-permute-start.3 = (bf16[3,1,256,128]{2,3,1,0:T(8,128)(2,1)S(1)}, bf16[3,1,256,128]{2,3,1,0:T(8,128)(2,1)S(1)}, u32[]{:S(2)}, u32[]{:S(2)}) collective-permute-start(bf16[3,1,256,128]{2,3,1,0:T(8,128)(2,1)S(1)} %pad_maximum_fusion), channel_id=1, source_target_pairs={{1,0},{3,2},{5,4},{7,6},{9,8},{11,10},{13,12},{15,14},{17,16},{19,... | collective-permute-start | bytes 589832 | tf_op jit(solution)/shard_map/ppermute | solution.py:15
  14.8 1.3 %collective-permute-start.2 = (bf16[3,1,256,128]{2,3,1,0:T(8,128)(2,1)S(1)}, bf16[3,1,256,128]{2,3,1,0:T(8,128)(2,1)S(1)}, u32[]{:S(2)}, u32[]{:S(2)}) collective-permute-start(bf16[3,1,256,128]{2,3,1,0:T(8,128)(2,1)S(1)} %pad_maximum_fusion), channel_id=1, source_target_pairs={{0,1},{2,3},{4,5},{6,7},{8,9},{10,11},{12,13},{14,15},{16,17},{18,... | collective-permute-start | bytes 589832 | tf_op jit(solution)/shard_map/ppermute | solution.py:14
  16.1 2.0 %collective-permute-done.2 = bf16[3,1,256,128]{2,3,1,0:T(8,128)(2,1)S(1)} collective-permute-done((bf16[3,1,256,128]{2,3,1,0:T(8,128)(2,1)S(1)}, bf16[3,1,256,128]{2,3,1,0:T(8,128)(2,1)S(1)}, u32[]{:S(2)}, u32[]{:S(2)}) %collective-permute-start.2) | collective-permute-done | bytes 196640 | tf_op jit(solution)/shard_map/ppermute | solution.py:14
  18.9 20.9 %while.3 = (s32[]{:T(128)}, bf16[16,64,128]{2,1,0:T(8,128)(2,1)S(1)}, f32[16,64,128]{2,1,0:T(8,128)S(1)}, s32[16,512]{1,0:T(8,128)S(1)}, bf16[2048,128]{1,0:T(8,...) while((s32[]{:T(128)}, ...), condition=%wide.region_2.3_spmd.clone, body=%wide.region_0.2_spmd.clone.sunk | while | flops 303620096 | bytes 1006193 | solution.py:64
  19.0 1.0 %multiply_convert_fusion.8 = bf16[64,8,128]{2,1,0:T(8,128)(2,1)S(1)} fusion(bf16[2048,128]{1,0:T(8,128)(2,1)S(1)} %get-tuple-element.254, s32[512]{0:T(512)S(1)} %bitcast.148, f32[128]{0:T(128)S(1)} %get-tuple-element.256, f32[64,128]{1,0:T(8,128)S(1)} %dynamic-slice_bitcast_fusion.2, bf16[2,128,128]{2,1,0:T(8,128)(2,1)S(1)} %get-tuple-element.255), kind=kOutput, calls=%fused_computation.9.clone.1 | convolution fusion | flops 286785536 | bytes 723456 | tf_op jit(solution)/shard_map/while/body/eval_jaxpr/dot_general | solution.py:54
  20.3 1.0 %multiply_convert_fusion.8 = bf16[64,8,128]{2,1,0:T(8,128)(2,1)S(1)} fusion(bf16[2048,128]{1,0:T(8,128)(2,1)S(1)} %get-tuple-element.254, s32[512]{0:T(512)S(1)} %bitcast.148, f32[128]{0:T(128)S(1)} %get-tuple-element.256, f32[64,128]{1,0:T(8,128)S(1)} %dynamic-slice_bitcast_fusion.2, bf16[2,128,128]{2,1,0:T(8,128)(2,1)S(1)} %get-tuple-element.255), kind=kOutput, calls=%fused_computation.9.clone.1 | convolution fusion | flops 286785536 | bytes 723456 | tf_op jit(solution)/shard_map/while/body/eval_jaxpr/dot_general | solution.py:54
  21.6 1.0 %multiply_convert_fusion.8 = bf16[64,8,128]{2,1,0:T(8,128)(2,1)S(1)} fusion(bf16[2048,128]{1,0:T(8,128)(2,1)S(1)} %get-tuple-element.254, s32[512]{0:T(512)S(1)} %bitcast.148, f32[128]{0:T(128)S(1)} %get-tuple-element.256, f32[64,128]{1,0:T(8,128)S(1)} %dynamic-slice_bitcast_fusion.2, bf16[2,128,128]{2,1,0:T(8,128)(2,1)S(1)} %get-tuple-element.255), kind=kOutput, calls=%fused_computation.9.clone.1 | convolution fusion | flops 286785536 | bytes 723456 | tf_op jit(solution)/shard_map/while/body/eval_jaxpr/dot_general | solution.py:54
  22.9 1.0 %multiply_convert_fusion.8 = bf16[64,8,128]{2,1,0:T(8,128)(2,1)S(1)} fusion(bf16[2048,128]{1,0:T(8,128)(2,1)S(1)} %get-tuple-element.254, s32[512]{0:T(512)S(1)} %bitcast.148, f32[128]{0:T(128)S(1)} %get-tuple-element.256, f32[64,128]{1,0:T(8,128)S(1)} %dynamic-slice_bitcast_fusion.2, bf16[2,128,128]{2,1,0:T(8,128)(2,1)S(1)} %get-tuple-element.255), kind=kOutput, calls=%fused_computation.9.clone.1 | convolution fusion | flops 286785536 | bytes 723456 | tf_op jit(solution)/shard_map/while/body/eval_jaxpr/dot_general | solution.py:54
  24.2 1.0 %multiply_convert_fusion.8 = bf16[64,8,128]{2,1,0:T(8,128)(2,1)S(1)} fusion(bf16[2048,128]{1,0:T(8,128)(2,1)S(1)} %get-tuple-element.254, s32[512]{0:T(512)S(1)} %bitcast.148, f32[128]{0:T(128)S(1)} %get-tuple-element.256, f32[64,128]{1,0:T(8,128)S(1)} %dynamic-slice_bitcast_fusion.2, bf16[2,128,128]{2,1,0:T(8,128)(2,1)S(1)} %get-tuple-element.255), kind=kOutput, calls=%fused_computation.9.clone.1 | convolution fusion | flops 286785536 | bytes 723456 | tf_op jit(solution)/shard_map/while/body/eval_jaxpr/dot_general | solution.py:54
  25.5 1.0 %multiply_convert_fusion.8 = bf16[64,8,128]{2,1,0:T(8,128)(2,1)S(1)} fusion(bf16[2048,128]{1,0:T(8,128)(2,1)S(1)} %get-tuple-element.254, s32[512]{0:T(512)S(1)} %bitcast.148, f32[128]{0:T(128)S(1)} %get-tuple-element.256, f32[64,128]{1,0:T(8,128)S(1)} %dynamic-slice_bitcast_fusion.2, bf16[2,128,128]{2,1,0:T(8,128)(2,1)S(1)} %get-tuple-element.255), kind=kOutput, calls=%fused_computation.9.clone.1 | convolution fusion | flops 286785536 | bytes 723456 | tf_op jit(solution)/shard_map/while/body/eval_jaxpr/dot_general | solution.py:54
  26.8 1.0 %multiply_convert_fusion.8 = bf16[64,8,128]{2,1,0:T(8,128)(2,1)S(1)} fusion(bf16[2048,128]{1,0:T(8,128)(2,1)S(1)} %get-tuple-element.254, s32[512]{0:T(512)S(1)} %bitcast.148, f32[128]{0:T(128)S(1)} %get-tuple-element.256, f32[64,128]{1,0:T(8,128)S(1)} %dynamic-slice_bitcast_fusion.2, bf16[2,128,128]{2,1,0:T(8,128)(2,1)S(1)} %get-tuple-element.255), kind=kOutput, calls=%fused_computation.9.clone.1 | convolution fusion | flops 286785536 | bytes 723456 | tf_op jit(solution)/shard_map/while/body/eval_jaxpr/dot_general | solution.py:54
  28.1 1.0 %multiply_convert_fusion.8 = bf16[64,8,128]{2,1,0:T(8,128)(2,1)S(1)} fusion(bf16[2048,128]{1,0:T(8,128)(2,1)S(1)} %get-tuple-element.254, s32[512]{0:T(512)S(1)} %bitcast.148, f32[128]{0:T(128)S(1)} %get-tuple-element.256, f32[64,128]{1,0:T(8,128)S(1)} %dynamic-slice_bitcast_fusion.2, bf16[2,128,128]{2,1,0:T(8,128)(2,1)S(1)} %get-tuple-element.255), kind=kOutput, calls=%fused_computation.9.clone.1 | convolution fusion | flops 286785536 | bytes 723456 | tf_op jit(solution)/shard_map/while/body/eval_jaxpr/dot_general | solution.py:54
  29.4 1.0 %multiply_convert_fusion.8 = bf16[64,8,128]{2,1,0:T(8,128)(2,1)S(1)} fusion(bf16[2048,128]{1,0:T(8,128)(2,1)S(1)} %get-tuple-element.254, s32[512]{0:T(512)S(1)} %bitcast.148, f32[128]{0:T(128)S(1)} %get-tuple-element.256, f32[64,128]{1,0:T(8,128)S(1)} %dynamic-slice_bitcast_fusion.2, bf16[2,128,128]{2,1,0:T(8,128)(2,1)S(1)} %get-tuple-element.255), kind=kOutput, calls=%fused_computation.9.clone.1 | convolution fusion | flops 286785536 | bytes 723456 | tf_op jit(solution)/shard_map/while/body/eval_jaxpr/dot_general | solution.py:54
  30.7 1.0 %multiply_convert_fusion.8 = bf16[64,8,128]{2,1,0:T(8,128)(2,1)S(1)} fusion(bf16[2048,128]{1,0:T(8,128)(2,1)S(1)} %get-tuple-element.254, s32[512]{0:T(512)S(1)} %bitcast.148, f32[128]{0:T(128)S(1)} %get-tuple-element.256, f32[64,128]{1,0:T(8,128)S(1)} %dynamic-slice_bitcast_fusion.2, bf16[2,128,128]{2,1,0:T(8,128)(2,1)S(1)} %get-tuple-element.255), kind=kOutput, calls=%fused_computation.9.clone.1 | convolution fusion | flops 286785536 | bytes 723456 | tf_op jit(solution)/shard_map/while/body/eval_jaxpr/dot_general | solution.py:54
  32.0 1.0 %multiply_convert_fusion.8 = bf16[64,8,128]{2,1,0:T(8,128)(2,1)S(1)} fusion(bf16[2048,128]{1,0:T(8,128)(2,1)S(1)} %get-tuple-element.254, s32[512]{0:T(512)S(1)} %bitcast.148, f32[128]{0:T(128)S(1)} %get-tuple-element.256, f32[64,128]{1,0:T(8,128)S(1)} %dynamic-slice_bitcast_fusion.2, bf16[2,128,128]{2,1,0:T(8,128)(2,1)S(1)} %get-tuple-element.255), kind=kOutput, calls=%fused_computation.9.clone.1 | convolution fusion | flops 286785536 | bytes 723456 | tf_op jit(solution)/shard_map/while/body/eval_jaxpr/dot_general | solution.py:54
  33.3 1.0 %multiply_convert_fusion.8 = bf16[64,8,128]{2,1,0:T(8,128)(2,1)S(1)} fusion(bf16[2048,128]{1,0:T(8,128)(2,1)S(1)} %get-tuple-element.254, s32[512]{0:T(512)S(1)} %bitcast.148, f32[128]{0:T(128)S(1)} %get-tuple-element.256, f32[64,128]{1,0:T(8,128)S(1)} %dynamic-slice_bitcast_fusion.2, bf16[2,128,128]{2,1,0:T(8,128)(2,1)S(1)} %get-tuple-element.255), kind=kOutput, calls=%fused_computation.9.clone.1 | convolution fusion | flops 286785536 | bytes 723456 | tf_op jit(solution)/shard_map/while/body/eval_jaxpr/dot_general | solution.py:54
  37.2 1.0 %multiply_convert_fusion.8 = bf16[64,8,128]{2,1,0:T(8,128)(2,1)S(1)} fusion(bf16[2048,128]{1,0:T(8,128)(2,1)S(1)} %get-tuple-element.254, s32[512]{0:T(512)S(1)} %bitcast.148, f32[128]{0:T(128)S(1)} %get-tuple-element.256, f32[64,128]{1,0:T(8,128)S(1)} %dynamic-slice_bitcast_fusion.2, bf16[2,128,128]{2,1,0:T(8,128)(2,1)S(1)} %get-tuple-element.255), kind=kOutput, calls=%fused_computation.9.clone.1 | convolution fusion | flops 286785536 | bytes 723456 | tf_op jit(solution)/shard_map/while/body/eval_jaxpr/dot_general | solution.py:54
  42.7 2.0 %collective-permute-start.7 = (f32[1,64,128]{2,1,0:T(8,128)S(1)}, f32[1,64,128]{2,1,0:T(8,128)S(1)}, u32[]{:S(2)}, u32[]{:S(2)}) collective-permute-start(f32[1,64,128]{2,1,0:T(8,128)S(1)} %convolution_bitcast_fusion), channel_id=1, source_target_pairs={{1,0},{3,2},{5,4},{7,6},{9,8},{11,10},{13,12},{15,14},{17,16},{19,... | collective-permute-start | bytes 98312 | tf_op jit(solution)/shard_map/ppermute | solution.py:15
  44.7 1.3 %collective-permute-start.6 = (f32[1,64,128]{2,1,0:T(8,128)S(1)}, f32[1,64,128]{2,1,0:T(8,128)S(1)}, u32[]{:S(2)}, u32[]{:S(2)}) collective-permute-start(f32[1,64,128]{2,1,0:T(8,128)S(1)} %convolution_bitcast_fusion.1), channel_id=1, source_target_pairs={{0,1},{2,3},{4,5},{6,7},{8,9},{10,11},{12,13},{14,15},{16,17},{18,... | collective-permute-start | bytes 98312 | tf_op jit(solution)/shard_map/ppermute | solution.py:14
  46.0 1.9 %collective-permute-start.5 = (f32[1,64,128]{2,1,0:T(8,128)S(1)}, f32[1,64,128]{2,1,0:T(8,128)S(1)}, u32[]{:S(2)}, u32[]{:S(2)}) collective-permute-start(f32[1,64,128]{2,1,0:T(8,128)S(1)} %convolution_bitcast_fusion.2), channel_id=1, source_target_pairs={{2,0},{4,2},{6,4},{8,6},{10,8},{12,10},{14,12},{3,1},{5,3},{7,5},{... | collective-permute-start | bytes 98312 | tf_op jit(solution)/shard_map/ppermute | solution.py:15
  48.0 3.4 %collective-permute-start.4 = (f32[1,64,128]{2,1,0:T(8,128)S(1)}, f32[1,64,128]{2,1,0:T(8,128)S(1)}, u32[]{:S(2)}, u32[]{:S(2)}) collective-permute-start(f32[1,64,128]{2,1,0:T(8,128)S(1)} %convolution_bitcast_fusion.3), channel_id=1, source_target_pairs={{0,2},{2,4},{4,6},{6,8},{8,10},{10,12},{12,14},{1,3},{3,5},{5,7},{... | collective-permute-start | bytes 98312 | tf_op jit(solution)/shard_map/ppermute | solution.py:14
  51.4 2.1 %collective-permute-done.4 = f32[1,64,128]{2,1,0:T(8,128)S(1)} collective-permute-done((f32[1,64,128]{2,1,0:T(8,128)S(1)}, f32[1,64,128]{2,1,0:T(8,128)S(1)}, u32[]{:S(2)}, u32[]{:S(2)}) %collective-permute-start.4) | collective-permute-done | bytes 32800 | tf_op jit(solution)/shard_map/ppermute | solution.py:14
  54.4 2.3 %collective-permute-start.9 = (bf16[1,1,64,128]{3,2,1,0:T(8,128)(2,1)S(1)}, bf16[1,1,64,128]{3,2,1,0:T(8,128)(2,1)S(1)}, u32[]{:S(2)}, u32[]{:S(2)}) collective-permute-start(bf16[1,1,64,128]{3,2,1,0:T(8,128)(2,1)S(1)} %bitcast.145), channel_id=1, source_target_pairs={{2,0},{4,2},{6,4},{8,6},{10,8},{12,10},{14,12},{3,1},{5,3},{7,5},{... | collective-permute-start | bytes 49160 | tf_op jit(solution)/shard_map/ppermute | solution.py:15
  56.8 2.9 %collective-permute-start.8 = (bf16[1,1,64,128]{3,2,1,0:T(8,128)(2,1)S(1)}, bf16[1,1,64,128]{3,2,1,0:T(8,128)(2,1)S(1)}, u32[]{:S(2)}, u32[]{:S(2)}) collective-permute-start(bf16[1,1,64,128]{3,2,1,0:T(8,128)(2,1)S(1)} %bitcast.146), channel_id=1, source_target_pairs={{0,2},{2,4},{4,6},{6,8},{8,10},{10,12},{12,14},{1,3},{3,5},{5,7},{... | collective-permute-start | bytes 49160 | tf_op jit(solution)/shard_map/ppermute | solution.py:14
  60.0 2.2 %collective-permute-done.8 = bf16[1,1,64,128]{3,2,1,0:T(8,128)(2,1)S(1)} collective-permute-done((bf16[1,1,64,128]{3,2,1,0:T(8,128)(2,1)S(1)}, bf16[1,1,64,128]{3,2,1,0:T(8,128)(2,1)S(1)}, u32[]{:S(2)}, u32[]{:S(2)}) %collective-permute-start.8) | collective-permute-done | bytes 16416 | tf_op jit(solution)/shard_map/ppermute | solution.py:14
  62.2 5.9 %collective-permute-start.11 = (bf16[3,1,64,128]{3,2,1,0:T(8,128)(2,1)S(1)}, bf16[3,1,64,128]{3,2,1,0:T(8,128)(2,1)S(1)}, u32[]{:S(2)}, u32[]{:S(2)}) collective-permute-start(bf16[3,1,64,128]{3,2,1,0:T(8,128)(2,1)S(1)} %pad_maximum_fusion.1), channel_id=1, source_target_pairs={{1,0},{3,2},{5,4},{7,6},{9,8},{11,10},{13,12},{15,14},{17,16},{19,... | collective-permute-start | bytes 147464 | tf_op jit(solution)/shard_map/ppermute | solution.py:15
  68.1 1.3 %collective-permute-start.10 = (bf16[3,1,64,128]{3,2,1,0:T(8,128)(2,1)S(1)}, bf16[3,1,64,128]{3,2,1,0:T(8,128)(2,1)S(1)}, u32[]{:S(2)}, u32[]{:S(2)}) collective-permute-start(bf16[3,1,64,128]{3,2,1,0:T(8,128)(2,1)S(1)} %pad_maximum_fusion.1), channel_id=1, source_target_pairs={{0,1},{2,3},{4,5},{6,7},{8,9},{10,11},{12,13},{14,15},{16,17},{18,... | collective-permute-start | bytes 147464 | tf_op jit(solution)/shard_map/ppermute | solution.py:14
  70.0 1.2 %collective-permute-done.10 = bf16[3,1,64,128]{3,2,1,0:T(8,128)(2,1)S(1)} collective-permute-done((bf16[3,1,64,128]{3,2,1,0:T(8,128)(2,1)S(1)}, bf16[3,1,64,128]{3,2,1,0:T(8,128)(2,1)S(1)}, u32[]{:S(2)}, u32[]{:S(2)}) %collective-permute-start.10) | collective-permute-done | bytes 49184 | tf_op jit(solution)/shard_map/ppermute | solution.py:14
  (150 shorter events, 16.9 us)
Async XLA Ops:
  0.6 39.2 %copy-start = (bf16[128,128]{1,0:T(8,128)(2,1)S(1)}, bf16[128,128]{1,0:T(8,128)(2,1)}, u32[]{:S(2)}) copy-start(bf16[128,128]{1,0:T(8,128)(2,1)} %param.28) | copy-start | bytes 98308
  0.6 6.5 %copy-start.11 = (bf16[1,1,1024]{2,1,0:T(2,128)(2,1)S(1)}, bf16[1,1,1024]{2,1,0:T(2,128)(2,1)}, u32[]{:S(2)}) copy-start(bf16[1,1,1024]{2,1,0:T(2,128)(2,1)} %param.21) | copy-start | bytes 6148
  0.7 6.6 %copy-start.5 = (s32[1,1,1024,8]{2,3,1,0:T(8,128)S(1)}, s32[1,1,1024,8]{2,3,1,0:T(8,128)}, u32[]{:S(2)}) copy-start(s32[1,1,1024,8]{2,3,1,0:T(8,128)} %param.19) | copy-start | bytes 98308
  1.8 7.4 %collective-permute-start.1 = (bf16[1,1,256,128]{2,3,1,0:T(8,128)(2,1)S(1)}, bf16[1,1,256,128]{2,3,1,0:T(8,128)(2,1)S(1)}, u32[]{:S(2)}, u32[]{:S(2)}) collective-permute-start(bf16[1,1,256,128]{2,3,1,0:T(8,128)(2,1)S(1)} %slice.52), channel_id=1, source_target_pairs={{2,0},{4,2},{6,4},{8,6},{10,8},{12,10},{14,12},{3,1},{5,3},{7,5},{... | collective-permute-start | bytes 196616 | tf_op jit(solution)/shard_map/ppermute | solution.py:15
  4.8 5.9 %collective-permute-start = (bf16[1,1,256,128]{2,3,1,0:T(8,128)(2,1)S(1)}, bf16[1,1,256,128]{2,3,1,0:T(8,128)(2,1)S(1)}, u32[]{:S(2)}, u32[]{:S(2)}) collective-permute-start(bf16[1,1,256,128]{2,3,1,0:T(8,128)(2,1)S(1)} %slice.52), channel_id=1, source_target_pairs={{0,2},{2,4},{4,6},{6,8},{8,10},{10,12},{12,14},{1,3},{3,5},{5,7},{... | collective-permute-start | bytes 196616 | tf_op jit(solution)/shard_map/ppermute | solution.py:14
  7.2 1.0 %copy-start.1 = (bf16[1,1,1024,128]{3,2,1,0:T(8,128)(2,1)S(1)}, bf16[1,1,1024,128]{3,2,1,0:T(8,128)(2,1)}, u32[]{:S(2)}) copy-start(bf16[1,1,1024,128]{3,2,1,0:T(8,128)(2,1)} %param.18) | copy-start | bytes 786436
  7.2 0.9 %copy-start.9 = (bf16[2,128,128]{2,1,0:T(8,128)(2,1)S(1)}, bf16[2,128,128]{2,1,0:T(8,128)(2,1)}, u32[]{:S(2)}) copy-start(bf16[2,128,128]{2,1,0:T(8,128)(2,1)} %param.26) | copy-start | bytes 196612
  8.2 0.8 %copy-start.8 = (bf16[2,128,128]{2,1,0:T(8,128)(2,1)S(1)}, bf16[2,128,128]{2,1,0:T(8,128)(2,1)}, u32[]{:S(2)}) copy-start(bf16[2,128,128]{2,1,0:T(8,128)(2,1)} %param.23) | copy-start | bytes 196612
  10.8 7.4 %collective-permute-start.3 = (bf16[3,1,256,128]{2,3,1,0:T(8,128)(2,1)S(1)}, bf16[3,1,256,128]{2,3,1,0:T(8,128)(2,1)S(1)}, u32[]{:S(2)}, u32[]{:S(2)}) collective-permute-start(bf16[3,1,256,128]{2,3,1,0:T(8,128)(2,1)S(1)} %pad_maximum_fusion), channel_id=1, source_target_pairs={{1,0},{3,2},{5,4},{7,6},{9,8},{11,10},{13,12},{15,14},{17,16},{19,... | collective-permute-start | bytes 589832 | tf_op jit(solution)/shard_map/ppermute | solution.py:15
  14.8 3.3 %collective-permute-start.2 = (bf16[3,1,256,128]{2,3,1,0:T(8,128)(2,1)S(1)}, bf16[3,1,256,128]{2,3,1,0:T(8,128)(2,1)S(1)}, u32[]{:S(2)}, u32[]{:S(2)}) collective-permute-start(bf16[3,1,256,128]{2,3,1,0:T(8,128)(2,1)S(1)} %pad_maximum_fusion), channel_id=1, source_target_pairs={{0,1},{2,3},{4,5},{6,7},{8,9},{10,11},{12,13},{14,15},{16,17},{18,... | collective-permute-start | bytes 589832 | tf_op jit(solution)/shard_map/ppermute | solution.py:14
  18.2 0.8 %copy-start.2 = (bf16[128,128]{1,0:T(8,128)(2,1)S(1)}, bf16[128,128]{1,0:T(8,128)(2,1)}, u32[]{:S(2)}) copy-start(bf16[128,128]{1,0:T(8,128)(2,1)} %param.25) | copy-start | bytes 98308
  18.2 0.8 %copy-start.14 = (f32[128]{0:T(128)S(1)}, f32[128]{0:T(128)}, u32[]{:S(2)}) copy-start(f32[128]{0:T(128)} %param.24) | copy-start | bytes 1540
  18.9 20.9 %copy-start.15 = (f32[128]{0:T(128)S(1)}, f32[128]{0:T(128)}, u32[]{:S(2)}) copy-start(f32[128]{0:T(128)} %param.27) | copy-start | bytes 1540
  40.3 0.7 copy-start.12
  40.9 0.7 copy-start.3
  41.9 11.6 %copy-start.7 = (bf16[64,128]{1,0:T(8,128)(2,1)S(1)}, bf16[64,128]{1,0:T(8,128)(2,1)}, u32[]{:S(2)}) copy-start(bf16[64,128]{1,0:T(8,128)(2,1)} %param.22) | copy-start | bytes 49156
  42.4 11.7 %copy-start.13 = (bf16[2,128,128]{2,1,0:T(8,128)(2,1)S(1)}, bf16[2,128,128]{2,1,0:T(8,128)(2,1)}, u32[]{:S(2)}) copy-start(bf16[2,128,128]{2,1,0:T(8,128)(2,1)} %param.31) | copy-start | bytes 196612
  42.4 11.7 %copy-start.16 = (f32[128]{0:T(128)S(1)}, f32[128]{0:T(128)}, u32[]{:S(2)}) copy-start(f32[128]{0:T(128)} %param.30) | copy-start | bytes 1540
  42.4 17.3 %copy-start.10 = (bf16[2,128,128]{2,1,0:T(8,128)(2,1)S(1)}, bf16[2,128,128]{2,1,0:T(8,128)(2,1)}, u32[]{:S(2)}) copy-start(bf16[2,128,128]{2,1,0:T(8,128)(2,1)} %param.32) | copy-start | bytes 196612
  42.7 8.7 %collective-permute-start.7 = (f32[1,64,128]{2,1,0:T(8,128)S(1)}, f32[1,64,128]{2,1,0:T(8,128)S(1)}, u32[]{:S(2)}, u32[]{:S(2)}) collective-permute-start(f32[1,64,128]{2,1,0:T(8,128)S(1)} %convolution_bitcast_fusion), channel_id=1, source_target_pairs={{1,0},{3,2},{5,4},{7,6},{9,8},{11,10},{13,12},{15,14},{17,16},{19,... | collective-permute-start | bytes 98312 | tf_op jit(solution)/shard_map/ppermute | solution.py:15
  44.7 6.6 %collective-permute-start.6 = (f32[1,64,128]{2,1,0:T(8,128)S(1)}, f32[1,64,128]{2,1,0:T(8,128)S(1)}, u32[]{:S(2)}, u32[]{:S(2)}) collective-permute-start(f32[1,64,128]{2,1,0:T(8,128)S(1)} %convolution_bitcast_fusion.1), channel_id=1, source_target_pairs={{0,1},{2,3},{4,5},{6,7},{8,9},{10,11},{12,13},{14,15},{16,17},{18,... | collective-permute-start | bytes 98312 | tf_op jit(solution)/shard_map/ppermute | solution.py:14
  46.0 5.3 %collective-permute-start.5 = (f32[1,64,128]{2,1,0:T(8,128)S(1)}, f32[1,64,128]{2,1,0:T(8,128)S(1)}, u32[]{:S(2)}, u32[]{:S(2)}) collective-permute-start(f32[1,64,128]{2,1,0:T(8,128)S(1)} %convolution_bitcast_fusion.2), channel_id=1, source_target_pairs={{2,0},{4,2},{6,4},{8,6},{10,8},{12,10},{14,12},{3,1},{5,3},{7,5},{... | collective-permute-start | bytes 98312 | tf_op jit(solution)/shard_map/ppermute | solution.py:15
  48.0 5.6 %collective-permute-start.4 = (f32[1,64,128]{2,1,0:T(8,128)S(1)}, f32[1,64,128]{2,1,0:T(8,128)S(1)}, u32[]{:S(2)}, u32[]{:S(2)}) collective-permute-start(f32[1,64,128]{2,1,0:T(8,128)S(1)} %convolution_bitcast_fusion.3), channel_id=1, source_target_pairs={{0,2},{2,4},{4,6},{6,8},{8,10},{10,12},{12,14},{1,3},{3,5},{5,7},{... | collective-permute-start | bytes 98312 | tf_op jit(solution)/shard_map/ppermute | solution.py:14
  54.4 15.3 %copy-start.4 = (bf16[64,128]{1,0:T(8,128)(2,1)}, bf16[64,128]{1,0:T(8,128)(2,1)S(1)}, u32[]{:S(2)}) copy-start(bf16[64,128]{1,0:T(8,128)(2,1)S(1)} %fusion.16) | copy-start | bytes 49156
  54.4 5.6 %collective-permute-start.9 = (bf16[1,1,64,128]{3,2,1,0:T(8,128)(2,1)S(1)}, bf16[1,1,64,128]{3,2,1,0:T(8,128)(2,1)S(1)}, u32[]{:S(2)}, u32[]{:S(2)}) collective-permute-start(bf16[1,1,64,128]{3,2,1,0:T(8,128)(2,1)S(1)} %bitcast.145), channel_id=1, source_target_pairs={{2,0},{4,2},{6,4},{8,6},{10,8},{12,10},{14,12},{3,1},{5,3},{7,5},{... | collective-permute-start | bytes 49160 | tf_op jit(solution)/shard_map/ppermute | solution.py:15
  56.8 5.4 %collective-permute-start.8 = (bf16[1,1,64,128]{3,2,1,0:T(8,128)(2,1)S(1)}, bf16[1,1,64,128]{3,2,1,0:T(8,128)(2,1)S(1)}, u32[]{:S(2)}, u32[]{:S(2)}) collective-permute-start(bf16[1,1,64,128]{3,2,1,0:T(8,128)(2,1)S(1)} %bitcast.146), channel_id=1, source_target_pairs={{0,2},{2,4},{4,6},{6,8},{8,10},{10,12},{12,14},{1,3},{3,5},{5,7},{... | collective-permute-start | bytes 49160 | tf_op jit(solution)/shard_map/ppermute | solution.py:14
  62.2 9.3 %collective-permute-start.11 = (bf16[3,1,64,128]{3,2,1,0:T(8,128)(2,1)S(1)}, bf16[3,1,64,128]{3,2,1,0:T(8,128)(2,1)S(1)}, u32[]{:S(2)}, u32[]{:S(2)}) collective-permute-start(bf16[3,1,64,128]{3,2,1,0:T(8,128)(2,1)S(1)} %pad_maximum_fusion.1), channel_id=1, source_target_pairs={{1,0},{3,2},{5,4},{7,6},{9,8},{11,10},{13,12},{15,14},{17,16},{19,... | collective-permute-start | bytes 147464 | tf_op jit(solution)/shard_map/ppermute | solution.py:15
  68.1 3.1 %collective-permute-start.10 = (bf16[3,1,64,128]{3,2,1,0:T(8,128)(2,1)S(1)}, bf16[3,1,64,128]{3,2,1,0:T(8,128)(2,1)S(1)}, u32[]{:S(2)}, u32[]{:S(2)}) collective-permute-start(bf16[3,1,64,128]{3,2,1,0:T(8,128)(2,1)S(1)} %pad_maximum_fusion.1), channel_id=1, source_target_pairs={{0,1},{2,3},{4,5},{6,7},{8,9},{10,11},{12,13},{14,15},{16,17},{18,... | collective-permute-start | bytes 147464 | tf_op jit(solution)/shard_map/ppermute | solution.py:14
  71.9 0.8 %copy-start.6 = (bf16[128,128]{1,0:T(8,128)(2,1)S(1)}, bf16[128,128]{1,0:T(8,128)(2,1)}, u32[]{:S(2)}) copy-start(bf16[128,128]{1,0:T(8,128)(2,1)} %param.33) | copy-start | bytes 98308
where the time goes:
time: 74.4 us; the launch traced here: 73.7 us
  starting transfers between devices  31.7 us (43%)
  matrix products  24.4 us (33%)
  waiting for transfers between devices  9.01 us (12%)
  local copies, waits for them, and re-layouts  6.31 us (8%)
  between operations  1.19 us (2%)
    ppermute x6, starting transfers between devices, padded_2(): after = lax.ppermute(first, axis, down)  19.3 us
    dot_general x16, matrix products, tile_one_block(): jnp.dot(rows, edge_in[1], preferred_element_type=jnp.float32)  16.2 us
    ppermute x6, starting transfers between devices, padded_2(): before = lax.ppermute(last, axis, up)  12.4 us
    ppermute x6, waiting for transfers between devices, padded_2(): before = lax.ppermute(last, axis, up)  8.99 us
    unnamed x42, local copies, waits for them, and re-layouts  5.46 us
    dot_general x16, matrix products, tile_one_block(): jnp.dot(edge_hidden.reshape(-1, width), edge_out, preferred_element_type=...  3.39 us
  transfers between devices with their start and end apart: 12, of which 5 were waited for; matrix products, arithmetic and copies ran while one was open for 3% of the time, Pallas kernels for 0%

commit v1 on v0

v1 whole, which is shorter than its diff:
```python
import functools

import jax
import jax.numpy as jnp
from jax import lax
from jax.experimental import pallas as pl
from jax.experimental.pallas import tpu as pltpu
from jax.sharding import PartitionSpec as P

F32 = jnp.float32
BF16 = jnp.bfloat16
I32 = jnp.int32
VMEM_LIMIT = 32 * 1024 * 1024
BLOCK = 128
GROUP = 4


def mm(a, b):
    return jnp.dot(a, b, preferred_element_type=F32)


def silu(x):
    half = 0.5 * x
    return half + half * jnp.tanh(half)


def normalise(values, gain):
    center = values - jnp.mean(values, axis=-1, keepdims=True)
    spread = jnp.mean(center * center, axis=-1, keepdims=True)
    return center * lax.rsqrt(spread + 1e-05) * gain


def split(values):
    high = values.astype(BF16)
    low = (values - high.astype(F32)).astype(BF16)
    return jnp.concatenate([high, low], axis=1)


def quotient(x, d):
    return lax.shift_right_logical(x, d.bit_length() - 1) if d & (d - 1) == 0 else x // d


def place(n):
    i, j = lax.axis_index("tx"), lax.axis_index("ty")
    return i, j, lax.rem(i, 2) == 0


def owners(n):
    i, j, even = place(n)
    mine = i * 2 + j
    return mine, jnp.where(even, mine + 2, mine - 2), jnp.where(even, mine - 2, mine + 2), mine + 1 - 2 * j


def spread(cols, lane, rows):
    return jnp.broadcast_to(cols[:, lane : lane + 1], (rows, 128))


def one_hot(where, first, count):
    parts = []
    for at in range(first, first + count, 128):
        lanes = (lax.broadcasted_iota(I32, where.shape, 1) + at).astype(F32).astype(BF16)
        parts.append(jnp.where(where == lanes, jnp.ones((), BF16), jnp.zeros((), BF16)))
    return jnp.concatenate(parts, axis=1)


def gathered(cols, table, degree, block):
    rim = table.shape[0] // 2
    pairs = []
    for k in range(0, degree, GROUP):
        ones = jnp.concatenate([one_hot(spread(cols, k + g, block), -rim, 2 * rim) for g in range(GROUP)], axis=0)
        got = mm(ones, table).astype(BF16)
        for g in range(GROUP):
            part = got[g * block : (g + 1) * block]
            pairs.append((part[:, :128], part[:, 128:], spread(cols, degree + k + g, block)))
    return pairs


def local_kernel(tiles, sources, cols, near):
    nodes, width = tiles.shape
    degree = sources.shape[0]
    rim = nodes // 4
    index = sources[...]
    rows = jnp.concatenate([((index & (2 * rim - 1)) - rim).astype(F32), quotient(index, 2 * rim).astype(F32)], axis=0)
    cols[...] = rows.T.astype(BF16)
    table = jnp.concatenate([tiles[: 2 * rim, :], tiles[2 * rim :, :]], axis=1)

    def step(at, _):
        first = pl.multiple_of(at * BLOCK, BLOCK)
        here = pl.ds(first, BLOCK)
        for k, (low, high, quarter) in enumerate(gathered(cols[here, :], table, degree, BLOCK)):
            near[k, here, :] = jnp.where(quarter == jnp.ones((), BF16), high, low)
        return 0

    lax.fori_loop(0, nodes // BLOCK, step, 0)


def node_kernel(
    n, tiles, around_a, around_b, around_s, cols, near, parents, weights,
    edge_in, edge_bias, edge_out, node_in, node_bias, node_out, node_gain,
    fine_mid, own, to_a, to_b, to_s, slots, total, weighted,
):
    nodes, width = tiles.shape
    degree = near.shape[0]
    co_rows = own.shape[0]
    i, j, even = place(n)
    none = jnp.zeros(around_a.shape, BF16)
    got_a, got_b, got_s = around_a[...], around_b[...], around_s[...]
    before = jnp.where(i > 0, jnp.where(even, got_b, got_a), none)
    after = jnp.where(i < n - 1, jnp.where(even, got_a, got_b), none)
    left, right = jnp.where(j > 0, got_s, none), jnp.where(j < 1, got_s, none)
    table = jnp.concatenate([jnp.concatenate([before, left], axis=1), jnp.concatenate([after, right], axis=1)], axis=0)
    project = edge_in[1]
    empty = jnp.zeros_like(project)
    project = jnp.concatenate(
        [jnp.concatenate([project, empty], axis=1), jnp.concatenate([empty, project], axis=1)], axis=0
    )

    def step(at, _):
        first = pl.multiple_of(at * BLOCK, BLOCK)
        here = pl.ds(first, BLOCK)
        dst_part = mm(tiles[here, :], edge_in[0]) + edge_bias[...]
        picked = []
        for k, (low, high, quarter) in enumerate(gathered(cols[here, :], table, degree, BLOCK)):
            far = jnp.where(quarter == jnp.full((), 3, BF16), high, low)
            picked.append(jnp.where(quarter < jnp.full((), 2, BF16), near[k, here, :], far))
        picked = jnp.concatenate(
            [jnp.concatenate([picked[k], picked[k + 1]], axis=1) for k in range(0, degree, 2)], axis=0
        )
        src = mm(picked, project)
        sums = jnp.zeros((BLOCK, width), F32)
        for k in range(degree):
            part = src[k // 2 * BLOCK : (k // 2 + 1) * BLOCK, k % 2 * width : (k % 2 + 1) * width]
            sums = sums + silu(dst_part + part).astype(BF16).astype(F32)
        total[here, :] = sums
        return 0

    lax.fori_loop(0, nodes // BLOCK, step, 0)
    node_weights = jnp.concatenate([node_in[0], node_in[1]], axis=0)
    out_twice = jnp.concatenate([edge_out[...], edge_out[...]], axis=0)
    ids = parents[...]
    block_of = quotient(ids, co_rows)
    slot = ids - block_of * co_rows
    for at, owner in enumerate(owners(n)):
        slot = jnp.where(block_of == owner, slot + at * co_rows, slot)
    slot = slot.astype(F32)
    scale = jnp.concatenate([slot, weights[...].astype(F32), jnp.zeros((6, nodes), F32)], axis=0).T
    slots[...] = scale.astype(BF16)
    for first in range(0, nodes, 256):
        here = pl.ds(first, 256)
        aggregate = mm(split(total[here, :]), out_twice).astype(BF16)
        both = jnp.concatenate([tiles[here, :], aggregate], axis=1)
        hidden = silu(mm(both, node_weights) + node_bias[...]).astype(BF16)
        update = normalise(mm(hidden, node_out[...]), node_gain[...])
        mid = (tiles[here, :].astype(F32) + update).astype(BF16)
        fine_mid[here, :] = mid
        weighted[here, :] = (mid.astype(F32) * scale[first : first + 256, 1:2]).astype(BF16)
    row = lax.broadcasted_iota(I32, (4 * co_rows, nodes), 0).astype(F32).astype(BF16)
    ones = jnp.where(row == slot.astype(BF16), jnp.ones((), BF16), jnp.zeros((), BF16))
    pooled = mm(ones, weighted[...])
    for at, ref in enumerate((own, to_a, to_b, to_s)):
        ref[...] = pooled[at * co_rows : (at + 1) * co_rows]


def coarse_kernel(state, own, from_a, from_b, from_s, coarse_gain, coarse_w, out):
    total = state[...].astype(F32) + own[...] + from_a[...] + from_b[...] + from_s[...]
    normed = normalise(total, coarse_gain[...]).astype(BF16)
    hidden = silu(mm(normed, coarse_w[0])).astype(BF16)
    out[...] = (total + mm(hidden, coarse_w[1])).astype(BF16)


def prolong_kernel(fine_mid, slots, own, from_a, from_b, from_s, prolong_in, prolong_out, out):
    nodes, width = fine_mid.shape
    co_rows = own.shape[0]
    coarse = jnp.concatenate([own[...], from_a[...], from_b[...], from_s[...]], axis=0)
    weights = jnp.concatenate([prolong_in[0], prolong_in[1]], axis=0)
    block = 256
    for first in range(0, nodes, block):
        here = pl.ds(first, block)
        ones = one_hot(spread(slots[here, :], 0, block), 0, 4 * co_rows)
        lifted = mm(ones, coarse).astype(BF16)
        mid = fine_mid[here, :]
        hidden = silu(mm(jnp.concatenate([mid, lifted], axis=1), weights)).astype(BF16)
        out[here, :] = (mid.astype(F32) + mm(hidden, prolong_out[...])).astype(BF16)


def call(kernel, outs, *args, flops=0, scratch=()):
    return pl.pallas_call(
        kernel,
        out_shape=outs,
        in_specs=[pl.BlockSpec(memory_space=pltpu.VMEM)] * len(args),
        out_specs=[pl.BlockSpec(memory_space=pltpu.VMEM)] * len(outs),
        scratch_shapes=scratch,
        compiler_params=pltpu.CompilerParams(vmem_limit_bytes=VMEM_LIMIT),
        cost_estimate=pl.CostEstimate(flops=flops, bytes_accessed=flops // 1000, transcendentals=0),
    )(*args)


def exchange(n, to_a, to_b, to_s):
    pairs_a = [(i, i ^ 1) for i in range(n)]
    pairs_b = []
    for i in range(n):
        for j in range(2):
            other = (((i - 1) ^ 1) + 1, j) if 0 < i < n - 1 else (i, 1 - j)
            pairs_b.append((i * 2 + j, other[0] * 2 + other[1]))
    return (
        lax.ppermute(to_a, "tx", pairs_a),
        lax.ppermute(to_b, ("tx", "ty"), pairs_b),
        lax.ppermute(to_s, "ty", [(0, 1), (1, 0)]),
    )


def body(
    tiles,
    sources,
    parents,
    restrict_w,
    coarse_state,
    edge_in,
    edge_bias,
    edge_out,
    node_in,
    node_bias,
    node_out,
    node_gain,
    coarse_gain,
    coarse_w,
    prolong_in,
    prolong_out,
):
    nodes, width = tiles.shape[2:]
    n = lax.axis_size("tx")
    co_rows = coarse_state.shape[0]
    degree = sources.shape[3]
    shape = jax.ShapeDtypeStruct

    latents = tiles[0, 0]
    boundary = latents[: nodes // 4]
    around = exchange(n, boundary, boundary, boundary)
    cols, near = call(
        local_kernel,
        [shape((nodes, 2 * degree), BF16), shape((degree, nodes, width), BF16)],
        latents, jnp.swapaxes(sources[0, 0], 0, 1),
        flops=4 * 2**30,
    )
    fine_mid, own, to_a, to_b, to_s, slots = call(
        functools.partial(node_kernel, n),
        [shape((nodes, width), BF16)] + [shape((co_rows, width), F32)] * 4 + [shape((nodes, 8), BF16)],
        latents, *around, cols, near, parents[0], restrict_w[0],
        edge_in, edge_bias[None], edge_out, node_in, node_bias[None], node_out, node_gain[None],
        flops=6 * 2**30,
        scratch=[pltpu.VMEM((nodes, width), F32), pltpu.VMEM((nodes, width), BF16)],
    )
    got = exchange(n, to_a, to_b, to_s)
    (coarse_out,) = call(
        coarse_kernel,
        [shape((co_rows, width), BF16)],
        coarse_state, own, *got, coarse_gain[None], coarse_w,
        flops=2**29,
    )
    beside = exchange(n, coarse_out, coarse_out, coarse_out)
    (fine_out,) = call(
        prolong_kernel,
        [shape((nodes, width), BF16)],
        fine_mid, slots, coarse_out, *beside, prolong_in, prolong_out,
        flops=2**30,
    )
    return (fine_out[None, None], coarse_out)


def solution(mesh):
    tile = P(("cases", "tx"), "ty", None, None)
    row = P(("cases", "tx"), "ty", None)
    coarse = P(("cases", "tx", "ty"), None)
    return jax.shard_map(
        body,
        mesh=mesh,
        in_specs=(tile, tile, row, row, coarse) + (P(),) * 11,
        out_specs=(tile, coarse),
        check_vma=False,
    )
```

time: 74.4 us -> 33.7 us (0.45)
  the two profiles are of different devices: /device:TPU:25 before, /device:TPU:0 now
where the time goes in v1:
time: 33.7 us; the launch traced here: 33.4 us
  Pallas kernels  14.4 us (43%)
  starting transfers between devices  9.45 us (28%)
  waiting for transfers between devices  5.3 us (16%)
  local copies, waits for them, and re-layouts  3.35 us (10%)
  between operations  0.87 us (3%)
    pallas_call x4, Pallas kernels, call(): pl.pallas_call(kernel, out_shape=outs, in_specs=[pl.BlockSpec(memory_spac...  14.4 us
    ppermute x3, starting transfers between devices, exchange(): lax.ppermute(to_a, 'tx', pairs_a)  7.87 us
    ppermute x3, waiting for transfers between devices, exchange(): lax.ppermute(to_a, 'tx', pairs_a)  5.28 us
    unnamed x34, local copies, waits for them, and re-layouts  2.5 us
    ppermute x3, starting transfers between devices, exchange(): lax.ppermute(to_s, 'ty', [(0, 1), (1, 0)])  0.95 us
    slice x1, local copies, waits for them, and re-layouts, body(): boundary = latents[:nodes // 4]  0.85 us
  transfers between devices with their start and end apart: 9, of which 2 were waited for; matrix products, arithmetic and copies ran while one was open for 0% of the time, Pallas kernels for 13%

profile of v1, /device:TPU:0, one launch (start us, length us, event | category | flops | bytes accessed | tf_op | source)
XLA Modules:
  0.0 33.4 jit_solution(2504441399018585742)
XLA Ops:
  0.6 0.8 %slice_bitcast_fusion = bf16[256,128]{1,0:T(8,128)(2,1)S(1)} fusion(bf16[1,1,1024,128]{3,2,1,0:T(8,128)(2,1)} %param.16), kind=kLoop, calls=%fused_computation | loop fusion | bytes 131072 | tf_op jit(solution)/shard_map/slice | solution.py:237
  1.5 0.5 %collective-permute-start.2 = (bf16[256,128]{1,0:T(8,128)(2,1)S(1)}, bf16[256,128]{1,0:T(8,128)(2,1)S(1)}, u32[]{:S(2)}, u32[]{:S(2)}) collective-permute-start(bf16[256,128]{1,0:T(8,128)(2,1)S(1)} %slice_bitcast_fusion), channel_id=1, source_target_pairs={{0,1},{1,0},{2,3},{3,2},{4,5},{5,4},{6,7},{7,6},{8,9},{9,8},{10,11... | collective-permute-start | bytes 196616 | tf_op jit(solution)/shard_map/ppermute | solution.py:208
  1.9 0.1 collective-permute-start.1
  2.0 4.0 %collective-permute-start = (bf16[256,128]{1,0:T(8,128)(2,1)S(1)}, bf16[256,128]{1,0:T(8,128)(2,1)S(1)}, u32[]{:S(2)}, u32[]{:S(2)}) collective-permute-start(bf16[256,128]{1,0:T(8,128)(2,1)S(1)} %slice_bitcast_fusion), channel_id=1, source_target_pairs={{0,2},{2,0},{4,6},{6,4},{8,10},{10,8},{12,14},{14,12},{1,3},{3,1},... | collective-permute-start | bytes 196616 | tf_op jit(solution)/shard_map/ppermute | solution.py:206
  6.0 0.9 %copy-done = bf16[1,1,1024,128]{3,2,1,0:T(8,128)(2,1)S(1)} copy-done((bf16[1,1,1024,128]{3,2,1,0:T(8,128)(2,1)S(1)}, bf16[1,1,1024,128]{3,2,1,0:T(8,128)(2,1)}, u32[]{:S(2)}) %copy-start) | copy-done | bytes 262168
  6.9 0.8 %copy-done.5 = s32[1,1,1024,8]{2,3,1,0:T(8,128)S(1)} copy-done((s32[1,1,1024,8]{2,3,1,0:T(8,128)S(1)}, s32[1,1,1024,8]{2,3,1,0:T(8,128)}, u32[]{:S(2)}) %copy-start.5) | copy-done | bytes 32792
  7.7 0.0 copy-start.11
  7.7 0.0 copy-start.12
  7.7 0.0 copy-start.13
  7.7 0.0 copy-start.14
  7.7 0.0 copy-start.15
  7.7 4.4 %shard_map.167 = (bf16[1024,16]{1,0:T(8,128)(2,1)S(1)}, bf16[8,1024,128]{2,1,0:T(8,128)(2,1)S(1)}) custom-call(bf16[1024,128]{1,0:T(8,128)(2,1)S(1)} %bitcast.13, s32[8,1024]{1,0:T(8,128)S(1)} %bitcast.15), custom_call_target="tpu_custom_call" | custom-call | flops 4294967296 | bytes 4294967 | tf_op jit(solution)/shard_map/pallas_call | solution.py:187
  12.2 0.0 collective-permute-done.1.around_b
  12.2 0.0 collective-permute-done.around_a
  12.3 0.0 copy-start.3
  12.3 0.0 copy-start.9
  12.3 0.0 copy-start.16
  12.4 0.0 copy-start.4
  12.4 0.0 copy-start.8
  12.4 7.2 %shard_map.168 = (bf16[1024,128]{1,0:T(8,128)(2,1)S(1)}, f32[64,128]{1,0:T(8,128)S(1)}, f32[64,128]{1,0:T(8,128)S(1)}, f32[64,128]{1,0:T(8,128)S(1)}, f32[64,128...) custom-call(bf16[1024,128]{1,0:T(8,128)(2,1)S(1)} %bitcast.14, bf16[256,128]{1,0:T(8,128)(2,1)S(1)} %collective-permute-done.around_a, ...), custom_call_target="tpu_custom_call" | custom-call | flops 6442450944 | bytes 6442450 | tf_op jit(solution)/shard_map/pallas_call | solution.py:187
  19.5 0.1 collective-permute-start.3
  19.6 0.1 collective-permute-start.4
  19.7 0.5 %collective-permute-start.5 = (f32[64,128]{1,0:T(8,128)S(1)}, f32[64,128]{1,0:T(8,128)S(1)}, u32[]{:S(2)}, u32[]{:S(2)}) collective-permute-start(f32[64,128]{1,0:T(8,128)S(1)} %get-tuple-element.17), channel_id=1, source_target_pairs={{0,1},{1,0},{2,3},{3,2},{4,5},{5,4},{6,7},{7,6},{8,9},{9,8},{10,11... | collective-permute-start | bytes 98312 | tf_op jit(solution)/shard_map/ppermute | solution.py:208
  20.2 3.3 %collective-permute-done.3.from_a = f32[64,128]{1,0:T(8,128)S(1)} collective-permute-done((f32[64,128]{1,0:T(8,128)S(1)}, f32[64,128]{1,0:T(8,128)S(1)}, u32[]{:S(2)}, u32[]{:S(2)}) %collective-permute-start.3) | collective-permute-done | bytes 32800 | tf_op jit(solution)/shard_map/ppermute | solution.py:206
  23.5 0.0 collective-permute-done.4.from_b
  23.5 0.0 collective-permute-done.5.from_s
  23.6 1.0 %shard_map.169.own = bf16[64,128]{1,0:T(8,128)(2,1)} custom-call(bf16[64,128]{1,0:T(8,128)(2,1)S(1)} %copy-done.9, f32[64,128]{1,0:T(8,128)S(1)} %get-tuple-element.14.own, f32[64,128]{1,0:T(8,128)S(1)} %collective-permute-done.3.from_a, f32[64,128]{1,0:T(8,128)S(1)} %collective-permute-done.4.from_b, f32[64,128]{1,0:T(8,128)S(1)} %collective-permute-done.5.from_s, ...), custom_call_target="tpu_custom_call" | custom-call | flops 536870912 | bytes 536870 | tf_op jit(solution)/shard_map/pallas_call | solution.py:187
  24.6 0.5 %collective-permute-start.7 = (bf16[64,128]{1,0:T(8,128)(2,1)}, bf16[64,128]{1,0:T(8,128)(2,1)S(1)}, u32[]{:S(2)}, u32[]{:S(2)}) collective-permute-start(bf16[64,128]{1,0:T(8,128)(2,1)} %shard_map.169.own), channel_id=1, source_target_pairs={{0,1},{1,0},{2,4},{3,5},{4,2},{5,3},{6,8},{7,9},{8,6},{9,7},{10,12... | collective-permute-start | bytes 49160 | tf_op jit(solution)/shard_map/ppermute | solution.py:207
  25.1 3.8 %collective-permute-start.6 = (bf16[64,128]{1,0:T(8,128)(2,1)}, bf16[64,128]{1,0:T(8,128)(2,1)S(1)}, u32[]{:S(2)}, u32[]{:S(2)}) collective-permute-start(bf16[64,128]{1,0:T(8,128)(2,1)} %shard_map.169.own), channel_id=1, source_target_pairs={{0,2},{2,0},{4,6},{6,4},{8,10},{10,8},{12,14},{14,12},{1,3},{3,1},... | collective-permute-start | bytes 49160 | tf_op jit(solution)/shard_map/ppermute | solution.py:206
  28.9 2.0 %collective-permute-done.6.from_a = bf16[64,128]{1,0:T(8,128)(2,1)S(1)} collective-permute-done((bf16[64,128]{1,0:T(8,128)(2,1)}, bf16[64,128]{1,0:T(8,128)(2,1)S(1)}, u32[]{:S(2)}, u32[]{:S(2)}) %collective-permute-start.6) | collective-permute-done | bytes 16416 | tf_op jit(solution)/shard_map/ppermute | solution.py:206
  30.9 0.7 %copy-done.10 = bf16[64,128]{1,0:T(8,128)(2,1)S(1)} copy-done((bf16[64,128]{1,0:T(8,128)(2,1)S(1)}, bf16[64,128]{1,0:T(8,128)(2,1)}, u32[]{:S(2)}) %copy-start.10) | copy-done | bytes 16408
  31.6 1.8 %shard_map.170 = bf16[1024,128]{1,0:T(8,128)(2,1)} custom-call(bf16[1024,128]{1,0:T(8,128)(2,1)S(1)} %get-tuple-element.12.fine_mid, bf16[1024,8]{1,0:T(8,128)(2,1)S(1)} %get-tuple-element.13.slots, bf16[64,128]{1,0:T(8,128)(2,1)S(1)} %copy-done.10, bf16[64,128]{1,0:T(8,128)(2,1)S(1)} %collective-permute-done.6.from_a, ...), custom_call_target="tpu_custom_call" | custom-call | flops 1073741824 | bytes 1073741 | tf_op jit(solution)/shard_map/pallas_call | solution.py:187
  (25 shorter events, 0.1 us)
Async XLA Ops:
  1.5 10.7 %collective-permute-start.2 = (bf16[256,128]{1,0:T(8,128)(2,1)S(1)}, bf16[256,128]{1,0:T(8,128)(2,1)S(1)}, u32[]{:S(2)}, u32[]{:S(2)}) collective-permute-start(bf16[256,128]{1,0:T(8,128)(2,1)S(1)} %slice_bitcast_fusion), channel_id=1, source_target_pairs={{0,1},{1,0},{2,3},{3,2},{4,5},{5,4},{6,7},{7,6},{8,9},{9,8},{10,11... | collective-permute-start | bytes 196616 | tf_op jit(solution)/shard_map/ppermute | solution.py:208
  1.9 10.3 %collective-permute-start.1 = (bf16[256,128]{1,0:T(8,128)(2,1)S(1)}, bf16[256,128]{1,0:T(8,128)(2,1)S(1)}, u32[]{:S(2)}, u32[]{:S(2)}) collective-permute-start(bf16[256,128]{1,0:T(8,128)(2,1)S(1)} %slice_bitcast_fusion), channel_id=1, source_target_pairs={{0,1},{1,0},{2,4},{3,5},{4,2},{5,3},{6,8},{7,9},{8,6},{9,7},{10,12... | collective-permute-start | bytes 196616 | tf_op jit(solution)/shard_map/ppermute | solution.py:207
  2.0 10.2 %collective-permute-start = (bf16[256,128]{1,0:T(8,128)(2,1)S(1)}, bf16[256,128]{1,0:T(8,128)(2,1)S(1)}, u32[]{:S(2)}, u32[]{:S(2)}) collective-permute-start(bf16[256,128]{1,0:T(8,128)(2,1)S(1)} %slice_bitcast_fusion), channel_id=1, source_target_pairs={{0,2},{2,0},{4,6},{6,4},{8,10},{10,8},{12,14},{14,12},{1,3},{3,1},... | collective-permute-start | bytes 196616 | tf_op jit(solution)/shard_map/ppermute | solution.py:206
  6.0 0.9 %copy-start = (bf16[1,1,1024,128]{3,2,1,0:T(8,128)(2,1)S(1)}, bf16[1,1,1024,128]{3,2,1,0:T(8,128)(2,1)}, u32[]{:S(2)}) copy-start(bf16[1,1,1024,128]{3,2,1,0:T(8,128)(2,1)} %param.16) | copy-start | bytes 786436
  6.9 0.8 %copy-start.5 = (s32[1,1,1024,8]{2,3,1,0:T(8,128)S(1)}, s32[1,1,1024,8]{2,3,1,0:T(8,128)}, u32[]{:S(2)}) copy-start(s32[1,1,1024,8]{2,3,1,0:T(8,128)} %param.17) | copy-start | bytes 98308
  7.7 4.6 %copy-start.1 = (bf16[2,128,128]{2,1,0:T(8,128)(2,1)S(1)}, bf16[2,128,128]{2,1,0:T(8,128)(2,1)}, u32[]{:S(2)}) copy-start(bf16[2,128,128]{2,1,0:T(8,128)(2,1)} %edge_in.1) | copy-start | bytes 196612
  7.7 4.6 %copy-start.2 = (bf16[2,128,128]{2,1,0:T(8,128)(2,1)S(1)}, bf16[2,128,128]{2,1,0:T(8,128)(2,1)}, u32[]{:S(2)}) copy-start(bf16[2,128,128]{2,1,0:T(8,128)(2,1)} %node_in.1) | copy-start | bytes 196612
  7.7 4.6 %copy-start.6 = (bf16[128,128]{1,0:T(8,128)(2,1)S(1)}, bf16[128,128]{1,0:T(8,128)(2,1)}, u32[]{:S(2)}) copy-start(bf16[128,128]{1,0:T(8,128)(2,1)} %edge_out.1) | copy-start | bytes 98308
  7.7 4.6 %copy-start.7 = (bf16[128,128]{1,0:T(8,128)(2,1)S(1)}, bf16[128,128]{1,0:T(8,128)(2,1)}, u32[]{:S(2)}) copy-start(bf16[128,128]{1,0:T(8,128)(2,1)} %node_out.1) | copy-start | bytes 98308
  7.7 4.6 %copy-start.11 = (s32[1,1,1024]{2,1,0:T(1,128)S(1)}, s32[1,1,1024]{2,1,0:T(1,128)}, u32[]{:S(2)}) copy-start(s32[1,1,1024]{2,1,0:T(1,128)} %param.18) | copy-start | bytes 12292
  7.7 4.6 %copy-start.12 = (bf16[1,1,1024]{2,1,0:T(2,128)(2,1)S(1)}, bf16[1,1,1024]{2,1,0:T(2,128)(2,1)}, u32[]{:S(2)}) copy-start(bf16[1,1,1024]{2,1,0:T(2,128)(2,1)} %param.19) | copy-start | bytes 6148
  7.7 4.6 %copy-start.13 = (f32[128]{0:T(128)S(1)}, f32[128]{0:T(128)}, u32[]{:S(2)}) copy-start(f32[128]{0:T(128)} %param.22) | copy-start | bytes 1540
  7.7 4.6 %copy-start.14 = (f32[128]{0:T(128)S(1)}, f32[128]{0:T(128)}, u32[]{:S(2)}) copy-start(f32[128]{0:T(128)} %param.25) | copy-start | bytes 1540
  7.7 4.6 %copy-start.15 = (f32[128]{0:T(128)S(1)}, f32[128]{0:T(128)}, u32[]{:S(2)}) copy-start(f32[128]{0:T(128)} %param.27) | copy-start | bytes 1540
  12.3 11.2 %copy-start.3 = (bf16[2,128,128]{2,1,0:T(8,128)(2,1)S(1)}, bf16[2,128,128]{2,1,0:T(8,128)(2,1)}, u32[]{:S(2)}) copy-start(bf16[2,128,128]{2,1,0:T(8,128)(2,1)} %coarse_w.1) | copy-start | bytes 196612
  12.3 11.2 %copy-start.9 = (bf16[64,128]{1,0:T(8,128)(2,1)S(1)}, bf16[64,128]{1,0:T(8,128)(2,1)}, u32[]{:S(2)}) copy-start(bf16[64,128]{1,0:T(8,128)(2,1)} %state.1) | copy-start | bytes 49156
  12.3 11.2 %copy-start.16 = (f32[128]{0:T(128)S(1)}, f32[128]{0:T(128)}, u32[]{:S(2)}) copy-start(f32[128]{0:T(128)} %param.28) | copy-start | bytes 1540
  12.4 18.5 %copy-start.4 = (bf16[2,128,128]{2,1,0:T(8,128)(2,1)S(1)}, bf16[2,128,128]{2,1,0:T(8,128)(2,1)}, u32[]{:S(2)}) copy-start(bf16[2,128,128]{2,1,0:T(8,128)(2,1)} %prolong_in.1) | copy-start | bytes 196612
  12.4 18.5 %copy-start.8 = (bf16[128,128]{1,0:T(8,128)(2,1)S(1)}, bf16[128,128]{1,0:T(8,128)(2,1)}, u32[]{:S(2)}) copy-start(bf16[128,128]{1,0:T(8,128)(2,1)} %prolong_out.1) | copy-start | bytes 98308
  19.5 4.0 %collective-permute-start.3 = (f32[64,128]{1,0:T(8,128)S(1)}, f32[64,128]{1,0:T(8,128)S(1)}, u32[]{:S(2)}, u32[]{:S(2)}) collective-permute-start(f32[64,128]{1,0:T(8,128)S(1)} %get-tuple-element.15), channel_id=1, source_target_pairs={{0,2},{2,0},{4,6},{6,4},{8,10},{10,8},{12,14},{14,12},{1,3},{3,1},... | collective-permute-start | bytes 98312 | tf_op jit(solution)/shard_map/ppermute | solution.py:206
  19.6 3.9 %collective-permute-start.4 = (f32[64,128]{1,0:T(8,128)S(1)}, f32[64,128]{1,0:T(8,128)S(1)}, u32[]{:S(2)}, u32[]{:S(2)}) collective-permute-start(f32[64,128]{1,0:T(8,128)S(1)} %get-tuple-element.16), channel_id=1, source_target_pairs={{0,1},{1,0},{2,4},{3,5},{4,2},{5,3},{6,8},{7,9},{8,6},{9,7},{10,12... | collective-permute-start | bytes 98312 | tf_op jit(solution)/shard_map/ppermute | solution.py:207
  19.7 3.8 %collective-permute-start.5 = (f32[64,128]{1,0:T(8,128)S(1)}, f32[64,128]{1,0:T(8,128)S(1)}, u32[]{:S(2)}, u32[]{:S(2)}) collective-permute-start(f32[64,128]{1,0:T(8,128)S(1)} %get-tuple-element.17), channel_id=1, source_target_pairs={{0,1},{1,0},{2,3},{3,2},{4,5},{5,4},{6,7},{7,6},{8,9},{9,8},{10,11... | collective-permute-start | bytes 98312 | tf_op jit(solution)/shard_map/ppermute | solution.py:208
  24.6 4.3 %collective-permute-start.8 = (bf16[64,128]{1,0:T(8,128)(2,1)}, bf16[64,128]{1,0:T(8,128)(2,1)S(1)}, u32[]{:S(2)}, u32[]{:S(2)}) collective-permute-start(bf16[64,128]{1,0:T(8,128)(2,1)} %shard_map.169.own), channel_id=1, source_target_pairs={{0,1},{1,0},{2,3},{3,2},{4,5},{5,4},{6,7},{7,6},{8,9},{9,8},{10,11... | collective-permute-start | bytes 49160 | tf_op jit(solution)/shard_map/ppermute | solution.py:208
  24.6 4.3 %collective-permute-start.7 = (bf16[64,128]{1,0:T(8,128)(2,1)}, bf16[64,128]{1,0:T(8,128)(2,1)S(1)}, u32[]{:S(2)}, u32[]{:S(2)}) collective-permute-start(bf16[64,128]{1,0:T(8,128)(2,1)} %shard_map.169.own), channel_id=1, source_target_pairs={{0,1},{1,0},{2,4},{3,5},{4,2},{5,3},{6,8},{7,9},{8,6},{9,7},{10,12... | collective-permute-start | bytes 49160 | tf_op jit(solution)/shard_map/ppermute | solution.py:207
  25.1 5.8 %collective-permute-start.6 = (bf16[64,128]{1,0:T(8,128)(2,1)}, bf16[64,128]{1,0:T(8,128)(2,1)S(1)}, u32[]{:S(2)}, u32[]{:S(2)}) collective-permute-start(bf16[64,128]{1,0:T(8,128)(2,1)} %shard_map.169.own), channel_id=1, source_target_pairs={{0,2},{2,0},{4,6},{6,4},{8,10},{10,8},{12,14},{14,12},{1,3},{3,1},... | collective-permute-start | bytes 49160 | tf_op jit(solution)/shard_map/ppermute | solution.py:206
  30.9 0.7 %copy-start.10 = (bf16[64,128]{1,0:T(8,128)(2,1)S(1)}, bf16[64,128]{1,0:T(8,128)(2,1)}, u32[]{:S(2)}) copy-start(bf16[64,128]{1,0:T(8,128)(2,1)} %shard_map.169.own) | copy-start | bytes 49156

commit v2 on v1

--- a/solution.py
+++ b/solution.py
@@ -12,7 +12,8 @@
 I32 = jnp.int32
 VMEM_LIMIT = 32 * 1024 * 1024
 BLOCK = 128
-GROUP = 4
+GROUP = 2
+UNROLL = 8
 
 
 def mm(a, b):
@@ -52,7 +53,7 @@
 
 
 def spread(cols, lane, rows):
-    return jnp.broadcast_to(cols[:, lane : lane + 1], (rows, 128))
+    return jnp.broadcast_to(cols[:, lane : lane + 1], (rows, 128)).astype(BF16)
 
 
 def one_hot(where, first, count):
@@ -75,13 +76,37 @@
     return pairs
 
 
-def local_kernel(tiles, sources, cols, near):
+def boundary_kernel(tiles, boundary):
+    boundary[...] = tiles[: boundary.shape[0], :]
+
+
+def local_kernel(
+    n, co_rows, tiles, sources, parents, weights, edge_in, edge_bias, cols, near, dst, scale, pool, lift
+):
     nodes, width = tiles.shape
-    degree = sources.shape[0]
+    degree = near.shape[0]
     rim = nodes // 4
     index = sources[...]
-    rows = jnp.concatenate([((index & (2 * rim - 1)) - rim).astype(F32), quotient(index, 2 * rim).astype(F32)], axis=0)
-    cols[...] = rows.T.astype(BF16)
+    ids = parents[...]
+    block_of = quotient(ids, co_rows)
+    slot = ids - block_of * co_rows
+    for at, owner in enumerate(owners(n)):
+        slot = jnp.where(block_of == owner, slot + at * co_rows, slot)
+    slot = slot.astype(F32)
+    rows = [
+        ((index & (2 * rim - 1)) - rim).astype(F32),
+        quotient(index, 2 * rim).astype(F32),
+        slot,
+        weights[...].astype(F32),
+        jnp.zeros((6, nodes), F32),
+    ]
+    turned = jnp.concatenate(rows, axis=0).T
+    cols[...] = turned
+    scale[...] = turned[:, 2 * degree + 1 : 2 * degree + 2] * jnp.ones((1, width), F32)
+    dst[...] = mm(tiles[...], edge_in[0]) + edge_bias[...]
+    row = lax.broadcasted_iota(I32, pool.shape, 0).astype(F32).astype(BF16)
+    pool[...] = jnp.where(row == slot.astype(BF16), jnp.ones((), BF16), jnp.zeros((), BF16))
+    lift[...] = one_hot(spread(cols[...], 2 * degree, nodes), 0, 4 * co_rows)
     table = jnp.concatenate([tiles[: 2 * rim, :], tiles[2 * rim :, :]], axis=1)
 
     def step(at, _):
@@ -91,13 +116,13 @@
             near[k, here, :] = jnp.where(quarter == jnp.ones((), BF16), high, low)
         return 0
 
-    lax.fori_loop(0, nodes // BLOCK, step, 0)
+    lax.fori_loop(0, nodes // BLOCK, step, 0, unroll=UNROLL)
 
 
 def node_kernel(
-    n, tiles, around_a, around_b, around_s, cols, near, parents, weights,
-    edge_in, edge_bias, edge_out, node_in, node_bias, node_out, node_gain,
-    fine_mid, own, to_a, to_b, to_s, slots, total, weighted,
+    n, tiles, around_a, around_b, around_s, cols, near, dst, scale, pool,
+    edge_in, edge_out, node_in, node_bias, node_out, node_gain,
+    fine_mid, own, to_a, to_b, to_s, total, weighted,
 ):
     nodes, width = tiles.shape
     degree = near.shape[0]
@@ -118,33 +143,22 @@
     def step(at, _):
         first = pl.multiple_of(at * BLOCK, BLOCK)
         here = pl.ds(first, BLOCK)
-        dst_part = mm(tiles[here, :], edge_in[0]) + edge_bias[...]
+        dst_part = dst[here, :]
+        sums = jnp.zeros((BLOCK, width), F32)
         picked = []
         for k, (low, high, quarter) in enumerate(gathered(cols[here, :], table, degree, BLOCK)):
             far = jnp.where(quarter == jnp.full((), 3, BF16), high, low)
             picked.append(jnp.where(quarter < jnp.full((), 2, BF16), near[k, here, :], far))
-        picked = jnp.concatenate(
-            [jnp.concatenate([picked[k], picked[k + 1]], axis=1) for k in range(0, degree, 2)], axis=0
-        )
-        src = mm(picked, project)
-        sums = jnp.zeros((BLOCK, width), F32)
-        for k in range(degree):
-            part = src[k // 2 * BLOCK : (k // 2 + 1) * BLOCK, k % 2 * width : (k % 2 + 1) * width]
-            sums = sums + silu(dst_part + part).astype(BF16).astype(F32)
+        for k in range(0, degree, 2):
+            got = mm(jnp.concatenate([picked[k], picked[k + 1]], axis=1), project)
+            for part in (got[:, :width], got[:, width:]):
+                sums = sums + silu(dst_part + part).astype(BF16).astype(F32)
         total[here, :] = sums
         return 0
 
-    lax.fori_loop(0, nodes // BLOCK, step, 0)
+    lax.fori_loop(0, nodes // BLOCK, step, 0, unroll=UNROLL)
     node_weights = jnp.concatenate([node_in[0], node_in[1]], axis=0)
     out_twice = jnp.concatenate([edge_out[...], edge_out[...]], axis=0)
-    ids = parents[...]
-    block_of = quotient(ids, co_rows)
-    slot = ids - block_of * co_rows
-    for at, owner in enumerate(owners(n)):
-        slot = jnp.where(block_of == owner, slot + at * co_rows, slot)
-    slot = slot.astype(F32)
-    scale = jnp.concatenate([slot, weights[...].astype(F32), jnp.zeros((6, nodes), F32)], axis=0).T
-    slots[...] = scale.astype(BF16)
     for first in range(0, nodes, 256):
         here = pl.ds(first, 256)
         aggregate = mm(split(total[here, :]), out_twice).astype(BF16)
@@ -153,12 +167,14 @@
         update = normalise(mm(hidden, node_out[...]), node_gain[...])
         mid = (tiles[here, :].astype(F32) + update).astype(BF16)
         fine_mid[here, :] = mid
-        weighted[here, :] = (mid.astype(F32) * scale[first : first + 256, 1:2]).astype(BF16)
-    row = lax.broadcasted_iota(I32, (4 * co_rows, nodes), 0).astype(F32).astype(BF16)
-    ones = jnp.where(row == slot.astype(BF16), jnp.ones((), BF16), jnp.zeros((), BF16))
-    pooled = mm(ones, weighted[...])
+        weighted[here, :] = (mid.astype(F32) * scale[here, :]).astype(BF16)
+    pooled = mm(pool[...], weighted[...])
     for at, ref in enumerate((own, to_a, to_b, to_s)):
         ref[...] = pooled[at * co_rows : (at + 1) * co_rows]
+
+
+def base_kernel(fine_mid, prolong_in, base):
+    base[...] = mm(fine_mid[...], prolong_in[0])
 
 
 def coarse_kernel(state, own, from_a, from_b, from_s, coarse_gain, coarse_w, out):
@@ -168,19 +184,17 @@
     out[...] = (total + mm(hidden, coarse_w[1])).astype(BF16)
 
 
-def prolong_kernel(fine_mid, slots, own, from_a, from_b, from_s, prolong_in, prolong_out, out):
+def prolong_kernel(fine_mid, base, lift, own, from_a, from_b, from_s, prolong_in, prolong_out, out, coarse_out):
+    coarse_out[...] = own[...]
     nodes, width = fine_mid.shape
-    co_rows = own.shape[0]
     coarse = jnp.concatenate([own[...], from_a[...], from_b[...], from_s[...]], axis=0)
-    weights = jnp.concatenate([prolong_in[0], prolong_in[1]], axis=0)
+    terms = split(mm(coarse, prolong_in[1]))
     block = 256
     for first in range(0, nodes, block):
         here = pl.ds(first, block)
-        ones = one_hot(spread(slots[here, :], 0, block), 0, 4 * co_rows)
-        lifted = mm(ones, coarse).astype(BF16)
-        mid = fine_mid[here, :]
-        hidden = silu(mm(jnp.concatenate([mid, lifted], axis=1), weights)).astype(BF16)
-        out[here, :] = (mid.astype(F32) + mm(hidden, prolong_out[...])).astype(BF16)
+        lifted = mm(lift[here, :], terms)
+        hidden = silu(base[here, :] + (lifted[:, :width] + lifted[:, width:])).astype(BF16)
+        out[here, :] = (fine_mid[here, :].astype(F32) + mm(hidden, prolong_out[...])).astype(BF16)
 
 
 def call(kernel, outs, *args, flops=0, scratch=()):
@@ -234,20 +248,27 @@
     shape = jax.ShapeDtypeStruct
 
     latents = tiles[0, 0]
-    boundary = latents[: nodes // 4]
+    (boundary,) = call(boundary_kernel, [shape((nodes // 4, width), BF16)], latents, flops=2**33)
     around = exchange(n, boundary, boundary, boundary)
-    cols, near = call(
-        local_kernel,
-        [shape((nodes, 2 * degree), BF16), shape((degree, nodes, width), BF16)],
-        latents, jnp.swapaxes(sources[0, 0], 0, 1),
-        flops=4 * 2**30,
-    )
-    fine_mid, own, to_a, to_b, to_s, slots = call(
+    cols, near, dst, scale, pool, lift = call(
+        functools.partial(local_kernel, n, co_rows),
+        [
+            shape((nodes, 24), F32),
+            shape((degree, nodes, width), BF16),
+            shape((nodes, width), F32),
+            shape((nodes, width), F32),
+            shape((4 * co_rows, nodes), BF16),
+            shape((nodes, 4 * co_rows), BF16),
+        ],
+        latents, jnp.swapaxes(sources[0, 0], 0, 1), parents[0], restrict_w[0], edge_in, edge_bias[None],
+        flops=2**34,
+    )
+    fine_mid, own, to_a, to_b, to_s = call(
         functools.partial(node_kernel, n),
-        [shape((nodes, width), BF16)] + [shape((co_rows, width), F32)] * 4 + [shape((nodes, 8), BF16)],
-        latents, *around, cols, near, parents[0], restrict_w[0],
-        edge_in, edge_bias[None], edge_out, node_in, node_bias[None], node_out, node_gain[None],
-        flops=6 * 2**30,
+        [shape((nodes, width), BF16)] + [shape((co_rows, width), F32)] * 4,
+        latents, *around, cols, near, dst, scale, pool,
+        edge_in, edge_out, node_in, node_bias[None], node_out, node_gain[None],
+        flops=2**34,
         scratch=[pltpu.VMEM((nodes, width), F32), pltpu.VMEM((nodes, width), BF16)],
     )
     got = exchange(n, to_a, to_b, to_s)
@@ -255,14 +276,15 @@
         coarse_kernel,
         [shape((co_rows, width), BF16)],
         coarse_state, own, *got, coarse_gain[None], coarse_w,
-        flops=2**29,
+        flops=2**32,
     )
     beside = exchange(n, coarse_out, coarse_out, coarse_out)
-    (fine_out,) = call(
+    (base,) = call(base_kernel, [shape((nodes, width), F32)], fine_mid, prolong_in, flops=2**29)
+    fine_out, coarse_out = call(
         prolong_kernel,
-        [shape((nodes, width), BF16)],
-        fine_mid, slots, coarse_out, *beside, prolong_in, prolong_out,
-        flops=2**30,
+        [shape((nodes, width), BF16), shape((co_rows, width), BF16)],
+        fine_mid, base, lift, coarse_out, *beside, prolong_in, prolong_out,
+        flops=2**32,
     )
     return (fine_out[None, None], coarse_out)
 

time: 33.7 us -> 28.7 us (0.85)
  Pallas kernels: 14.4 us -> 10.4 us
  starting transfers between devices: 9.45 us -> 13.4 us
  waiting for transfers between devices: 5.3 us -> 2.89 us
  local copies, waits for them, and re-layouts: 3.35 us -> 1.03 us
    pallas_call x4 -> x6, Pallas kernels: 14.4 us -> 10.4 us  [call(): pl.pallas_call(kernel, out_shape=outs, in_specs=[pl.BlockSpec(memory_spac...]
    ppermute x3, starting transfers between devices: 7.87 us -> 11.8 us  [exchange(): lax.ppermute(to_a, 'tx', pairs_a)]
    ppermute x3, waiting for transfers between devices: 5.28 us -> 2.87 us  [exchange(): lax.ppermute(to_a, 'tx', pairs_a)]
    unnamed x34 -> x32, local copies, waits for them, and re-layouts: 2.5 us -> 1.03 us
    slice x1 -> x0, local copies, waits for them, and re-layouts: 0.85 us -> none  [body(): boundary = latents[:nodes // 4]]
  transfers between devices with their start and end apart: 9 -> 9, of which waited for: 2 -> 2; matrix products, arithmetic and copies ran while one was open for 0% -> 0% of each run, Pallas kernels for 13% -> 11%
where the time goes in v2:
time: 28.7 us; the launch traced here: 28.5 us
  starting transfers between devices  13.4 us (47%)
  Pallas kernels  10.4 us (36%)
  waiting for transfers between devices  2.89 us (10%)
  local copies, waits for them, and re-layouts  1.03 us (4%)
  between operations  0.88 us (3%)
    ppermute x3, starting transfers between devices, exchange(): lax.ppermute(to_a, 'tx', pairs_a)  11.8 us
    pallas_call x6, Pallas kernels, call(): pl.pallas_call(kernel, out_shape=outs, in_specs=[pl.BlockSpec(memory_spac...  10.4 us
    ppermute x3, waiting for transfers between devices, exchange(): lax.ppermute(to_a, 'tx', pairs_a)  2.87 us
    ppermute x3, starting transfers between devices, exchange(): lax.ppermute(to_s, 'ty', [(0, 1), (1, 0)])  1.07 us
    unnamed x32, local copies, waits for them, and re-layouts  1.03 us
    ppermute x3, starting transfers between devices, exchange(): lax.ppermute(to_b, ('tx', 'ty'), pairs_b)  0.58 us
  transfers between devices with their start and end apart: 9, of which 2 were waited for; matrix products, arithmetic and copies ran while one was open for 0% of the time, Pallas kernels for 11%

profile of v2, /device:TPU:0, one launch (start us, length us, event | category | flops | bytes accessed | tf_op | source)
XLA Modules:
  0.0 28.5 jit_solution(8662258914315497854)
XLA Ops:
  0.6 0.9 %copy-done = bf16[1,1,1024,128]{3,2,1,0:T(8,128)(2,1)S(1)} copy-done((bf16[1,1,1024,128]{3,2,1,0:T(8,128)(2,1)S(1)}, bf16[1,1,1024,128]{3,2,1,0:T(8,128)(2,1)}, u32[]{:S(2)}) %copy-start) | copy-done | bytes 262168
  1.6 0.5 %collective-permute-start.2 = (bf16[256,128]{1,0:T(8,128)(2,1)S(1)}, bf16[256,128]{1,0:T(8,128)(2,1)S(1)}, u32[]{:S(2)}, u32[]{:S(2)}) collective-permute-start(bf16[256,128]{1,0:T(8,128)(2,1)S(1)} %shard_map.167), channel_id=1, source_target_pairs={{0,1},{1,0},{2,3},{3,2},{4,5},{5,4},{6,7},{7,6},{8,9},{9,8},{10,11... | collective-permute-start | bytes 196616 | tf_op jit(solution)/shard_map/ppermute | solution.py:222
  2.1 0.1 collective-permute-start.1
  2.2 4.0 %collective-permute-start = (bf16[256,128]{1,0:T(8,128)(2,1)S(1)}, bf16[256,128]{1,0:T(8,128)(2,1)S(1)}, u32[]{:S(2)}, u32[]{:S(2)}) collective-permute-start(bf16[256,128]{1,0:T(8,128)(2,1)S(1)} %shard_map.167), channel_id=1, source_target_pairs={{0,2},{2,0},{4,6},{6,4},{8,10},{10,8},{12,14},{14,12},{1,3},{3,1},... | collective-permute-start | bytes 196616 | tf_op jit(solution)/shard_map/ppermute | solution.py:220
  6.3 0.0 copy-start.2
  6.3 0.0 copy-start.6
  6.3 0.0 copy-start.7
  6.3 0.0 copy-start.13
  6.3 0.0 copy-start.14
  6.3 3.0 %shard_map.168 = (f32[1024,24]{1,0:T(8,128)S(1)}, bf16[8,1024,128]{2,1,0:T(8,128)(2,1)S(1)}, f32[1024,128]{1,0:T(8,128)S(1)}, f32[1024,128]{1,0:T(8,128)S(1)}, b...) custom-call(bf16[1024,128]{1,0:T(8,128)(2,1)S(1)} %bitcast.12, s32[8,1024]{1,0:T(8,128)S(1)} %bitcast.14, ...), custom_call_target="tpu_custom_call" | custom-call | flops 17179869184 | bytes 17179868 | tf_op jit(solution)/shard_map/pallas_call | solution.py:201
  9.3 0.0 collective-permute-done.2.around_s
  9.3 0.0 collective-permute-done.1.around_b
  9.3 0.0 collective-permute-done.around_a
  9.4 0.0 copy-start.3
  9.4 0.0 copy-start.9
  9.4 0.0 copy-start.15
  9.4 5.0 %shard_map.169 = (bf16[1024,128]{1,0:T(8,128)(2,1)S(1)}, f32[64,128]{1,0:T(8,128)S(1)}, f32[64,128]{1,0:T(8,128)S(1)}, f32[64,128]{1,0:T(8,128)S(1)}, f32[64,128]{1,0:T(8,128)S(1)}) custom-call(bf16[1024,128]{1,0:T(8,128)(2,1)S(1)} %bitcast.13, bf16[256,128]{1,0:T(8,128)(2,1)S(1)} %collective-permute-done.around_a, ...), custom_call_target="tpu_custom_call" | custom-call | flops 17179869184 | bytes 17179868 | tf_op jit(solution)/shard_map/pallas_call | solution.py:201
  14.4 2.2 %collective-permute-start.3 = (f32[64,128]{1,0:T(8,128)S(1)}, f32[64,128]{1,0:T(8,128)S(1)}, u32[]{:S(2)}, u32[]{:S(2)}) collective-permute-start(f32[64,128]{1,0:T(8,128)S(1)} %get-tuple-element.23), channel_id=1, source_target_pairs={{0,2},{2,0},{4,6},{6,4},{8,10},{10,8},{12,14},{14,12},{1,3},{3,1},... | collective-permute-start | bytes 98312 | tf_op jit(solution)/shard_map/ppermute | solution.py:220
  16.6 0.0 collective-permute-start.4
  16.6 0.5 %collective-permute-start.5 = (f32[64,128]{1,0:T(8,128)S(1)}, f32[64,128]{1,0:T(8,128)S(1)}, u32[]{:S(2)}, u32[]{:S(2)}) collective-permute-start(f32[64,128]{1,0:T(8,128)S(1)} %get-tuple-element.25), channel_id=1, source_target_pairs={{0,1},{1,0},{2,3},{3,2},{4,5},{5,4},{6,7},{7,6},{8,9},{9,8},{10,11... | collective-permute-start | bytes 98312 | tf_op jit(solution)/shard_map/ppermute | solution.py:222
  17.1 1.4 %collective-permute-done.3.from_a = f32[64,128]{1,0:T(8,128)S(1)} collective-permute-done((f32[64,128]{1,0:T(8,128)S(1)}, f32[64,128]{1,0:T(8,128)S(1)}, u32[]{:S(2)}, u32[]{:S(2)}) %collective-permute-start.3) | collective-permute-done | bytes 32800 | tf_op jit(solution)/shard_map/ppermute | solution.py:220
  18.5 0.0 collective-permute-done.4.from_b
  18.5 0.0 copy-start.4
  18.6 0.0 copy-start.8
  18.6 0.4 %shard_map.171.own = bf16[64,128]{1,0:T(8,128)(2,1)S(1)} custom-call(bf16[64,128]{1,0:T(8,128)(2,1)S(1)} %copy-done.9, f32[64,128]{1,0:T(8,128)S(1)} %get-tuple-element.22.own, f32[64,128]{1,0:T(8,128)S(1)} %collective-permute-done.3.from_a, f32[64,128]{1,0:T(8,128)S(1)} %collective-permute-done.4.from_b, f32[64,128]{1,0:T(8,128)S(1)} %collective-permute-done.5.from_s, ...), custom_call_target="tpu_custom_call" | custom-call | flops 4294967296 | bytes 4294967 | tf_op jit(solution)/shard_map/pallas_call | solution.py:201
  19.0 0.0 collective-permute-start.8
  19.0 0.5 %collective-permute-start.7 = (bf16[64,128]{1,0:T(8,128)(2,1)S(1)}, bf16[64,128]{1,0:T(8,128)(2,1)S(1)}, u32[]{:S(2)}, u32[]{:S(2)}) collective-permute-start(bf16[64,128]{1,0:T(8,128)(2,1)S(1)} %shard_map.171.own), channel_id=1, source_target_pairs={{0,1},{1,0},{2,4},{3,5},{4,2},{5,3},{6,8},{7,9},{8,6},{9,7},{10,12... | collective-permute-start | bytes 49160 | tf_op jit(solution)/shard_map/ppermute | solution.py:221
  19.5 5.5 %collective-permute-start.6 = (bf16[64,128]{1,0:T(8,128)(2,1)S(1)}, bf16[64,128]{1,0:T(8,128)(2,1)S(1)}, u32[]{:S(2)}, u32[]{:S(2)}) collective-permute-start(bf16[64,128]{1,0:T(8,128)(2,1)S(1)} %shard_map.171.own), channel_id=1, source_target_pairs={{0,2},{2,0},{4,6},{6,4},{8,10},{10,8},{12,14},{14,12},{1,3},{3,1},... | collective-permute-start | bytes 49160 | tf_op jit(solution)/shard_map/ppermute | solution.py:220
  25.1 0.2 shard_map.170.base
  25.3 0.0 collective-permute-done.7.from_b
  25.3 1.5 %collective-permute-done.6.from_a = bf16[64,128]{1,0:T(8,128)(2,1)S(1)} collective-permute-done((bf16[64,128]{1,0:T(8,128)(2,1)S(1)}, bf16[64,128]{1,0:T(8,128)(2,1)S(1)}, u32[]{:S(2)}, u32[]{:S(2)}) %collective-permute-start.6) | collective-permute-done | bytes 16416 | tf_op jit(solution)/shard_map/ppermute | solution.py:220
  26.8 1.8 %shard_map.172 = (bf16[1024,128]{1,0:T(8,128)(2,1)}, bf16[64,128]{1,0:T(8,128)(2,1)}) custom-call(bf16[1024,128]{1,0:T(8,128)(2,1)S(1)} %get-tuple-element.20.fine_mid, f32[1024,128]{1,0:T(8,128)S(1)} %shard_map.170.base, bf16[1024,256]{1,0:T(8,128)(2,1)S(1)} %get-tuple-element.21.lift, bf16[64,128]{1,0:T(8,128)(2,1)S(1)} %shard_map.171.own, ...), custom_call_target="tpu_custom_call" | custom-call | flops 4294967296 | bytes 4294967 | tf_op jit(solution)/shard_map/pallas_call | solution.py:201
  (24 shorter events, 0.1 us)
Async XLA Ops:
  0.6 1.0 %copy-start = (bf16[1,1,1024,128]{3,2,1,0:T(8,128)(2,1)S(1)}, bf16[1,1,1024,128]{3,2,1,0:T(8,128)(2,1)}, u32[]{:S(2)}) copy-start(bf16[1,1,1024,128]{3,2,1,0:T(8,128)(2,1)} %param.16) | copy-start | bytes 786436
  1.6 4.7 %copy-start.1 = (bf16[2,128,128]{2,1,0:T(8,128)(2,1)S(1)}, bf16[2,128,128]{2,1,0:T(8,128)(2,1)}, u32[]{:S(2)}) copy-start(bf16[2,128,128]{2,1,0:T(8,128)(2,1)} %edge_in.3) | copy-start | bytes 196612
  1.6 4.7 %copy-start.5 = (s32[1,1,1024,8]{2,3,1,0:T(8,128)S(1)}, s32[1,1,1024,8]{2,3,1,0:T(8,128)}, u32[]{:S(2)}) copy-start(s32[1,1,1024,8]{2,3,1,0:T(8,128)} %param.17) | copy-start | bytes 98308
  1.6 4.7 %copy-start.10 = (s32[1,1,1024]{2,1,0:T(1,128)S(1)}, s32[1,1,1024]{2,1,0:T(1,128)}, u32[]{:S(2)}) copy-start(s32[1,1,1024]{2,1,0:T(1,128)} %param.18) | copy-start | bytes 12292
  1.6 4.7 %copy-start.11 = (bf16[1,1,1024]{2,1,0:T(2,128)(2,1)S(1)}, bf16[1,1,1024]{2,1,0:T(2,128)(2,1)}, u32[]{:S(2)}) copy-start(bf16[1,1,1024]{2,1,0:T(2,128)(2,1)} %param.19) | copy-start | bytes 6148
  1.6 4.7 %copy-start.12 = (f32[128]{0:T(128)S(1)}, f32[128]{0:T(128)}, u32[]{:S(2)}) copy-start(f32[128]{0:T(128)} %param.22) | copy-start | bytes 1540
  1.6 7.7 %collective-permute-start.2 = (bf16[256,128]{1,0:T(8,128)(2,1)S(1)}, bf16[256,128]{1,0:T(8,128)(2,1)S(1)}, u32[]{:S(2)}, u32[]{:S(2)}) collective-permute-start(bf16[256,128]{1,0:T(8,128)(2,1)S(1)} %shard_map.167), channel_id=1, source_target_pairs={{0,1},{1,0},{2,3},{3,2},{4,5},{5,4},{6,7},{7,6},{8,9},{9,8},{10,11... | collective-permute-start | bytes 196616 | tf_op jit(solution)/shard_map/ppermute | solution.py:222
  2.1 7.2 %collective-permute-start.1 = (bf16[256,128]{1,0:T(8,128)(2,1)S(1)}, bf16[256,128]{1,0:T(8,128)(2,1)S(1)}, u32[]{:S(2)}, u32[]{:S(2)}) collective-permute-start(bf16[256,128]{1,0:T(8,128)(2,1)S(1)} %shard_map.167), channel_id=1, source_target_pairs={{0,1},{1,0},{2,4},{3,5},{4,2},{5,3},{6,8},{7,9},{8,6},{9,7},{10,12... | collective-permute-start | bytes 196616 | tf_op jit(solution)/shard_map/ppermute | solution.py:221
  2.2 7.1 %collective-permute-start = (bf16[256,128]{1,0:T(8,128)(2,1)S(1)}, bf16[256,128]{1,0:T(8,128)(2,1)S(1)}, u32[]{:S(2)}, u32[]{:S(2)}) collective-permute-start(bf16[256,128]{1,0:T(8,128)(2,1)S(1)} %shard_map.167), channel_id=1, source_target_pairs={{0,2},{2,0},{4,6},{6,4},{8,10},{10,8},{12,14},{14,12},{1,3},{3,1},... | collective-permute-start | bytes 196616 | tf_op jit(solution)/shard_map/ppermute | solution.py:220
  6.3 3.1 %copy-start.2 = (bf16[2,128,128]{2,1,0:T(8,128)(2,1)S(1)}, bf16[2,128,128]{2,1,0:T(8,128)(2,1)}, u32[]{:S(2)}) copy-start(bf16[2,128,128]{2,1,0:T(8,128)(2,1)} %node_in.1) | copy-start | bytes 196612
  6.3 3.1 %copy-start.6 = (bf16[128,128]{1,0:T(8,128)(2,1)S(1)}, bf16[128,128]{1,0:T(8,128)(2,1)}, u32[]{:S(2)}) copy-start(bf16[128,128]{1,0:T(8,128)(2,1)} %edge_out.1) | copy-start | bytes 98308
  6.3 3.1 %copy-start.7 = (bf16[128,128]{1,0:T(8,128)(2,1)S(1)}, bf16[128,128]{1,0:T(8,128)(2,1)}, u32[]{:S(2)}) copy-start(bf16[128,128]{1,0:T(8,128)(2,1)} %node_out.1) | copy-start | bytes 98308
  6.3 3.0 %copy-start.13 = (f32[128]{0:T(128)S(1)}, f32[128]{0:T(128)}, u32[]{:S(2)}) copy-start(f32[128]{0:T(128)} %param.25) | copy-start | bytes 1540
  6.3 3.0 %copy-start.14 = (f32[128]{0:T(128)S(1)}, f32[128]{0:T(128)}, u32[]{:S(2)}) copy-start(f32[128]{0:T(128)} %param.27) | copy-start | bytes 1540
  9.4 9.1 %copy-start.3 = (bf16[2,128,128]{2,1,0:T(8,128)(2,1)S(1)}, bf16[2,128,128]{2,1,0:T(8,128)(2,1)}, u32[]{:S(2)}) copy-start(bf16[2,128,128]{2,1,0:T(8,128)(2,1)} %coarse_w.1) | copy-start | bytes 196612
  9.4 9.1 %copy-start.9 = (bf16[64,128]{1,0:T(8,128)(2,1)S(1)}, bf16[64,128]{1,0:T(8,128)(2,1)}, u32[]{:S(2)}) copy-start(bf16[64,128]{1,0:T(8,128)(2,1)} %state.1) | copy-start | bytes 49156
  9.4 9.1 %copy-start.15 = (f32[128]{0:T(128)S(1)}, f32[128]{0:T(128)}, u32[]{:S(2)}) copy-start(f32[128]{0:T(128)} %param.28) | copy-start | bytes 1540
  14.4 4.1 %collective-permute-start.3 = (f32[64,128]{1,0:T(8,128)S(1)}, f32[64,128]{1,0:T(8,128)S(1)}, u32[]{:S(2)}, u32[]{:S(2)}) collective-permute-start(f32[64,128]{1,0:T(8,128)S(1)} %get-tuple-element.23), channel_id=1, source_target_pairs={{0,2},{2,0},{4,6},{6,4},{8,10},{10,8},{12,14},{14,12},{1,3},{3,1},... | collective-permute-start | bytes 98312 | tf_op jit(solution)/shard_map/ppermute | solution.py:220
  16.6 1.9 %collective-permute-start.4 = (f32[64,128]{1,0:T(8,128)S(1)}, f32[64,128]{1,0:T(8,128)S(1)}, u32[]{:S(2)}, u32[]{:S(2)}) collective-permute-start(f32[64,128]{1,0:T(8,128)S(1)} %get-tuple-element.24), channel_id=1, source_target_pairs={{0,1},{1,0},{2,4},{3,5},{4,2},{5,3},{6,8},{7,9},{8,6},{9,7},{10,12... | collective-permute-start | bytes 98312 | tf_op jit(solution)/shard_map/ppermute | solution.py:221
  16.6 1.9 %collective-permute-start.5 = (f32[64,128]{1,0:T(8,128)S(1)}, f32[64,128]{1,0:T(8,128)S(1)}, u32[]{:S(2)}, u32[]{:S(2)}) collective-permute-start(f32[64,128]{1,0:T(8,128)S(1)} %get-tuple-element.25), channel_id=1, source_target_pairs={{0,1},{1,0},{2,3},{3,2},{4,5},{5,4},{6,7},{7,6},{8,9},{9,8},{10,11... | collective-permute-start | bytes 98312 | tf_op jit(solution)/shard_map/ppermute | solution.py:222
  18.5 6.5 %copy-start.4 = (bf16[2,128,128]{2,1,0:T(8,128)(2,1)S(1)}, bf16[2,128,128]{2,1,0:T(8,128)(2,1)}, u32[]{:S(2)}) copy-start(bf16[2,128,128]{2,1,0:T(8,128)(2,1)} %prolong_in.3) | copy-start | bytes 196612
  18.6 8.2 %copy-start.8 = (bf16[128,128]{1,0:T(8,128)(2,1)S(1)}, bf16[128,128]{1,0:T(8,128)(2,1)}, u32[]{:S(2)}) copy-start(bf16[128,128]{1,0:T(8,128)(2,1)} %prolong_out.1) | copy-start | bytes 98308
  19.0 6.3 %collective-permute-start.8 = (bf16[64,128]{1,0:T(8,128)(2,1)S(1)}, bf16[64,128]{1,0:T(8,128)(2,1)S(1)}, u32[]{:S(2)}, u32[]{:S(2)}) collective-permute-start(bf16[64,128]{1,0:T(8,128)(2,1)S(1)} %shard_map.171.own), channel_id=1, source_target_pairs={{0,1},{1,0},{2,3},{3,2},{4,5},{5,4},{6,7},{7,6},{8,9},{9,8},{10,11... | collective-permute-start | bytes 49160 | tf_op jit(solution)/shard_map/ppermute | solution.py:222
  19.0 6.2 %collective-permute-start.7 = (bf16[64,128]{1,0:T(8,128)(2,1)S(1)}, bf16[64,128]{1,0:T(8,128)(2,1)S(1)}, u32[]{:S(2)}, u32[]{:S(2)}) collective-permute-start(bf16[64,128]{1,0:T(8,128)(2,1)S(1)} %shard_map.171.own), channel_id=1, source_target_pairs={{0,1},{1,0},{2,4},{3,5},{4,2},{5,3},{6,8},{7,9},{8,6},{9,7},{10,12... | collective-permute-start | bytes 49160 | tf_op jit(solution)/shard_map/ppermute | solution.py:221
  19.5 7.2 %collective-permute-start.6 = (bf16[64,128]{1,0:T(8,128)(2,1)S(1)}, bf16[64,128]{1,0:T(8,128)(2,1)S(1)}, u32[]{:S(2)}, u32[]{:S(2)}) collective-permute-start(bf16[64,128]{1,0:T(8,128)(2,1)S(1)} %shard_map.171.own), channel_id=1, source_target_pairs={{0,2},{2,0},{4,6},{6,4},{8,10},{10,8},{12,14},{14,12},{1,3},{3,1},... | collective-permute-start | bytes 49160 | tf_op jit(solution)/shard_map/ppermute | solution.py:220

commit v3 on v2

--- a/solution.py
+++ b/solution.py
@@ -14,6 +14,8 @@
 BLOCK = 128
 GROUP = 2
 UNROLL = 8
+CHUNK = 1024
+PARTS = 4
 
 
 def mm(a, b):
@@ -64,28 +66,17 @@
     return jnp.concatenate(parts, axis=1)
 
 
-def gathered(cols, table, degree, block):
-    rim = table.shape[0] // 2
-    pairs = []
-    for k in range(0, degree, GROUP):
-        ones = jnp.concatenate([one_hot(spread(cols, k + g, block), -rim, 2 * rim) for g in range(GROUP)], axis=0)
-        got = mm(ones, table).astype(BF16)
-        for g in range(GROUP):
-            part = got[g * block : (g + 1) * block]
-            pairs.append((part[:, :128], part[:, 128:], spread(cols, degree + k + g, block)))
-    return pairs
-
-
 def boundary_kernel(tiles, boundary):
     boundary[...] = tiles[: boundary.shape[0], :]
 
 
 def local_kernel(
-    n, co_rows, tiles, sources, parents, weights, edge_in, edge_bias, cols, near, dst, scale, pool, lift
+    n, co_rows, tiles, around_s, sources, parents, weights, edge_in, edge_bias, cols, near, scale, pool, lift, picked
 ):
     nodes, width = tiles.shape
     degree = near.shape[0]
     rim = nodes // 4
+    j = lax.axis_index("ty")
     index = sources[...]
     ids = parents[...]
     block_of = quotient(ids, co_rows)
@@ -93,74 +84,93 @@
     for at, owner in enumerate(owners(n)):
         slot = jnp.where(block_of == owner, slot + at * co_rows, slot)
     slot = slot.astype(F32)
+    piece = quotient(index, rim)
+    low = index & (rim - 1)
+    nowhere = 2 * rim
     rows = [
         ((index & (2 * rim - 1)) - rim).astype(F32),
-        quotient(index, 2 * rim).astype(F32),
+        jnp.where(piece == 7 - j, low, nowhere).astype(F32),
+        jnp.where((piece == 4) | (piece == 5), index - 5 * rim, nowhere).astype(F32),
+        piece.astype(F32),
         slot,
         weights[...].astype(F32),
         jnp.zeros((6, nodes), F32),
     ]
     turned = jnp.concatenate(rows, axis=0).T
     cols[...] = turned
-    scale[...] = turned[:, 2 * degree + 1 : 2 * degree + 2] * jnp.ones((1, width), F32)
-    dst[...] = mm(tiles[...], edge_in[0]) + edge_bias[...]
+    scale[...] = turned[:, 4 * degree + 1 : 4 * degree + 2] * jnp.ones((1, width), F32)
     row = lax.broadcasted_iota(I32, pool.shape, 0).astype(F32).astype(BF16)
     pool[...] = jnp.where(row == slot.astype(BF16), jnp.ones((), BF16), jnp.zeros((), BF16))
-    lift[...] = one_hot(spread(cols[...], 2 * degree, nodes), 0, 4 * co_rows)
+    lift[...] = one_hot(spread(cols[...], 4 * degree, nodes), 0, 4 * co_rows)
+    project = edge_in[1]
+    empty = jnp.zeros_like(project)
+    project = jnp.concatenate(
+        [jnp.concatenate([project, empty], axis=1), jnp.concatenate([empty, project], axis=1)], axis=0
+    )
     table = jnp.concatenate([tiles[: 2 * rim, :], tiles[2 * rim :, :]], axis=1)
+    side = around_s[...]
 
     def step(at, _):
         first = pl.multiple_of(at * BLOCK, BLOCK)
         here = pl.ds(first, BLOCK)
-        for k, (low, high, quarter) in enumerate(gathered(cols[here, :], table, degree, BLOCK)):
-            near[k, here, :] = jnp.where(quarter == jnp.ones((), BF16), high, low)
+        col = cols[here, :]
+        for k in range(0, degree, GROUP):
+            group = range(k, k + GROUP)
+            ones = jnp.concatenate([one_hot(spread(col, g, BLOCK), -rim, 2 * rim) for g in group], axis=0)
+            got = mm(ones, table).astype(BF16)
+            ones = jnp.concatenate([one_hot(spread(col, degree + g, BLOCK), 0, rim) for g in group], axis=0)
+            beside = mm(ones, side).astype(BF16)
+            for g in group:
+                part = slice((g - k) * BLOCK, (g - k + 1) * BLOCK)
+                of = spread(col, 3 * degree + g, BLOCK)
+                value = jnp.where(of < jnp.full((), 2, BF16), got[part, :width], got[part, width:])
+                value = jnp.where(of < jnp.full((), 4, BF16), value, beside[part])
+                picked[g // 2, here, g % 2 * width : (g % 2 + 1) * width] = value
         return 0
 
     lax.fori_loop(0, nodes // BLOCK, step, 0, unroll=UNROLL)
+    dst = mm(tiles[...], edge_in[0]) + edge_bias[...]
+    for pair in range(degree // 2):
+        src = mm(picked[pair], project)
+        near[2 * pair] = dst + src[:, :width]
+        near[2 * pair + 1] = dst + src[:, width:]
 
 
 def node_kernel(
-    n, tiles, around_a, around_b, around_s, cols, near, dst, scale, pool,
-    edge_in, edge_out, node_in, node_bias, node_out, node_gain,
+    n, tiles, around_a, around_b, cols, near, scale, pool, edge_in, edge_out, node_in, node_bias, node_out, node_gain,
     fine_mid, own, to_a, to_b, to_s, total, weighted,
 ):
     nodes, width = tiles.shape
     degree = near.shape[0]
+    rim = nodes // 4
     co_rows = own.shape[0]
     i, j, even = place(n)
     none = jnp.zeros(around_a.shape, BF16)
-    got_a, got_b, got_s = around_a[...], around_b[...], around_s[...]
+    got_a, got_b = around_a[...], around_b[...]
     before = jnp.where(i > 0, jnp.where(even, got_b, got_a), none)
     after = jnp.where(i < n - 1, jnp.where(even, got_a, got_b), none)
-    left, right = jnp.where(j > 0, got_s, none), jnp.where(j < 1, got_s, none)
-    table = jnp.concatenate([jnp.concatenate([before, left], axis=1), jnp.concatenate([after, right], axis=1)], axis=0)
-    project = edge_in[1]
-    empty = jnp.zeros_like(project)
-    project = jnp.concatenate(
-        [jnp.concatenate([project, empty], axis=1), jnp.concatenate([empty, project], axis=1)], axis=0
-    )
+    table = split(mm(jnp.concatenate([before, after], axis=0), edge_in[1]))
 
     def step(at, _):
         first = pl.multiple_of(at * BLOCK, BLOCK)
         here = pl.ds(first, BLOCK)
-        dst_part = dst[here, :]
+        col = cols[here, :]
         sums = jnp.zeros((BLOCK, width), F32)
-        picked = []
-        for k, (low, high, quarter) in enumerate(gathered(cols[here, :], table, degree, BLOCK)):
-            far = jnp.where(quarter == jnp.full((), 3, BF16), high, low)
-            picked.append(jnp.where(quarter < jnp.full((), 2, BF16), near[k, here, :], far))
-        for k in range(0, degree, 2):
-            got = mm(jnp.concatenate([picked[k], picked[k + 1]], axis=1), project)
-            for part in (got[:, :width], got[:, width:]):
-                sums = sums + silu(dst_part + part).astype(BF16).astype(F32)
+        for k in range(0, degree, GROUP):
+            ones = [one_hot(spread(col, 2 * degree + k + g, BLOCK), -rim, 2 * rim) for g in range(GROUP)]
+            got = mm(jnp.concatenate(ones, axis=0), table)
+            for g in range(GROUP):
+                part = got[g * BLOCK : (g + 1) * BLOCK]
+                edge = near[k + g, here, :] + (part[:, :width] + part[:, width:])
+                sums = sums + silu(edge).astype(BF16).astype(F32)
         total[here, :] = sums
         return 0
 
     lax.fori_loop(0, nodes // BLOCK, step, 0, unroll=UNROLL)
     node_weights = jnp.concatenate([node_in[0], node_in[1]], axis=0)
     out_twice = jnp.concatenate([edge_out[...], edge_out[...]], axis=0)
-    for first in range(0, nodes, 256):
-        here = pl.ds(first, 256)
+    for first in range(0, nodes, CHUNK):
+        here = pl.ds(first, CHUNK)
         aggregate = mm(split(total[here, :]), out_twice).astype(BF16)
         both = jnp.concatenate([tiles[here, :], aggregate], axis=1)
         hidden = silu(mm(both, node_weights) + node_bias[...]).astype(BF16)
@@ -184,25 +194,33 @@
     out[...] = (total + mm(hidden, coarse_w[1])).astype(BF16)
 
 
-def prolong_kernel(fine_mid, base, lift, own, from_a, from_b, from_s, prolong_in, prolong_out, out, coarse_out):
-    coarse_out[...] = own[...]
+def prolong_kernel(
+    fine_mid, base, lift, own, from_a, from_b, from_s, prolong_in, prolong_out, out, coarse_out, ready, sems
+):
     nodes, width = fine_mid.shape
+    copies = [pltpu.make_async_copy(own, coarse_out, sems.at[PARTS])]
+    copies[0].start()
     coarse = jnp.concatenate([own[...], from_a[...], from_b[...], from_s[...]], axis=0)
     terms = split(mm(coarse, prolong_in[1]))
-    block = 256
-    for first in range(0, nodes, block):
-        here = pl.ds(first, block)
-        lifted = mm(lift[here, :], terms)
-        hidden = silu(base[here, :] + (lifted[:, :width] + lifted[:, width:])).astype(BF16)
-        out[here, :] = (fine_mid[here, :].astype(F32) + mm(hidden, prolong_out[...])).astype(BF16)
-
-
-def call(kernel, outs, *args, flops=0, scratch=()):
+    lifted = mm(lift[...], terms)
+    hidden = silu(base[...] + (lifted[:, :width] + lifted[:, width:])).astype(BF16)
+    block = nodes // PARTS
+    for at in range(PARTS):
+        part = slice(at * block, (at + 1) * block)
+        here = pl.ds(at * block, block)
+        ready[here, :] = (fine_mid[here, :].astype(F32) + mm(hidden[part], prolong_out[...])).astype(BF16)
+        copies.append(pltpu.make_async_copy(ready.at[here], out.at[here], sems.at[at]))
+        copies[-1].start()
+    for copy in copies:
+        copy.wait()
+
+
+def call(kernel, outs, *args, flops=0, scratch=(), to=pltpu.VMEM):
     return pl.pallas_call(
         kernel,
         out_shape=outs,
         in_specs=[pl.BlockSpec(memory_space=pltpu.VMEM)] * len(args),
-        out_specs=[pl.BlockSpec(memory_space=pltpu.VMEM)] * len(outs),
+        out_specs=[pl.BlockSpec(memory_space=to)] * len(outs),
         scratch_shapes=scratch,
         compiler_params=pltpu.CompilerParams(vmem_limit_bytes=VMEM_LIMIT),
         cost_estimate=pl.CostEstimate(flops=flops, bytes_accessed=flops // 1000, transcendentals=0),
@@ -249,24 +267,24 @@
 
     latents = tiles[0, 0]
     (boundary,) = call(boundary_kernel, [shape((nodes // 4, width), BF16)], latents, flops=2**33)
-    around = exchange(n, boundary, boundary, boundary)
-    cols, near, dst, scale, pool, lift = call(
+    around_a, around_b, around_s = exchange(n, boundary, boundary, boundary)
+    cols, near, scale, pool, lift = call(
         functools.partial(local_kernel, n, co_rows),
         [
-            shape((nodes, 24), F32),
-            shape((degree, nodes, width), BF16),
-            shape((nodes, width), F32),
+            shape((nodes, 40), F32),
+            shape((degree, nodes, width), F32),
             shape((nodes, width), F32),
             shape((4 * co_rows, nodes), BF16),
             shape((nodes, 4 * co_rows), BF16),
         ],
-        latents, jnp.swapaxes(sources[0, 0], 0, 1), parents[0], restrict_w[0], edge_in, edge_bias[None],
+        latents, around_s, jnp.swapaxes(sources[0, 0], 0, 1), parents[0], restrict_w[0], edge_in, edge_bias[None],
         flops=2**34,
+        scratch=[pltpu.VMEM((degree // 2, nodes, 2 * width), BF16)],
     )
     fine_mid, own, to_a, to_b, to_s = call(
         functools.partial(node_kernel, n),
         [shape((nodes, width), BF16)] + [shape((co_rows, width), F32)] * 4,
-        latents, *around, cols, near, dst, scale, pool,
+        latents, around_a, around_b, cols, near, scale, pool,
         edge_in, edge_out, node_in, node_bias[None], node_out, node_gain[None],
         flops=2**34,
         scratch=[pltpu.VMEM((nodes, width), F32), pltpu.VMEM((nodes, width), BF16)],
@@ -284,6 +302,8 @@
         prolong_kernel,
         [shape((nodes, width), BF16), shape((co_rows, width), BF16)],
         fine_mid, base, lift, coarse_out, *beside, prolong_in, prolong_out,
+        to=pl.ANY,
+        scratch=[pltpu.VMEM((nodes, width), BF16), pltpu.SemaphoreType.DMA((PARTS + 1,))],
         flops=2**32,
     )
     return (fine_out[None, None], coarse_out)

time: 28.7 us -> 27 us (0.941)
  starting transfers between devices: 13.4 us -> 10 us
  waiting for transfers between devices: 2.89 us -> 4.52 us
    ppermute x3, starting transfers between devices: 11.8 us -> 8.38 us  [exchange(): lax.ppermute(to_a, 'tx', pairs_a)]
    ppermute x3, waiting for transfers between devices: 2.87 us -> 4.5 us  [exchange(): lax.ppermute(to_a, 'tx', pairs_a)]
  transfers between devices with their start and end apart: 9 -> 9, of which waited for: 2 -> 2; matrix products, arithmetic and copies ran while one was open for 0% -> 0% of each run, Pallas kernels for 11% -> 18%
where the time goes in v3:
time: 27 us; the launch traced here: 26.8 us
  Pallas kernels  10.4 us (39%)
  starting transfers between devices  10 us (37%)
  waiting for transfers between devices  4.52 us (17%)
  local copies, waits for them, and re-layouts  1.03 us (4%)
  between operations  0.89 us (3%)
    pallas_call x6, Pallas kernels, call(): pl.pallas_call(kernel, out_shape=outs, in_specs=[pl.BlockSpec(memory_spac...  10.4 us
    ppermute x3, starting transfers between devices, exchange(): lax.ppermute(to_a, 'tx', pairs_a)  8.38 us
    ppermute x3, waiting for transfers between devices, exchange(): lax.ppermute(to_a, 'tx', pairs_a)  4.5 us
    ppermute x3, starting transfers between devices, exchange(): lax.ppermute(to_s, 'ty', [(0, 1), (1, 0)])  1.07 us
    unnamed x32, local copies, waits for them, and re-layouts  1.03 us
    ppermute x3, starting transfers between devices, exchange(): lax.ppermute(to_b, ('tx', 'ty'), pairs_b)  0.58 us
  transfers between devices with their start and end apart: 9, of which 2 were waited for; matrix products, arithmetic and copies ran while one was open for 0% of the time, Pallas kernels for 18%

profile of v3, /device:TPU:0, one launch (start us, length us, event | category | flops | bytes accessed | tf_op | source)
XLA Modules:
  0.0 26.8 jit_solution(9301420321953956017)
XLA Ops:
  0.6 0.9 %copy-done = bf16[1,1,1024,128]{3,2,1,0:T(8,128)(2,1)S(1)} copy-done((bf16[1,1,1024,128]{3,2,1,0:T(8,128)(2,1)S(1)}, bf16[1,1,1024,128]{3,2,1,0:T(8,128)(2,1)}, u32[]{:S(2)}) %copy-start) | copy-done | bytes 262168
  1.6 0.5 %collective-permute-start.2 = (bf16[256,128]{1,0:T(8,128)(2,1)S(1)}, bf16[256,128]{1,0:T(8,128)(2,1)S(1)}, u32[]{:S(2)}, u32[]{:S(2)}) collective-permute-start(bf16[256,128]{1,0:T(8,128)(2,1)S(1)} %shard_map.167), channel_id=1, source_target_pairs={{0,1},{1,0},{2,3},{3,2},{4,5},{5,4},{6,7},{7,6},{8,9},{9,8},{10,11... | collective-permute-start | bytes 196616 | tf_op jit(solution)/shard_map/ppermute | solution.py:240
  2.1 0.1 collective-permute-start.1
  2.2 4.0 %collective-permute-start = (bf16[256,128]{1,0:T(8,128)(2,1)S(1)}, bf16[256,128]{1,0:T(8,128)(2,1)S(1)}, u32[]{:S(2)}, u32[]{:S(2)}) collective-permute-start(bf16[256,128]{1,0:T(8,128)(2,1)S(1)} %shard_map.167), channel_id=1, source_target_pairs={{0,2},{2,0},{4,6},{6,4},{8,10},{10,8},{12,14},{14,12},{1,3},{3,1},... | collective-permute-start | bytes 196616 | tf_op jit(solution)/shard_map/ppermute | solution.py:238
  6.2 0.0 collective-permute-done.2.around_s
  6.3 0.0 copy-start.2
  6.3 0.0 copy-start.6
  6.3 0.0 copy-start.7
  6.3 0.0 copy-start.13
  6.3 0.0 copy-start.14
  6.4 4.7 %shard_map.168 = (f32[1024,40]{1,0:T(8,128)S(1)}, f32[8,1024,128]{2,1,0:T(8,128)S(1)}, f32[1024,128]{1,0:T(8,128)S(1)}, bf16[256,1024]{1,0:T(8,128)(2,1)S(1)}, bf16[1024,256]{1,0:T(8,128)(2,1)S(1)}) custom-call(bf16[1024,128]{1,0:T(8,128)(2,1)S(1)} %bitcast.12, bf16[256,128]{1,0:T(8,128)(2,1)S(1)} %collective-permute-done.2.around_s, ...), custom_call_target="tpu_custom_call" | custom-call | flops 17179869184 | bytes 17179868 | tf_op jit(solution)/shard_map/pallas_call | solution.py:219
  11.1 0.0 collective-permute-done.around_a
  11.1 0.0 copy-start.3
  11.1 0.0 copy-start.9
  11.1 0.0 copy-start.15
  11.2 3.7 %shard_map.169 = (bf16[1024,128]{1,0:T(8,128)(2,1)S(1)}, f32[64,128]{1,0:T(8,128)S(1)}, f32[64,128]{1,0:T(8,128)S(1)}, f32[64,128]{1,0:T(8,128)S(1)}, f32[64,128]{1,0:T(8,128)S(1)}) custom-call(bf16[1024,128]{1,0:T(8,128)(2,1)S(1)} %bitcast.13, bf16[256,128]{1,0:T(8,128)(2,1)S(1)} %collective-permute-done.around_a, ...), custom_call_target="tpu_custom_call" | custom-call | flops 17179869184 | bytes 17179868 | tf_op jit(solution)/shard_map/pallas_call | solution.py:219
  14.9 0.5 %collective-permute-start.3 = (f32[64,128]{1,0:T(8,128)S(1)}, f32[64,128]{1,0:T(8,128)S(1)}, u32[]{:S(2)}, u32[]{:S(2)}) collective-permute-start(f32[64,128]{1,0:T(8,128)S(1)} %get-tuple-element.21), channel_id=1, source_target_pairs={{0,2},{2,0},{4,6},{6,4},{8,10},{10,8},{12,14},{14,12},{1,3},{3,1},... | collective-permute-start | bytes 98312 | tf_op jit(solution)/shard_map/ppermute | solution.py:238
  15.3 0.0 collective-permute-start.4
  15.3 0.5 %collective-permute-start.5 = (f32[64,128]{1,0:T(8,128)S(1)}, f32[64,128]{1,0:T(8,128)S(1)}, u32[]{:S(2)}, u32[]{:S(2)}) collective-permute-start(f32[64,128]{1,0:T(8,128)S(1)} %get-tuple-element.23), channel_id=1, source_target_pairs={{0,1},{1,0},{2,3},{3,2},{4,5},{5,4},{6,7},{7,6},{8,9},{9,8},{10,11... | collective-permute-start | bytes 98312 | tf_op jit(solution)/shard_map/ppermute | solution.py:240
  15.8 3.0 %collective-permute-done.3.from_a = f32[64,128]{1,0:T(8,128)S(1)} collective-permute-done((f32[64,128]{1,0:T(8,128)S(1)}, f32[64,128]{1,0:T(8,128)S(1)}, u32[]{:S(2)}, u32[]{:S(2)}) %collective-permute-start.3) | collective-permute-done | bytes 32800 | tf_op jit(solution)/shard_map/ppermute | solution.py:238
  18.9 0.0 collective-permute-done.4.from_b
  18.9 0.0 collective-permute-done.5.from_s
  18.9 0.0 copy-start.4
  18.9 0.0 copy-start.8
  18.9 0.4 %shard_map.171.own = bf16[64,128]{1,0:T(8,128)(2,1)S(1)} custom-call(bf16[64,128]{1,0:T(8,128)(2,1)S(1)} %copy-done.9, f32[64,128]{1,0:T(8,128)S(1)} %get-tuple-element.20.own, f32[64,128]{1,0:T(8,128)S(1)} %collective-permute-done.3.from_a, f32[64,128]{1,0:T(8,128)S(1)} %collective-permute-done.4.from_b, f32[64,128]{1,0:T(8,128)S(1)} %collective-permute-done.5.from_s, ...), custom_call_target="tpu_custom_call" | custom-call | flops 4294967296 | bytes 4294967 | tf_op jit(solution)/shard_map/pallas_call | solution.py:219
  19.3 0.0 collective-permute-start.8
  19.4 0.5 %collective-permute-start.7 = (bf16[64,128]{1,0:T(8,128)(2,1)S(1)}, bf16[64,128]{1,0:T(8,128)(2,1)S(1)}, u32[]{:S(2)}, u32[]{:S(2)}) collective-permute-start(bf16[64,128]{1,0:T(8,128)(2,1)S(1)} %shard_map.171.own), channel_id=1, source_target_pairs={{0,1},{1,0},{2,4},{3,5},{4,2},{5,3},{6,8},{7,9},{8,6},{9,7},{10,12... | collective-permute-start | bytes 49160 | tf_op jit(solution)/shard_map/ppermute | solution.py:239
  19.9 3.9 %collective-permute-start.6 = (bf16[64,128]{1,0:T(8,128)(2,1)S(1)}, bf16[64,128]{1,0:T(8,128)(2,1)S(1)}, u32[]{:S(2)}, u32[]{:S(2)}) collective-permute-start(bf16[64,128]{1,0:T(8,128)(2,1)S(1)} %shard_map.171.own), channel_id=1, source_target_pairs={{0,2},{2,0},{4,6},{6,4},{8,10},{10,8},{12,14},{14,12},{1,3},{3,1},... | collective-permute-start | bytes 49160 | tf_op jit(solution)/shard_map/ppermute | solution.py:238
  23.8 0.2 shard_map.170.base
  24.0 0.0 collective-permute-done.7.from_b
  24.0 1.5 %collective-permute-done.6.from_a = bf16[64,128]{1,0:T(8,128)(2,1)S(1)} collective-permute-done((bf16[64,128]{1,0:T(8,128)(2,1)S(1)}, bf16[64,128]{1,0:T(8,128)(2,1)S(1)}, u32[]{:S(2)}, u32[]{:S(2)}) %collective-permute-start.6) | collective-permute-done | bytes 16416 | tf_op jit(solution)/shard_map/ppermute | solution.py:238
  25.5 1.3 %shard_map.172 = (bf16[1024,128]{1,0:T(8,128)(2,1)}, bf16[64,128]{1,0:T(8,128)(2,1)}) custom-call(bf16[1024,128]{1,0:T(8,128)(2,1)S(1)} %get-tuple-element.18.fine_mid, f32[1024,128]{1,0:T(8,128)S(1)} %shard_map.170.base, bf16[1024,256]{1,0:T(8,128)(2,1)S(1)} %get-tuple-element.19.lift, bf16[64,128]{1,0:T(8,128)(2,1)S(1)} %shard_map.171.own, ...), custom_call_target="tpu_custom_call" | custom-call | flops 4294967296 | bytes 4294967 | tf_op jit(solution)/shard_map/pallas_call | solution.py:219
  (24 shorter events, 0.1 us)
Async XLA Ops:
  0.6 1.0 %copy-start = (bf16[1,1,1024,128]{3,2,1,0:T(8,128)(2,1)S(1)}, bf16[1,1,1024,128]{3,2,1,0:T(8,128)(2,1)}, u32[]{:S(2)}) copy-start(bf16[1,1,1024,128]{3,2,1,0:T(8,128)(2,1)} %param.16) | copy-start | bytes 786436
  1.6 4.7 %copy-start.1 = (bf16[2,128,128]{2,1,0:T(8,128)(2,1)S(1)}, bf16[2,128,128]{2,1,0:T(8,128)(2,1)}, u32[]{:S(2)}) copy-start(bf16[2,128,128]{2,1,0:T(8,128)(2,1)} %edge_in.3) | copy-start | bytes 196612
  1.6 4.7 %copy-start.5 = (s32[1,1,1024,8]{2,3,1,0:T(8,128)S(1)}, s32[1,1,1024,8]{2,3,1,0:T(8,128)}, u32[]{:S(2)}) copy-start(s32[1,1,1024,8]{2,3,1,0:T(8,128)} %param.17) | copy-start | bytes 98308
  1.6 4.7 %copy-start.10 = (s32[1,1,1024]{2,1,0:T(1,128)S(1)}, s32[1,1,1024]{2,1,0:T(1,128)}, u32[]{:S(2)}) copy-start(s32[1,1,1024]{2,1,0:T(1,128)} %param.18) | copy-start | bytes 12292
  1.6 4.7 %copy-start.11 = (bf16[1,1,1024]{2,1,0:T(2,128)(2,1)S(1)}, bf16[1,1,1024]{2,1,0:T(2,128)(2,1)}, u32[]{:S(2)}) copy-start(bf16[1,1,1024]{2,1,0:T(2,128)(2,1)} %param.19) | copy-start | bytes 6148
  1.6 4.7 %copy-start.12 = (f32[128]{0:T(128)S(1)}, f32[128]{0:T(128)}, u32[]{:S(2)}) copy-start(f32[128]{0:T(128)} %param.22) | copy-start | bytes 1540
  1.6 4.6 %collective-permute-start.2 = (bf16[256,128]{1,0:T(8,128)(2,1)S(1)}, bf16[256,128]{1,0:T(8,128)(2,1)S(1)}, u32[]{:S(2)}, u32[]{:S(2)}) collective-permute-start(bf16[256,128]{1,0:T(8,128)(2,1)S(1)} %shard_map.167), channel_id=1, source_target_pairs={{0,1},{1,0},{2,3},{3,2},{4,5},{5,4},{6,7},{7,6},{8,9},{9,8},{10,11... | collective-permute-start | bytes 196616 | tf_op jit(solution)/shard_map/ppermute | solution.py:240
  2.1 8.9 %collective-permute-start.1 = (bf16[256,128]{1,0:T(8,128)(2,1)S(1)}, bf16[256,128]{1,0:T(8,128)(2,1)S(1)}, u32[]{:S(2)}, u32[]{:S(2)}) collective-permute-start(bf16[256,128]{1,0:T(8,128)(2,1)S(1)} %shard_map.167), channel_id=1, source_target_pairs={{0,1},{1,0},{2,4},{3,5},{4,2},{5,3},{6,8},{7,9},{8,6},{9,7},{10,12... | collective-permute-start | bytes 196616 | tf_op jit(solution)/shard_map/ppermute | solution.py:239
  2.2 8.8 %collective-permute-start = (bf16[256,128]{1,0:T(8,128)(2,1)S(1)}, bf16[256,128]{1,0:T(8,128)(2,1)S(1)}, u32[]{:S(2)}, u32[]{:S(2)}) collective-permute-start(bf16[256,128]{1,0:T(8,128)(2,1)S(1)} %shard_map.167), channel_id=1, source_target_pairs={{0,2},{2,0},{4,6},{6,4},{8,10},{10,8},{12,14},{14,12},{1,3},{3,1},... | collective-permute-start | bytes 196616 | tf_op jit(solution)/shard_map/ppermute | solution.py:238
  6.3 4.8 %copy-start.2 = (bf16[2,128,128]{2,1,0:T(8,128)(2,1)S(1)}, bf16[2,128,128]{2,1,0:T(8,128)(2,1)}, u32[]{:S(2)}) copy-start(bf16[2,128,128]{2,1,0:T(8,128)(2,1)} %node_in.1) | copy-start | bytes 196612
  6.3 4.8 %copy-start.6 = (bf16[128,128]{1,0:T(8,128)(2,1)S(1)}, bf16[128,128]{1,0:T(8,128)(2,1)}, u32[]{:S(2)}) copy-start(bf16[128,128]{1,0:T(8,128)(2,1)} %edge_out.1) | copy-start | bytes 98308
  6.3 4.8 %copy-start.7 = (bf16[128,128]{1,0:T(8,128)(2,1)S(1)}, bf16[128,128]{1,0:T(8,128)(2,1)}, u32[]{:S(2)}) copy-start(bf16[128,128]{1,0:T(8,128)(2,1)} %node_out.1) | copy-start | bytes 98308
  6.3 4.8 %copy-start.13 = (f32[128]{0:T(128)S(1)}, f32[128]{0:T(128)}, u32[]{:S(2)}) copy-start(f32[128]{0:T(128)} %param.25) | copy-start | bytes 1540
  6.3 4.8 %copy-start.14 = (f32[128]{0:T(128)S(1)}, f32[128]{0:T(128)}, u32[]{:S(2)}) copy-start(f32[128]{0:T(128)} %param.27) | copy-start | bytes 1540
  11.1 7.8 %copy-start.3 = (bf16[2,128,128]{2,1,0:T(8,128)(2,1)S(1)}, bf16[2,128,128]{2,1,0:T(8,128)(2,1)}, u32[]{:S(2)}) copy-start(bf16[2,128,128]{2,1,0:T(8,128)(2,1)} %coarse_w.1) | copy-start | bytes 196612
  11.1 7.7 %copy-start.9 = (bf16[64,128]{1,0:T(8,128)(2,1)S(1)}, bf16[64,128]{1,0:T(8,128)(2,1)}, u32[]{:S(2)}) copy-start(bf16[64,128]{1,0:T(8,128)(2,1)} %state.1) | copy-start | bytes 49156
  11.1 7.7 %copy-start.15 = (f32[128]{0:T(128)S(1)}, f32[128]{0:T(128)}, u32[]{:S(2)}) copy-start(f32[128]{0:T(128)} %param.28) | copy-start | bytes 1540
  14.9 4.0 %collective-permute-start.3 = (f32[64,128]{1,0:T(8,128)S(1)}, f32[64,128]{1,0:T(8,128)S(1)}, u32[]{:S(2)}, u32[]{:S(2)}) collective-permute-start(f32[64,128]{1,0:T(8,128)S(1)} %get-tuple-element.21), channel_id=1, source_target_pairs={{0,2},{2,0},{4,6},{6,4},{8,10},{10,8},{12,14},{14,12},{1,3},{3,1},... | collective-permute-start | bytes 98312 | tf_op jit(solution)/shard_map/ppermute | solution.py:238
  15.3 3.5 %collective-permute-start.4 = (f32[64,128]{1,0:T(8,128)S(1)}, f32[64,128]{1,0:T(8,128)S(1)}, u32[]{:S(2)}, u32[]{:S(2)}) collective-permute-start(f32[64,128]{1,0:T(8,128)S(1)} %get-tuple-element.22), channel_id=1, source_target_pairs={{0,1},{1,0},{2,4},{3,5},{4,2},{5,3},{6,8},{7,9},{8,6},{9,7},{10,12... | collective-permute-start | bytes 98312 | tf_op jit(solution)/shard_map/ppermute | solution.py:239
  15.3 3.5 %collective-permute-start.5 = (f32[64,128]{1,0:T(8,128)S(1)}, f32[64,128]{1,0:T(8,128)S(1)}, u32[]{:S(2)}, u32[]{:S(2)}) collective-permute-start(f32[64,128]{1,0:T(8,128)S(1)} %get-tuple-element.23), channel_id=1, source_target_pairs={{0,1},{1,0},{2,3},{3,2},{4,5},{5,4},{6,7},{7,6},{8,9},{9,8},{10,11... | collective-permute-start | bytes 98312 | tf_op jit(solution)/shard_map/ppermute | solution.py:240
  18.9 4.9 %copy-start.4 = (bf16[2,128,128]{2,1,0:T(8,128)(2,1)S(1)}, bf16[2,128,128]{2,1,0:T(8,128)(2,1)}, u32[]{:S(2)}) copy-start(bf16[2,128,128]{2,1,0:T(8,128)(2,1)} %prolong_in.3) | copy-start | bytes 196612
  18.9 6.6 %copy-start.8 = (bf16[128,128]{1,0:T(8,128)(2,1)S(1)}, bf16[128,128]{1,0:T(8,128)(2,1)}, u32[]{:S(2)}) copy-start(bf16[128,128]{1,0:T(8,128)(2,1)} %prolong_out.1) | copy-start | bytes 98308
  19.3 4.6 %collective-permute-start.8 = (bf16[64,128]{1,0:T(8,128)(2,1)S(1)}, bf16[64,128]{1,0:T(8,128)(2,1)S(1)}, u32[]{:S(2)}, u32[]{:S(2)}) collective-permute-start(bf16[64,128]{1,0:T(8,128)(2,1)S(1)} %shard_map.171.own), channel_id=1, source_target_pairs={{0,1},{1,0},{2,3},{3,2},{4,5},{5,4},{6,7},{7,6},{8,9},{9,8},{10,11... | collective-permute-start | bytes 49160 | tf_op jit(solution)/shard_map/ppermute | solution.py:240
  19.4 4.6 %collective-permute-start.7 = (bf16[64,128]{1,0:T(8,128)(2,1)S(1)}, bf16[64,128]{1,0:T(8,128)(2,1)S(1)}, u32[]{:S(2)}, u32[]{:S(2)}) collective-permute-start(bf16[64,128]{1,0:T(8,128)(2,1)S(1)} %shard_map.171.own), channel_id=1, source_target_pairs={{0,1},{1,0},{2,4},{3,5},{4,2},{5,3},{6,8},{7,9},{8,6},{9,7},{10,12... | collective-permute-start | bytes 49160 | tf_op jit(solution)/shard_map/ppermute | solution.py:239
  19.9 5.6 %collective-permute-start.6 = (bf16[64,128]{1,0:T(8,128)(2,1)S(1)}, bf16[64,128]{1,0:T(8,128)(2,1)S(1)}, u32[]{:S(2)}, u32[]{:S(2)}) collective-permute-start(bf16[64,128]{1,0:T(8,128)(2,1)S(1)} %shard_map.171.own), channel_id=1, source_target_pairs={{0,2},{2,0},{4,6},{6,4},{8,10},{10,8},{12,14},{14,12},{1,3},{3,1},... | collective-permute-start | bytes 49160 | tf_op jit(solution)/shard_map/ppermute | solution.py:238

commit v4 on v3

--- a/solution.py
+++ b/solution.py
@@ -10,6 +10,7 @@
 F32 = jnp.float32
 BF16 = jnp.bfloat16
 I32 = jnp.int32
+SENT = F32
 VMEM_LIMIT = 32 * 1024 * 1024
 BLOCK = 128
 GROUP = 2
@@ -22,8 +23,7 @@
     return jnp.dot(a, b, preferred_element_type=F32)
 
 
-def silu(x):
-    half = 0.5 * x
+def silu_of_twice(half):
     return half + half * jnp.tanh(half)
 
 
@@ -70,13 +70,11 @@
     boundary[...] = tiles[: boundary.shape[0], :]
 
 
-def local_kernel(
-    n, co_rows, tiles, around_s, sources, parents, weights, edge_in, edge_bias, cols, near, scale, pool, lift, picked
-):
+def local_kernel(n, co_rows, tiles, sources, parents, weights, cols, near, scale, pool, lift):
     nodes, width = tiles.shape
     degree = near.shape[0]
     rim = nodes // 4
-    j = lax.axis_index("ty")
+    i, j, even = place(n)
     index = sources[...]
     ids = parents[...]
     block_of = quotient(ids, co_rows)
@@ -87,10 +85,12 @@
     piece = quotient(index, rim)
     low = index & (rim - 1)
     nowhere = 2 * rim
+    inner = (i > 0) & (i < n - 1)
+    piece_a, piece_b = jnp.where(even, 5, 4), jnp.where(inner, jnp.where(even, 4, 5), -1)
     rows = [
-        ((index & (2 * rim - 1)) - rim).astype(F32),
-        jnp.where(piece == 7 - j, low, nowhere).astype(F32),
-        jnp.where((piece == 4) | (piece == 5), index - 5 * rim, nowhere).astype(F32),
+        jnp.where(piece < 4, (index & (2 * rim - 1)) - rim, nowhere).astype(F32),
+        jnp.where((piece == piece_a) | (piece == 7 - j), low, nowhere).astype(F32),
+        jnp.where(piece == piece_b, low, nowhere).astype(F32),
         piece.astype(F32),
         slot,
         weights[...].astype(F32),
@@ -102,13 +102,7 @@
     row = lax.broadcasted_iota(I32, pool.shape, 0).astype(F32).astype(BF16)
     pool[...] = jnp.where(row == slot.astype(BF16), jnp.ones((), BF16), jnp.zeros((), BF16))
     lift[...] = one_hot(spread(cols[...], 4 * degree, nodes), 0, 4 * co_rows)
-    project = edge_in[1]
-    empty = jnp.zeros_like(project)
-    project = jnp.concatenate(
-        [jnp.concatenate([project, empty], axis=1), jnp.concatenate([empty, project], axis=1)], axis=0
-    )
     table = jnp.concatenate([tiles[: 2 * rim, :], tiles[2 * rim :, :]], axis=1)
-    side = around_s[...]
 
     def step(at, _):
         first = pl.multiple_of(at * BLOCK, BLOCK)
@@ -118,38 +112,58 @@
             group = range(k, k + GROUP)
             ones = jnp.concatenate([one_hot(spread(col, g, BLOCK), -rim, 2 * rim) for g in group], axis=0)
             got = mm(ones, table).astype(BF16)
-            ones = jnp.concatenate([one_hot(spread(col, degree + g, BLOCK), 0, rim) for g in group], axis=0)
-            beside = mm(ones, side).astype(BF16)
             for g in group:
                 part = slice((g - k) * BLOCK, (g - k + 1) * BLOCK)
                 of = spread(col, 3 * degree + g, BLOCK)
-                value = jnp.where(of < jnp.full((), 2, BF16), got[part, :width], got[part, width:])
-                value = jnp.where(of < jnp.full((), 4, BF16), value, beside[part])
-                picked[g // 2, here, g % 2 * width : (g % 2 + 1) * width] = value
+                near[g, here, :] = jnp.where(of < jnp.full((), 2, BF16), got[part, :width], got[part, width:])
         return 0
 
     lax.fori_loop(0, nodes // BLOCK, step, 0, unroll=UNROLL)
-    dst = mm(tiles[...], edge_in[0]) + edge_bias[...]
+
+
+def side_kernel(tiles, around_a, around_s, cols, near, edge_in, edge_bias, edges, picked):
+    nodes, width = tiles.shape
+    degree = near.shape[0]
+    rim = nodes // 4
+    table = jnp.concatenate([around_a[...], around_s[...]], axis=1)
+
+    def step(at, _):
+        first = pl.multiple_of(at * BLOCK, BLOCK)
+        here = pl.ds(first, BLOCK)
+        col = cols[here, :]
+        for k in range(0, degree, GROUP):
+            group = range(k, k + GROUP)
+            ones = jnp.concatenate([one_hot(spread(col, degree + g, BLOCK), 0, rim) for g in group], axis=0)
+            got = mm(ones, table).astype(BF16)
+            for g in group:
+                part = slice((g - k) * BLOCK, (g - k + 1) * BLOCK)
+                of = spread(col, 3 * degree + g, BLOCK)
+                value = jnp.where(of < jnp.full((), 6, BF16), got[part, :width], got[part, width:])
+                picked[g // 2, here, g % 2 * width : (g % 2 + 1) * width] = value + near[g, here, :]
+        return 0
+
+    lax.fori_loop(0, nodes // BLOCK, step, 0, unroll=UNROLL)
+    project = 0.5 * edge_in[1]
+    empty = jnp.zeros_like(project)
+    project = jnp.concatenate(
+        [jnp.concatenate([project, empty], axis=1), jnp.concatenate([empty, project], axis=1)], axis=0
+    )
+    dst = mm(tiles[...], 0.5 * edge_in[0]) + 0.5 * edge_bias[...]
     for pair in range(degree // 2):
         src = mm(picked[pair], project)
-        near[2 * pair] = dst + src[:, :width]
-        near[2 * pair + 1] = dst + src[:, width:]
+        edges[2 * pair] = dst + src[:, :width]
+        edges[2 * pair + 1] = dst + src[:, width:]
 
 
 def node_kernel(
-    n, tiles, around_a, around_b, cols, near, scale, pool, edge_in, edge_out, node_in, node_bias, node_out, node_gain,
+    tiles, around_b, cols, near, scale, pool, edge_in, edge_out, node_in, node_bias, node_out, node_gain,
     fine_mid, own, to_a, to_b, to_s, total, weighted,
 ):
     nodes, width = tiles.shape
     degree = near.shape[0]
     rim = nodes // 4
     co_rows = own.shape[0]
-    i, j, even = place(n)
-    none = jnp.zeros(around_a.shape, BF16)
-    got_a, got_b = around_a[...], around_b[...]
-    before = jnp.where(i > 0, jnp.where(even, got_b, got_a), none)
-    after = jnp.where(i < n - 1, jnp.where(even, got_a, got_b), none)
-    table = split(mm(jnp.concatenate([before, after], axis=0), edge_in[1]))
+    table = split(mm(around_b[...], 0.5 * edge_in[1]))
 
     def step(at, _):
         first = pl.multiple_of(at * BLOCK, BLOCK)
@@ -157,41 +171,45 @@
         col = cols[here, :]
         sums = jnp.zeros((BLOCK, width), F32)
         for k in range(0, degree, GROUP):
-            ones = [one_hot(spread(col, 2 * degree + k + g, BLOCK), -rim, 2 * rim) for g in range(GROUP)]
+            ones = [one_hot(spread(col, 2 * degree + k + g, BLOCK), 0, rim) for g in range(GROUP)]
             got = mm(jnp.concatenate(ones, axis=0), table)
             for g in range(GROUP):
                 part = got[g * BLOCK : (g + 1) * BLOCK]
                 edge = near[k + g, here, :] + (part[:, :width] + part[:, width:])
-                sums = sums + silu(edge).astype(BF16).astype(F32)
+                sums = sums + silu_of_twice(edge).astype(BF16).astype(F32)
         total[here, :] = sums
         return 0
 
     lax.fori_loop(0, nodes // BLOCK, step, 0, unroll=UNROLL)
-    node_weights = jnp.concatenate([node_in[0], node_in[1]], axis=0)
+    node_weights = 0.5 * jnp.concatenate([node_in[0], node_in[1]], axis=0)
     out_twice = jnp.concatenate([edge_out[...], edge_out[...]], axis=0)
     for first in range(0, nodes, CHUNK):
         here = pl.ds(first, CHUNK)
         aggregate = mm(split(total[here, :]), out_twice).astype(BF16)
         both = jnp.concatenate([tiles[here, :], aggregate], axis=1)
-        hidden = silu(mm(both, node_weights) + node_bias[...]).astype(BF16)
+        hidden = silu_of_twice(mm(both, node_weights) + 0.5 * node_bias[...]).astype(BF16)
         update = normalise(mm(hidden, node_out[...]), node_gain[...])
         mid = (tiles[here, :].astype(F32) + update).astype(BF16)
         fine_mid[here, :] = mid
         weighted[here, :] = (mid.astype(F32) * scale[here, :]).astype(BF16)
     pooled = mm(pool[...], weighted[...])
     for at, ref in enumerate((own, to_a, to_b, to_s)):
-        ref[...] = pooled[at * co_rows : (at + 1) * co_rows]
+        ref[...] = pooled[at * co_rows : (at + 1) * co_rows].astype(ref.dtype)
 
 
 def base_kernel(fine_mid, prolong_in, base):
-    base[...] = mm(fine_mid[...], prolong_in[0])
-
-
-def coarse_kernel(state, own, from_a, from_b, from_s, coarse_gain, coarse_w, out):
-    total = state[...].astype(F32) + own[...] + from_a[...] + from_b[...] + from_s[...]
+    base[...] = mm(fine_mid[...], 0.5 * prolong_in[0])
+
+
+def coarse_kernel(state, own, from_b, from_a, from_s, coarse_gain, coarse_w, *outs):
+    total = state[...].astype(F32) + own[...]
+    for ref in (from_a, from_b, from_s):
+        total = total + ref[...].astype(F32)
     normed = normalise(total, coarse_gain[...]).astype(BF16)
-    hidden = silu(mm(normed, coarse_w[0])).astype(BF16)
-    out[...] = (total + mm(hidden, coarse_w[1])).astype(BF16)
+    hidden = silu_of_twice(mm(normed, 0.5 * coarse_w[0])).astype(BF16)
+    total = (total + mm(hidden, coarse_w[1])).astype(BF16)
+    for out in outs:
+        out[...] = total
 
 
 def prolong_kernel(
@@ -201,9 +219,9 @@
     copies = [pltpu.make_async_copy(own, coarse_out, sems.at[PARTS])]
     copies[0].start()
     coarse = jnp.concatenate([own[...], from_a[...], from_b[...], from_s[...]], axis=0)
-    terms = split(mm(coarse, prolong_in[1]))
+    terms = split(mm(coarse, 0.5 * prolong_in[1]))
     lifted = mm(lift[...], terms)
-    hidden = silu(base[...] + (lifted[:, :width] + lifted[:, width:])).astype(BF16)
+    hidden = silu_of_twice(base[...] + (lifted[:, :width] + lifted[:, width:])).astype(BF16)
     block = nodes // PARTS
     for at in range(PARTS):
         part = slice(at * block, (at + 1) * block)
@@ -272,36 +290,41 @@
         functools.partial(local_kernel, n, co_rows),
         [
             shape((nodes, 40), F32),
-            shape((degree, nodes, width), F32),
+            shape((degree, nodes, width), BF16),
             shape((nodes, width), F32),
             shape((4 * co_rows, nodes), BF16),
             shape((nodes, 4 * co_rows), BF16),
         ],
-        latents, around_s, jnp.swapaxes(sources[0, 0], 0, 1), parents[0], restrict_w[0], edge_in, edge_bias[None],
-        flops=2**34,
+        latents, jnp.swapaxes(sources[0, 0], 0, 1), parents[0], restrict_w[0],
+        flops=2**33,
+    )
+    (edges,) = call(
+        side_kernel,
+        [shape((degree, nodes, width), F32)],
+        latents, around_a, around_s, cols, near, edge_in, edge_bias[None],
+        flops=2**33,
         scratch=[pltpu.VMEM((degree // 2, nodes, 2 * width), BF16)],
     )
     fine_mid, own, to_a, to_b, to_s = call(
-        functools.partial(node_kernel, n),
-        [shape((nodes, width), BF16)] + [shape((co_rows, width), F32)] * 4,
-        latents, around_a, around_b, cols, near, scale, pool,
-        edge_in, edge_out, node_in, node_bias[None], node_out, node_gain[None],
-        flops=2**34,
+        node_kernel,
+        [shape((nodes, width), BF16), shape((co_rows, width), F32)] + [shape((co_rows, width), SENT)] * 3,
+        latents, around_b, cols, edges, scale, pool, edge_in, edge_out, node_in, node_bias[None], node_out, node_gain[None],
+        flops=2**33,
         scratch=[pltpu.VMEM((nodes, width), F32), pltpu.VMEM((nodes, width), BF16)],
     )
     got = exchange(n, to_a, to_b, to_s)
-    (coarse_out,) = call(
+    coarse_out, *sent = call(
         coarse_kernel,
-        [shape((co_rows, width), BF16)],
-        coarse_state, own, *got, coarse_gain[None], coarse_w,
+        [shape((co_rows, width), BF16)] * 4,
+        coarse_state, own, got[1], got[0], got[2], coarse_gain[None], coarse_w,
         flops=2**32,
     )
-    beside = exchange(n, coarse_out, coarse_out, coarse_out)
+    beside = exchange(n, *sent)
     (base,) = call(base_kernel, [shape((nodes, width), F32)], fine_mid, prolong_in, flops=2**29)
     fine_out, coarse_out = call(
         prolong_kernel,
         [shape((nodes, width), BF16), shape((co_rows, width), BF16)],
-        fine_mid, base, lift, coarse_out, *beside, prolong_in, prolong_out,
+        fine_mid, base, lift, coarse_out, beside[0], beside[1], beside[2], prolong_in, prolong_out,
         to=pl.ANY,
         scratch=[pltpu.VMEM((nodes, width), BF16), pltpu.SemaphoreType.DMA((PARTS + 1,))],
         flops=2**32,

time: 27 us -> 26.3 us (0.974)
  the two profiles are of different devices: /device:TPU:0 before, /device:TPU:18 now
where the time goes in v4:
time: 26.3 us; the launch traced here: 26.1 us
  Pallas kernels  10.1 us (38%)
  starting transfers between devices  7.12 us (27%)
  waiting for transfers between devices  6.96 us (26%)
  local copies, waits for them, and re-layouts  1.03 us (4%)
  between operations  0.88 us (3%)
    pallas_call x7, Pallas kernels, call(): pl.pallas_call(kernel, out_shape=outs, in_specs=[pl.BlockSpec(memory_spac...  10.1 us
    ppermute x3, starting transfers between devices, exchange(): lax.ppermute(to_b, ('tx', 'ty'), pairs_b)  3.87 us
    ppermute x3, waiting for transfers between devices, exchange(): lax.ppermute(to_b, ('tx', 'ty'), pairs_b)  3.72 us
    ppermute x3, waiting for transfers between devices, exchange(): lax.ppermute(to_a, 'tx', pairs_a)  3.24 us
    ppermute x3, starting transfers between devices, exchange(): lax.ppermute(to_a, 'tx', pairs_a)  3.17 us
    unnamed x32, local copies, waits for them, and re-layouts  1.03 us
  transfers between devices with their start and end apart: 9, of which 4 were waited for; matrix products, arithmetic and copies ran while one was open for 0% of the time, Pallas kernels for 21%

profile of v4, /device:TPU:18, one launch (start us, length us, event | category | flops | bytes accessed | tf_op | source)
XLA Modules:
  0.0 26.1 jit_solution(8711176604406143664)
XLA Ops:
  0.6 0.9 %copy-done = bf16[1,1,1024,128]{3,2,1,0:T(8,128)(2,1)S(1)} copy-done((bf16[1,1,1024,128]{3,2,1,0:T(8,128)(2,1)S(1)}, bf16[1,1,1024,128]{3,2,1,0:T(8,128)(2,1)}, u32[]{:S(2)}) %copy-start) | copy-done | bytes 262168
  1.6 0.1 collective-permute-start.2
  1.7 1.6 %collective-permute-start.1 = (bf16[256,128]{1,0:T(8,128)(2,1)S(1)}, bf16[256,128]{1,0:T(8,128)(2,1)S(1)}, u32[]{:S(2)}, u32[]{:S(2)}) collective-permute-start(bf16[256,128]{1,0:T(8,128)(2,1)S(1)} %shard_map.167), channel_id=1, source_target_pairs={{0,2},{2,0},{4,6},{6,4},{8,10},{10,8},{12,14},{14,12},{1,3},{3,1},... | collective-permute-start | bytes 196616 | tf_op jit(solution)/shard_map/ppermute | solution.py:256
  3.3 0.4 %collective-permute-start = (bf16[256,128]{1,0:T(8,128)(2,1)S(1)}, bf16[256,128]{1,0:T(8,128)(2,1)S(1)}, u32[]{:S(2)}, u32[]{:S(2)}) collective-permute-start(bf16[256,128]{1,0:T(8,128)(2,1)S(1)} %shard_map.167), channel_id=1, source_target_pairs={{0,1},{1,0},{2,4},{3,5},{4,2},{5,3},{6,8},{7,9},{8,6},{9,7},{10,12... | collective-permute-start | bytes 196616 | tf_op jit(solution)/shard_map/ppermute | solution.py:257
  3.7 0.0 copy-start.12
  3.7 2.9 %shard_map.168 = (f32[1024,40]{1,0:T(8,128)S(1)}, bf16[8,1024,128]{2,1,0:T(8,128)(2,1)S(1)}, f32[1024,128]{1,0:T(8,128)S(1)}, bf16[256,1024]{1,0:T(8,128)(2,1)S(1)}, bf16[1024,256]{1,0:T(8,128)(2,1)S(1)}) custom-call(bf16[1024,128]{1,0:T(8,128)(2,1)S(1)} %bitcast.12, s32[8,1024]{1,0:T(8,128)S(1)} %bitcast.15, s32[1,1024]{1,0:T(1,128)S(1)} %bitcast.16, ...), custom_call_target="tpu_custom_call" | custom-call | flops 8589934592 | bytes 8589934 | tf_op jit(solution)/shard_map/pallas_call | solution.py:237
  6.6 0.0 collective-permute-done.1.around_a
  6.7 0.0 copy-start.2
  6.7 0.0 copy-start.6
  6.7 0.0 copy-start.7
  6.7 0.0 copy-start.13
  6.7 0.0 copy-start.14
  6.7 2.4 %shard_map.169.near = f32[8,1024,128]{2,1,0:T(8,128)S(1)} custom-call(bf16[1024,128]{1,0:T(8,128)(2,1)S(1)} %bitcast.13, bf16[256,128]{1,0:T(8,128)(2,1)S(1)} %collective-permute-done.1.around_a, bf16[256,128]{1,0:T(8,128)(2,1)S(1)} %collective-permute-done.2.around_s, f32[1024,40]{1,0:T(8,128)S(1)} %get-tuple-element.18.cols, ...), custom_call_target="tpu_custom_call" | custom-call | flops 8589934592 | bytes 8589934 | tf_op jit(solution)/shard_map/pallas_call | solution.py:237
  9.2 0.0 copy-start.3
  9.2 0.0 copy-start.9
  9.2 0.0 copy-start.15
  9.2 2.8 %shard_map.170 = (bf16[1024,128]{1,0:T(8,128)(2,1)S(1)}, f32[64,128]{1,0:T(8,128)S(1)}, f32[64,128]{1,0:T(8,128)S(1)}, f32[64,128]{1,0:T(8,128)S(1)}, f32[64,128]{1,0:T(8,128)S(1)}) custom-call(bf16[1024,128]{1,0:T(8,128)(2,1)S(1)} %bitcast.14, bf16[256,128]{1,0:T(8,128)(2,1)S(1)} %collective-permute-done.around_b, f32[1024,40]{1,0:T(8,128)S(1)} %get-tuple-element.18.cols, ...), custom_call_target="tpu_custom_call" | custom-call | flops 8589934592 | bytes 8589934 | tf_op jit(solution)/shard_map/pallas_call | solution.py:237
  12.1 2.6 %collective-permute-start.3 = (f32[64,128]{1,0:T(8,128)S(1)}, f32[64,128]{1,0:T(8,128)S(1)}, u32[]{:S(2)}, u32[]{:S(2)}) collective-permute-start(f32[64,128]{1,0:T(8,128)S(1)} %get-tuple-element.25), channel_id=1, source_target_pairs={{0,1},{1,0},{2,4},{3,5},{4,2},{5,3},{6,8},{7,9},{8,6},{9,7},{10,12... | collective-permute-start | bytes 98312 | tf_op jit(solution)/shard_map/ppermute | solution.py:257
  14.7 0.5 %collective-permute-start.4 = (f32[64,128]{1,0:T(8,128)S(1)}, f32[64,128]{1,0:T(8,128)S(1)}, u32[]{:S(2)}, u32[]{:S(2)}) collective-permute-start(f32[64,128]{1,0:T(8,128)S(1)} %get-tuple-element.26), channel_id=1, source_target_pairs={{0,2},{2,0},{4,6},{6,4},{8,10},{10,8},{12,14},{14,12},{1,3},{3,1},... | collective-permute-start | bytes 98312 | tf_op jit(solution)/shard_map/ppermute | solution.py:256
  15.1 0.0 collective-permute-start.5
  15.1 1.8 %collective-permute-done.3.from_b = f32[64,128]{1,0:T(8,128)S(1)} collective-permute-done((f32[64,128]{1,0:T(8,128)S(1)}, f32[64,128]{1,0:T(8,128)S(1)}, u32[]{:S(2)}, u32[]{:S(2)}) %collective-permute-start.3) | collective-permute-done | bytes 32800 | tf_op jit(solution)/shard_map/ppermute | solution.py:257
  16.9 1.6 %collective-permute-done.4.from_a = f32[64,128]{1,0:T(8,128)S(1)} collective-permute-done((f32[64,128]{1,0:T(8,128)S(1)}, f32[64,128]{1,0:T(8,128)S(1)}, u32[]{:S(2)}, u32[]{:S(2)}) %collective-permute-start.4) | collective-permute-done | bytes 32800 | tf_op jit(solution)/shard_map/ppermute | solution.py:256
  18.6 0.0 copy-start.4
  18.6 0.0 copy-start.8
  18.6 0.4 %shard_map.172 = (bf16[64,128]{1,0:T(8,128)(2,1)S(1)}, bf16[64,128]{1,0:T(8,128)(2,1)S(1)}, bf16[64,128]{1,0:T(8,128)(2,1)S(1)}, bf16[64,128]{1,0:T(8,128)(2,1)S(1)}) custom-call(bf16[64,128]{1,0:T(8,128)(2,1)S(1)} %copy-done.9, f32[64,128]{1,0:T(8,128)S(1)} %get-tuple-element.24.own, f32[64,128]{1,0:T(8,128)S(1)} %collective-permute-done.3.from_b, ...), custom_call_target="tpu_custom_call" | custom-call | flops 4294967296 | bytes 4294967 | tf_op jit(solution)/shard_map/pallas_call | solution.py:237
  19.0 1.1 %collective-permute-start.6 = (bf16[64,128]{1,0:T(8,128)(2,1)S(1)}, bf16[64,128]{1,0:T(8,128)(2,1)S(1)}, u32[]{:S(2)}, u32[]{:S(2)}) collective-permute-start(bf16[64,128]{1,0:T(8,128)(2,1)S(1)} %get-tuple-element.29), channel_id=1, source_target_pairs={{0,2},{2,0},{4,6},{6,4},{8,10},{10,8},{12,14},{14,12},{1,3},{3,1},... | collective-permute-start | bytes 49160 | tf_op jit(solution)/shard_map/ppermute | solution.py:256
  20.1 0.9 %collective-permute-start.7 = (bf16[64,128]{1,0:T(8,128)(2,1)S(1)}, bf16[64,128]{1,0:T(8,128)(2,1)S(1)}, u32[]{:S(2)}, u32[]{:S(2)}) collective-permute-start(bf16[64,128]{1,0:T(8,128)(2,1)S(1)} %get-tuple-element.30), channel_id=1, source_target_pairs={{0,1},{1,0},{2,4},{3,5},{4,2},{5,3},{6,8},{7,9},{8,6},{9,7},{10,12... | collective-permute-start | bytes 49160 | tf_op jit(solution)/shard_map/ppermute | solution.py:257
  21.0 0.0 collective-permute-start.8
  21.0 0.2 shard_map.171.base
  21.2 1.6 %collective-permute-done.6.from_a = bf16[64,128]{1,0:T(8,128)(2,1)S(1)} collective-permute-done((bf16[64,128]{1,0:T(8,128)(2,1)S(1)}, bf16[64,128]{1,0:T(8,128)(2,1)S(1)}, u32[]{:S(2)}, u32[]{:S(2)}) %collective-permute-start.6) | collective-permute-done | bytes 16416 | tf_op jit(solution)/shard_map/ppermute | solution.py:256
  22.8 1.9 %collective-permute-done.7.from_b = bf16[64,128]{1,0:T(8,128)(2,1)S(1)} collective-permute-done((bf16[64,128]{1,0:T(8,128)(2,1)S(1)}, bf16[64,128]{1,0:T(8,128)(2,1)S(1)}, u32[]{:S(2)}, u32[]{:S(2)}) %collective-permute-start.7) | collective-permute-done | bytes 16416 | tf_op jit(solution)/shard_map/ppermute | solution.py:257
  24.8 1.3 %shard_map.173 = (bf16[1024,128]{1,0:T(8,128)(2,1)}, bf16[64,128]{1,0:T(8,128)(2,1)}) custom-call(bf16[1024,128]{1,0:T(8,128)(2,1)S(1)} %get-tuple-element.22.fine_mid, f32[1024,128]{1,0:T(8,128)S(1)} %shard_map.171.base, bf16[1024,256]{1,0:T(8,128)(2,1)S(1)} %get-tuple-element.23.lift, bf16[64,128]{1,0:T(8,128)(2,1)S(1)} %get-tuple-element.28.own, ...), custom_call_target="tpu_custom_call" | custom-call | flops 4294967296 | bytes 4294967 | tf_op jit(solution)/shard_map/pallas_call | solution.py:237
  (25 shorter events, 0.1 us)
Async XLA Ops:
  0.6 1.0 %copy-start = (bf16[1,1,1024,128]{3,2,1,0:T(8,128)(2,1)S(1)}, bf16[1,1,1024,128]{3,2,1,0:T(8,128)(2,1)}, u32[]{:S(2)}) copy-start(bf16[1,1,1024,128]{3,2,1,0:T(8,128)(2,1)} %param.16) | copy-start | bytes 786436
  1.6 2.1 %copy-start.5 = (s32[1,1,1024,8]{2,3,1,0:T(8,128)S(1)}, s32[1,1,1024,8]{2,3,1,0:T(8,128)}, u32[]{:S(2)}) copy-start(s32[1,1,1024,8]{2,3,1,0:T(8,128)} %param.17) | copy-start | bytes 98308
  1.6 2.1 %copy-start.10 = (s32[1,1,1024]{2,1,0:T(1,128)S(1)}, s32[1,1,1024]{2,1,0:T(1,128)}, u32[]{:S(2)}) copy-start(s32[1,1,1024]{2,1,0:T(1,128)} %param.18) | copy-start | bytes 12292
  1.6 2.1 %copy-start.11 = (bf16[1,1,1024]{2,1,0:T(2,128)(2,1)S(1)}, bf16[1,1,1024]{2,1,0:T(2,128)(2,1)}, u32[]{:S(2)}) copy-start(bf16[1,1,1024]{2,1,0:T(2,128)(2,1)} %param.19) | copy-start | bytes 6148
  1.6 5.0 %collective-permute-start.2 = (bf16[256,128]{1,0:T(8,128)(2,1)S(1)}, bf16[256,128]{1,0:T(8,128)(2,1)S(1)}, u32[]{:S(2)}, u32[]{:S(2)}) collective-permute-start(bf16[256,128]{1,0:T(8,128)(2,1)S(1)} %shard_map.167), channel_id=1, source_target_pairs={{0,1},{1,0},{2,3},{3,2},{4,5},{5,4},{6,7},{7,6},{8,9},{9,8},{10,11... | collective-permute-start | bytes 196616 | tf_op jit(solution)/shard_map/ppermute | solution.py:258
  1.7 5.0 %collective-permute-start.1 = (bf16[256,128]{1,0:T(8,128)(2,1)S(1)}, bf16[256,128]{1,0:T(8,128)(2,1)S(1)}, u32[]{:S(2)}, u32[]{:S(2)}) collective-permute-start(bf16[256,128]{1,0:T(8,128)(2,1)S(1)} %shard_map.167), channel_id=1, source_target_pairs={{0,2},{2,0},{4,6},{6,4},{8,10},{10,8},{12,14},{14,12},{1,3},{3,1},... | collective-permute-start | bytes 196616 | tf_op jit(solution)/shard_map/ppermute | solution.py:256
  3.3 5.9 %collective-permute-start = (bf16[256,128]{1,0:T(8,128)(2,1)S(1)}, bf16[256,128]{1,0:T(8,128)(2,1)S(1)}, u32[]{:S(2)}, u32[]{:S(2)}) collective-permute-start(bf16[256,128]{1,0:T(8,128)(2,1)S(1)} %shard_map.167), channel_id=1, source_target_pairs={{0,1},{1,0},{2,4},{3,5},{4,2},{5,3},{6,8},{7,9},{8,6},{9,7},{10,12... | collective-permute-start | bytes 196616 | tf_op jit(solution)/shard_map/ppermute | solution.py:257
  3.7 3.0 %copy-start.1 = (bf16[2,128,128]{2,1,0:T(8,128)(2,1)S(1)}, bf16[2,128,128]{2,1,0:T(8,128)(2,1)}, u32[]{:S(2)}) copy-start(bf16[2,128,128]{2,1,0:T(8,128)(2,1)} %edge_in.3) | copy-start | bytes 196612
  3.7 3.0 %copy-start.12 = (f32[128]{0:T(128)S(1)}, f32[128]{0:T(128)}, u32[]{:S(2)}) copy-start(f32[128]{0:T(128)} %param.22) | copy-start | bytes 1540
  6.7 2.5 %copy-start.2 = (bf16[2,128,128]{2,1,0:T(8,128)(2,1)S(1)}, bf16[2,128,128]{2,1,0:T(8,128)(2,1)}, u32[]{:S(2)}) copy-start(bf16[2,128,128]{2,1,0:T(8,128)(2,1)} %node_in.1) | copy-start | bytes 196612
  6.7 2.5 %copy-start.6 = (bf16[128,128]{1,0:T(8,128)(2,1)S(1)}, bf16[128,128]{1,0:T(8,128)(2,1)}, u32[]{:S(2)}) copy-start(bf16[128,128]{1,0:T(8,128)(2,1)} %edge_out.1) | copy-start | bytes 98308
  6.7 2.5 %copy-start.7 = (bf16[128,128]{1,0:T(8,128)(2,1)S(1)}, bf16[128,128]{1,0:T(8,128)(2,1)}, u32[]{:S(2)}) copy-start(bf16[128,128]{1,0:T(8,128)(2,1)} %node_out.1) | copy-start | bytes 98308
  6.7 2.5 %copy-start.13 = (f32[128]{0:T(128)S(1)}, f32[128]{0:T(128)}, u32[]{:S(2)}) copy-start(f32[128]{0:T(128)} %param.25) | copy-start | bytes 1540
  6.7 2.5 %copy-start.14 = (f32[128]{0:T(128)S(1)}, f32[128]{0:T(128)}, u32[]{:S(2)}) copy-start(f32[128]{0:T(128)} %param.27) | copy-start | bytes 1540
  9.2 9.4 %copy-start.3 = (bf16[2,128,128]{2,1,0:T(8,128)(2,1)S(1)}, bf16[2,128,128]{2,1,0:T(8,128)(2,1)}, u32[]{:S(2)}) copy-start(bf16[2,128,128]{2,1,0:T(8,128)(2,1)} %coarse_w.1) | copy-start | bytes 196612
  9.2 9.4 %copy-start.9 = (bf16[64,128]{1,0:T(8,128)(2,1)S(1)}, bf16[64,128]{1,0:T(8,128)(2,1)}, u32[]{:S(2)}) copy-start(bf16[64,128]{1,0:T(8,128)(2,1)} %state.1) | copy-start | bytes 49156
  9.2 9.4 %copy-start.15 = (f32[128]{0:T(128)S(1)}, f32[128]{0:T(128)}, u32[]{:S(2)}) copy-start(f32[128]{0:T(128)} %param.28) | copy-start | bytes 1540
  12.1 4.9 %collective-permute-start.3 = (f32[64,128]{1,0:T(8,128)S(1)}, f32[64,128]{1,0:T(8,128)S(1)}, u32[]{:S(2)}, u32[]{:S(2)}) collective-permute-start(f32[64,128]{1,0:T(8,128)S(1)} %get-tuple-element.25), channel_id=1, source_target_pairs={{0,1},{1,0},{2,4},{3,5},{4,2},{5,3},{6,8},{7,9},{8,6},{9,7},{10,12... | collective-permute-start | bytes 98312 | tf_op jit(solution)/shard_map/ppermute | solution.py:257
  14.7 3.9 %collective-permute-start.4 = (f32[64,128]{1,0:T(8,128)S(1)}, f32[64,128]{1,0:T(8,128)S(1)}, u32[]{:S(2)}, u32[]{:S(2)}) collective-permute-start(f32[64,128]{1,0:T(8,128)S(1)} %get-tuple-element.26), channel_id=1, source_target_pairs={{0,2},{2,0},{4,6},{6,4},{8,10},{10,8},{12,14},{14,12},{1,3},{3,1},... | collective-permute-start | bytes 98312 | tf_op jit(solution)/shard_map/ppermute | solution.py:256
  15.1 3.4 %collective-permute-start.5 = (f32[64,128]{1,0:T(8,128)S(1)}, f32[64,128]{1,0:T(8,128)S(1)}, u32[]{:S(2)}, u32[]{:S(2)}) collective-permute-start(f32[64,128]{1,0:T(8,128)S(1)} %get-tuple-element.27), channel_id=1, source_target_pairs={{0,1},{1,0},{2,3},{3,2},{4,5},{5,4},{6,7},{7,6},{8,9},{9,8},{10,11... | collective-permute-start | bytes 98312 | tf_op jit(solution)/shard_map/ppermute | solution.py:258
  18.6 2.4 %copy-start.4 = (bf16[2,128,128]{2,1,0:T(8,128)(2,1)S(1)}, bf16[2,128,128]{2,1,0:T(8,128)(2,1)}, u32[]{:S(2)}) copy-start(bf16[2,128,128]{2,1,0:T(8,128)(2,1)} %prolong_in.3) | copy-start | bytes 196612
  18.6 6.2 %copy-start.8 = (bf16[128,128]{1,0:T(8,128)(2,1)S(1)}, bf16[128,128]{1,0:T(8,128)(2,1)}, u32[]{:S(2)}) copy-start(bf16[128,128]{1,0:T(8,128)(2,1)} %prolong_out.1) | copy-start | bytes 98308
  19.0 3.8 %collective-permute-start.6 = (bf16[64,128]{1,0:T(8,128)(2,1)S(1)}, bf16[64,128]{1,0:T(8,128)(2,1)S(1)}, u32[]{:S(2)}, u32[]{:S(2)}) collective-permute-start(bf16[64,128]{1,0:T(8,128)(2,1)S(1)} %get-tuple-element.29), channel_id=1, source_target_pairs={{0,2},{2,0},{4,6},{6,4},{8,10},{10,8},{12,14},{14,12},{1,3},{3,1},... | collective-permute-start | bytes 49160 | tf_op jit(solution)/shard_map/ppermute | solution.py:256
  20.1 4.6 %collective-permute-start.7 = (bf16[64,128]{1,0:T(8,128)(2,1)S(1)}, bf16[64,128]{1,0:T(8,128)(2,1)S(1)}, u32[]{:S(2)}, u32[]{:S(2)}) collective-permute-start(bf16[64,128]{1,0:T(8,128)(2,1)S(1)} %get-tuple-element.30), channel_id=1, source_target_pairs={{0,1},{1,0},{2,4},{3,5},{4,2},{5,3},{6,8},{7,9},{8,6},{9,7},{10,12... | collective-permute-start | bytes 49160 | tf_op jit(solution)/shard_map/ppermute | solution.py:257
  21.0 3.8 %collective-permute-start.8 = (bf16[64,128]{1,0:T(8,128)(2,1)S(1)}, bf16[64,128]{1,0:T(8,128)(2,1)S(1)}, u32[]{:S(2)}, u32[]{:S(2)}) collective-permute-start(bf16[64,128]{1,0:T(8,128)(2,1)S(1)} %get-tuple-element.31), channel_id=1, source_target_pairs={{0,1},{1,0},{2,3},{3,2},{4,5},{5,4},{6,7},{7,6},{8,9},{9,8},{10,11... | collective-permute-start | bytes 49160 | tf_op jit(solution)/shard_map/ppermute | solution.py:258

commit v5 on v4

--- a/solution.py
+++ b/solution.py
@@ -10,7 +10,6 @@
 F32 = jnp.float32
 BF16 = jnp.bfloat16
 I32 = jnp.int32
-SENT = F32
 VMEM_LIMIT = 32 * 1024 * 1024
 BLOCK = 128
 GROUP = 2
@@ -33,10 +32,17 @@
     return center * lax.rsqrt(spread + 1e-05) * gain
 
 
+def two_terms(values):
+    high = values.astype(BF16)
+    return high, (values - high.astype(F32)).astype(BF16)
+
+
 def split(values):
-    high = values.astype(BF16)
-    low = (values - high.astype(F32)).astype(BF16)
-    return jnp.concatenate([high, low], axis=1)
+    return jnp.concatenate(two_terms(values), axis=1)
+
+
+def rows_of(ref, at, count):
+    return ref[at * count : (at + 1) * count, :]
 
 
 def quotient(x, d):
@@ -156,8 +162,8 @@
 
 
 def node_kernel(
-    tiles, around_b, cols, near, scale, pool, edge_in, edge_out, node_in, node_bias, node_out, node_gain,
-    fine_mid, own, to_a, to_b, to_s, total, weighted,
+    tiles, around_b, cols, near, scale, pool, edge_in, edge_out, node_in, node_bias, node_out, node_gain, state,
+    fine_mid, own, sums_out, total, weighted,
 ):
     nodes, width = tiles.shape
     degree = near.shape[0]
@@ -193,32 +199,63 @@
         fine_mid[here, :] = mid
         weighted[here, :] = (mid.astype(F32) * scale[here, :]).astype(BF16)
     pooled = mm(pool[...], weighted[...])
-    for at, ref in enumerate((own, to_a, to_b, to_s)):
-        ref[...] = pooled[at * co_rows : (at + 1) * co_rows].astype(ref.dtype)
+    mine = pooled[:co_rows] + state[...].astype(F32)
+    own[...] = mine
+    high, low = two_terms(mine)
+    to_a, to_b, to_s = (pooled[at * co_rows : (at + 1) * co_rows].astype(BF16) for at in (1, 2, 3))
+    sums_out[...] = jnp.concatenate([high, low, to_s, to_a, to_b], axis=0)
 
 
 def base_kernel(fine_mid, prolong_in, base):
     base[...] = mm(fine_mid[...], 0.5 * prolong_in[0])
 
 
-def coarse_kernel(state, own, from_b, from_a, from_s, coarse_gain, coarse_w, *outs):
-    total = state[...].astype(F32) + own[...]
-    for ref in (from_a, from_b, from_s):
-        total = total + ref[...].astype(F32)
+def first_is_a(n):
+    i, _, even = place(n)
+    return even == (lax.rem(i, 4) < 2)
+
+
+def share_kernel(n, own, sums, mate, near, mate_near, to_a, to_b, to_first, to_second):
+    count = own.shape[0]
+    _, _, mine_s, mine_a, mine_b = (rows_of(sums, at, count) for at in range(5))
+    high, low, mate_s, mate_a, mate_b = (rows_of(mate, at, count) for at in range(5))
+    total = own[...] + mate_s.astype(F32)
+    near[...] = total
+    mate_near[...] = high.astype(F32) + low.astype(F32) + mine_s.astype(F32)
+    to_a[...] = jnp.concatenate([*two_terms(total), mine_a, mate_a], axis=0)
+    to_b[...] = jnp.concatenate([*two_terms(total), mine_b, mate_b], axis=0)
+    first = first_is_a(n)
+    to_first[...] = jnp.where(first, mine_a, mine_b)
+    to_second[...] = jnp.where(first, mine_b, mine_a)
+
+
+def prolong_kernel(
+    n, fine_mid, base, lift, near, mate_near, sums, from_b, from_a, from_first, from_second, coarse_gain, coarse_w,
+    prolong_in, prolong_out, out, coarse_out, ready, coarse_ready, sems,
+):
+    nodes, width = fine_mid.shape
+    count = near.shape[0]
+    i, _, _ = place(n)
+    far_first = from_first[...].astype(F32)
+    far_second = jnp.where((i > 1) & (i < n - 2), from_second[...].astype(F32), 0.0)
+    first = first_is_a(n)
+    high_a, low_a, to_me_a, to_mate_a = (rows_of(from_a, at, count).astype(F32) for at in range(4))
+    high_b, low_b, to_me_b, to_mate_b = (rows_of(from_b, at, count).astype(F32) for at in range(4))
+    total = jnp.concatenate(
+        [
+            near[...] + to_me_a + to_me_b,
+            high_a + low_a + rows_of(sums, 3, count).astype(F32) + jnp.where(first, far_first, far_second),
+            high_b + low_b + rows_of(sums, 4, count).astype(F32) + jnp.where(first, far_second, far_first),
+            mate_near[...] + to_mate_a + to_mate_b,
+        ],
+        axis=0,
+    )
     normed = normalise(total, coarse_gain[...]).astype(BF16)
     hidden = silu_of_twice(mm(normed, 0.5 * coarse_w[0])).astype(BF16)
-    total = (total + mm(hidden, coarse_w[1])).astype(BF16)
-    for out in outs:
-        out[...] = total
-
-
-def prolong_kernel(
-    fine_mid, base, lift, own, from_a, from_b, from_s, prolong_in, prolong_out, out, coarse_out, ready, sems
-):
-    nodes, width = fine_mid.shape
-    copies = [pltpu.make_async_copy(own, coarse_out, sems.at[PARTS])]
+    coarse = (total + mm(hidden, coarse_w[1])).astype(BF16)
+    coarse_ready[...] = coarse[:count]
+    copies = [pltpu.make_async_copy(coarse_ready, coarse_out, sems.at[PARTS])]
     copies[0].start()
-    coarse = jnp.concatenate([own[...], from_a[...], from_b[...], from_s[...]], axis=0)
     terms = split(mm(coarse, 0.5 * prolong_in[1]))
     lifted = mm(lift[...], terms)
     hidden = silu_of_twice(base[...] + (lifted[:, :width] + lifted[:, width:])).astype(BF16)
@@ -245,18 +282,20 @@
     )(*args)
 
 
-def exchange(n, to_a, to_b, to_s):
-    pairs_a = [(i, i ^ 1) for i in range(n)]
-    pairs_b = []
-    for i in range(n):
-        for j in range(2):
-            other = (((i - 1) ^ 1) + 1, j) if 0 < i < n - 1 else (i, 1 - j)
-            pairs_b.append((i * 2 + j, other[0] * 2 + other[1]))
-    return (
-        lax.ppermute(to_a, "tx", pairs_a),
-        lax.ppermute(to_b, ("tx", "ty"), pairs_b),
-        lax.ppermute(to_s, "ty", [(0, 1), (1, 0)]),
-    )
+def pairs(n):
+    def both(partner):
+        steps = []
+        for i in range(n):
+            for j in range(2):
+                k = partner(i)
+                steps.append((i * 2 + j, k * 2 + j if 0 <= k < n else i * 2 + 1 - j))
+        return steps
+
+    return both(lambda i: i ^ 1), both(lambda i: ((i - 1) ^ 1) + 1), both(lambda i: i ^ 2), both(lambda i: ((i - 2) ^ 2) + 2)
+
+
+def swap(value):
+    return lax.ppermute(value, "ty", [(0, 1), (1, 0)])
 
 
 def body(
@@ -285,7 +324,11 @@
 
     latents = tiles[0, 0]
     (boundary,) = call(boundary_kernel, [shape((nodes // 4, width), BF16)], latents, flops=2**33)
-    around_a, around_b, around_s = exchange(n, boundary, boundary, boundary)
+    pairs_a, pairs_b, pairs_first, pairs_second = pairs(n)
+    all_tiles = ("tx", "ty")
+    around_a = lax.ppermute(boundary, all_tiles, pairs_a)
+    around_b = lax.ppermute(boundary, all_tiles, pairs_b)
+    around_s = swap(boundary)
     cols, near, scale, pool, lift = call(
         functools.partial(local_kernel, n, co_rows),
         [
@@ -305,28 +348,36 @@
         flops=2**33,
         scratch=[pltpu.VMEM((degree // 2, nodes, 2 * width), BF16)],
     )
-    fine_mid, own, to_a, to_b, to_s = call(
+    fine_mid, own, sums = call(
         node_kernel,
-        [shape((nodes, width), BF16), shape((co_rows, width), F32)] + [shape((co_rows, width), SENT)] * 3,
+        [shape((nodes, width), BF16), shape((co_rows, width), F32), shape((5 * co_rows, width), BF16)],
         latents, around_b, cols, edges, scale, pool, edge_in, edge_out, node_in, node_bias[None], node_out, node_gain[None],
+        coarse_state,
         flops=2**33,
         scratch=[pltpu.VMEM((nodes, width), F32), pltpu.VMEM((nodes, width), BF16)],
     )
-    got = exchange(n, to_a, to_b, to_s)
-    coarse_out, *sent = call(
-        coarse_kernel,
-        [shape((co_rows, width), BF16)] * 4,
-        coarse_state, own, got[1], got[0], got[2], coarse_gain[None], coarse_w,
+    near, mate_near, to_a, to_b, to_first, to_second = call(
+        functools.partial(share_kernel, n),
+        [shape((co_rows, width), F32)] * 2 + [shape((4 * co_rows, width), BF16)] * 2 + [shape((co_rows, width), BF16)] * 2,
+        own, sums, swap(sums),
         flops=2**32,
     )
-    beside = exchange(n, *sent)
     (base,) = call(base_kernel, [shape((nodes, width), F32)], fine_mid, prolong_in, flops=2**29)
     fine_out, coarse_out = call(
-        prolong_kernel,
+        functools.partial(prolong_kernel, n),
         [shape((nodes, width), BF16), shape((co_rows, width), BF16)],
-        fine_mid, base, lift, coarse_out, beside[0], beside[1], beside[2], prolong_in, prolong_out,
+        fine_mid, base, lift, near, mate_near, sums,
+        lax.ppermute(to_b, all_tiles, pairs_b),
+        lax.ppermute(to_a, all_tiles, pairs_a),
+        lax.ppermute(to_first, all_tiles, pairs_first),
+        lax.ppermute(to_second, all_tiles, pairs_second),
+        coarse_gain[None], coarse_w, prolong_in, prolong_out,
         to=pl.ANY,
-        scratch=[pltpu.VMEM((nodes, width), BF16), pltpu.SemaphoreType.DMA((PARTS + 1,))],
+        scratch=[
+            pltpu.VMEM((nodes, width), BF16),
+            pltpu.VMEM((co_rows, width), BF16),
+            pltpu.SemaphoreType.DMA((PARTS + 1,)),
+        ],
         flops=2**32,
     )
     return (fine_out[None, None], coarse_out)

time: 26.3 us -> 23.8 us (0.905)
  the two profiles are of different devices: /device:TPU:18 before, /device:TPU:0 now
where the time goes in v5:
time: 23.8 us; the launch traced here: 23.3 us
  Pallas kernels  10.1 us (42%)
  starting transfers between devices  8.18 us (34%)
  waiting for transfers between devices  3.16 us (13%)
  local copies, waits for them, and re-layouts  1.01 us (4%)
  between operations  0.83 us (3%)
    pallas_call x7, Pallas kernels, call(): pl.pallas_call(kernel, out_shape=outs, in_specs=[pl.BlockSpec(memory_spac...  10.1 us
    ppermute x1, starting transfers between devices, body(): lax.ppermute(to_a, all_tiles, pairs_a)  2.61 us
    ppermute x1, starting transfers between devices, body(): around_a = lax.ppermute(boundary, all_tiles, pairs_a)  2.59 us
    ppermute x1, starting transfers between devices, body(): lax.ppermute(to_first, all_tiles, pairs_first)  1.88 us
    ppermute x1, waiting for transfers between devices, body(): lax.ppermute(to_first, all_tiles, pairs_first)  1.75 us
    ppermute x2, waiting for transfers between devices, swap(): return lax.ppermute(value, 'ty', [(0, 1), (1, 0)])  1.14 us
    unnamed x32, local copies, waits for them, and re-layouts  1.01 us
    ppermute x2, starting transfers between devices, swap(): return lax.ppermute(value, 'ty', [(0, 1), (1, 0)])  0.72 us
  transfers between devices with their start and end apart: 8, of which 3 were waited for; matrix products, arithmetic and copies ran while one was open for 0% of the time, Pallas kernels for 24%

profile of v5, /device:TPU:0, one launch (start us, length us, event | category | flops | bytes accessed | tf_op | source)
XLA Modules:
  0.0 23.3 jit_solution(12014256256534259626)
XLA Ops:
  0.6 0.0 copy-start
  0.6 0.9 %copy-done = bf16[1,1,1024,128]{3,2,1,0:T(8,128)(2,1)S(1)} copy-done((bf16[1,1,1024,128]{3,2,1,0:T(8,128)(2,1)S(1)}, bf16[1,1,1024,128]{3,2,1,0:T(8,128)(2,1)}, u32[]{:S(2)}) %copy-start) | copy-done | bytes 262168
  1.6 0.5 %collective-permute-start.2 = (bf16[256,128]{1,0:T(8,128)(2,1)S(1)}, bf16[256,128]{1,0:T(8,128)(2,1)S(1)}, u32[]{:S(2)}, u32[]{:S(2)}) collective-permute-start(bf16[256,128]{1,0:T(8,128)(2,1)S(1)} %shard_map.167), channel_id=1, source_target_pairs={{0,1},{1,0},{2,3},{3,2},{4,5},{5,4},{6,7},{7,6},{8,9},{9,8},{10,11... | collective-permute-start | bytes 196616 | tf_op jit(solution)/shard_map/ppermute | solution.py:298
  2.1 2.6 %collective-permute-start.1 = (bf16[256,128]{1,0:T(8,128)(2,1)S(1)}, bf16[256,128]{1,0:T(8,128)(2,1)S(1)}, u32[]{:S(2)}, u32[]{:S(2)}) collective-permute-start(bf16[256,128]{1,0:T(8,128)(2,1)S(1)} %shard_map.167), channel_id=1, source_target_pairs={{0,2},{1,3},{2,0},{3,1},{4,6},{5,7},{6,4},{7,5},{8,10},{9,11},{10,... | collective-permute-start | bytes 196616 | tf_op jit(solution)/shard_map/ppermute | solution.py:329
  4.7 0.2 collective-permute-start
  4.9 0.0 copy-done.5
  4.9 0.0 copy-done.10
  4.9 0.0 copy-done.11
  4.9 0.0 copy-start.12
  4.9 2.9 %shard_map.168 = (f32[1024,40]{1,0:T(8,128)S(1)}, bf16[8,1024,128]{2,1,0:T(8,128)(2,1)S(1)}, f32[1024,128]{1,0:T(8,128)S(1)}, bf16[256,1024]{1,0:T(8,128)(2,1)S(1)}, bf16[1024,256]{1,0:T(8,128)(2,1)S(1)}) custom-call(bf16[1024,128]{1,0:T(8,128)(2,1)S(1)} %bitcast.12, s32[8,1024]{1,0:T(8,128)S(1)} %bitcast.15, s32[1,1024]{1,0:T(1,128)S(1)} %bitcast.16, ...), custom_call_target="tpu_custom_call" | custom-call | flops 8589934592 | bytes 8589934 | tf_op jit(solution)/shard_map/pallas_call | solution.py:274
  7.8 0.0 collective-permute-done.2.around_s
  7.9 0.3 %collective-permute-done.1.around_a = bf16[256,128]{1,0:T(8,128)(2,1)S(1)} collective-permute-done((bf16[256,128]{1,0:T(8,128)(2,1)S(1)}, bf16[256,128]{1,0:T(8,128)(2,1)S(1)}, u32[]{:S(2)}, u32[]{:S(2)}) %collective-permute-start.1) | collective-permute-done | bytes 65568 | tf_op jit(solution)/shard_map/ppermute | solution.py:329
  8.1 0.0 copy-done.1
  8.1 0.0 copy-start.7
  8.1 0.0 copy-start.9
  8.1 0.0 copy-start.13
  8.2 0.0 copy-start.14
  8.2 2.4 %shard_map.169.near = f32[8,1024,128]{2,1,0:T(8,128)S(1)} custom-call(bf16[1024,128]{1,0:T(8,128)(2,1)S(1)} %bitcast.13, bf16[256,128]{1,0:T(8,128)(2,1)S(1)} %collective-permute-done.1.around_a, bf16[256,128]{1,0:T(8,128)(2,1)S(1)} %collective-permute-done.2.around_s, f32[1024,40]{1,0:T(8,128)S(1)} %get-tuple-element.18.cols, ...), custom_call_target="tpu_custom_call" | custom-call | flops 8589934592 | bytes 8589934 | tf_op jit(solution)/shard_map/pallas_call | solution.py:274
  10.6 0.0 collective-permute-done.around_b
  10.7 2.8 %shard_map.170 = (bf16[1024,128]{1,0:T(8,128)(2,1)S(1)}, f32[64,128]{1,0:T(8,128)S(1)}, bf16[320,128]{1,0:T(8,128)(2,1)S(1)}) custom-call(bf16[1024,128]{1,0:T(8,128)(2,1)S(1)} %bitcast.14, bf16[256,128]{1,0:T(8,128)(2,1)S(1)} %collective-permute-done.around_b, f32[1024,40]{1,0:T(8,128)S(1)} %get-tuple-element.18.cols, f32[8,1024,128]{2,1,0:T(8,128)S(1)} %shard_map.169.near, ...), custom_call_target="tpu_custom_call" | custom-call | flops 8589934592 | bytes 8589934 | tf_op jit(solution)/shard_map/pallas_call | solution.py:274
  13.4 0.2 collective-permute-start.3
  13.6 1.1 %collective-permute-done.3.mate = bf16[320,128]{1,0:T(8,128)(2,1)S(1)} collective-permute-done((bf16[320,128]{1,0:T(8,128)(2,1)S(1)}, bf16[320,128]{1,0:T(8,128)(2,1)S(1)}, u32[]{:S(2)}, u32[]{:S(2)}) %collective-permute-start.3) | collective-permute-done | bytes 81952 | tf_op jit(solution)/shard_map/ppermute | solution.py:298
  14.8 0.2 collective-permute-start.4
  15.1 2.6 %collective-permute-start.5 = (bf16[256,128]{1,0:T(8,128)(2,1)S(1)}, bf16[256,128]{1,0:T(8,128)(2,1)S(1)}, u32[]{:S(2)}, u32[]{:S(2)}) collective-permute-start(bf16[256,128]{1,0:T(8,128)(2,1)S(1)} %get-tuple-element.29), channel_id=1, source_target_pairs={{0,2},{1,3},{2,0},{3,1},{4,6},{5,7},{6,4},{7,5},{8,10},{9,11},{10,... | collective-permute-start | bytes 196616 | tf_op jit(solution)/shard_map/ppermute | solution.py:371
  17.7 1.9 %collective-permute-start.6 = (bf16[64,128]{1,0:T(8,128)(2,1)S(1)}, bf16[64,128]{1,0:T(8,128)(2,1)S(1)}, u32[]{:S(2)}, u32[]{:S(2)}) collective-permute-start(bf16[64,128]{1,0:T(8,128)(2,1)S(1)} %get-tuple-element.30), channel_id=1, source_target_pairs={{0,4},{1,5},{2,6},{3,7},{4,0},{5,1},{6,2},{7,3},{8,12},{9,13},{10,... | collective-permute-start | bytes 49160 | tf_op jit(solution)/shard_map/ppermute | solution.py:372
  19.5 0.0 collective-permute-start.7
  19.5 0.2 shard_map.171.base
  19.8 1.8 %collective-permute-done.6.from_first = bf16[64,128]{1,0:T(8,128)(2,1)S(1)} collective-permute-done((bf16[64,128]{1,0:T(8,128)(2,1)S(1)}, bf16[64,128]{1,0:T(8,128)(2,1)S(1)}, u32[]{:S(2)}, u32[]{:S(2)}) %collective-permute-start.6) | collective-permute-done | bytes 16416 | tf_op jit(solution)/shard_map/ppermute | solution.py:372
  21.5 0.0 collective-permute-done.7.from_second
  21.5 0.0 collective-permute-done.4.from_b
  21.5 0.0 collective-permute-done.5.from_a
  21.6 1.7 %shard_map.173 = (bf16[1024,128]{1,0:T(8,128)(2,1)}, bf16[64,128]{1,0:T(8,128)(2,1)}) custom-call(bf16[1024,128]{1,0:T(8,128)(2,1)S(1)} %get-tuple-element.22.fine_mid, f32[1024,128]{1,0:T(8,128)S(1)} %shard_map.171.base, bf16[1024,256]{1,0:T(8,128)(2,1)S(1)} %get-tuple-element.23.lift, f32[64,128]{1,0:T(8,128)S(1)} %get-tuple-element.26.near, ...), custom_call_target="tpu_custom_call" | custom-call | flops 4294967296 | bytes 4294967 | tf_op jit(solution)/shard_map/pallas_call | solution.py:274
  (23 shorter events, 0.1 us)
Async XLA Ops:
  0.6 1.0 %copy-start = (bf16[1,1,1024,128]{3,2,1,0:T(8,128)(2,1)S(1)}, bf16[1,1,1024,128]{3,2,1,0:T(8,128)(2,1)}, u32[]{:S(2)}) copy-start(bf16[1,1,1024,128]{3,2,1,0:T(8,128)(2,1)} %param.16) | copy-start | bytes 786436
  1.6 3.3 %copy-start.5 = (s32[1,1,1024,8]{2,3,1,0:T(8,128)S(1)}, s32[1,1,1024,8]{2,3,1,0:T(8,128)}, u32[]{:S(2)}) copy-start(s32[1,1,1024,8]{2,3,1,0:T(8,128)} %param.17) | copy-start | bytes 98308
  1.6 3.3 %copy-start.10 = (s32[1,1,1024]{2,1,0:T(1,128)S(1)}, s32[1,1,1024]{2,1,0:T(1,128)}, u32[]{:S(2)}) copy-start(s32[1,1,1024]{2,1,0:T(1,128)} %param.18) | copy-start | bytes 12292
  1.6 3.3 %copy-start.11 = (bf16[1,1,1024]{2,1,0:T(2,128)(2,1)S(1)}, bf16[1,1,1024]{2,1,0:T(2,128)(2,1)}, u32[]{:S(2)}) copy-start(bf16[1,1,1024]{2,1,0:T(2,128)(2,1)} %param.19) | copy-start | bytes 6148
  1.6 6.2 %collective-permute-start.2 = (bf16[256,128]{1,0:T(8,128)(2,1)S(1)}, bf16[256,128]{1,0:T(8,128)(2,1)S(1)}, u32[]{:S(2)}, u32[]{:S(2)}) collective-permute-start(bf16[256,128]{1,0:T(8,128)(2,1)S(1)} %shard_map.167), channel_id=1, source_target_pairs={{0,1},{1,0},{2,3},{3,2},{4,5},{5,4},{6,7},{7,6},{8,9},{9,8},{10,11... | collective-permute-start | bytes 196616 | tf_op jit(solution)/shard_map/ppermute | solution.py:298
  2.1 6.0 %collective-permute-start.1 = (bf16[256,128]{1,0:T(8,128)(2,1)S(1)}, bf16[256,128]{1,0:T(8,128)(2,1)S(1)}, u32[]{:S(2)}, u32[]{:S(2)}) collective-permute-start(bf16[256,128]{1,0:T(8,128)(2,1)S(1)} %shard_map.167), channel_id=1, source_target_pairs={{0,2},{1,3},{2,0},{3,1},{4,6},{5,7},{6,4},{7,5},{8,10},{9,11},{10,... | collective-permute-start | bytes 196616 | tf_op jit(solution)/shard_map/ppermute | solution.py:329
  4.7 5.9 %collective-permute-start = (bf16[256,128]{1,0:T(8,128)(2,1)S(1)}, bf16[256,128]{1,0:T(8,128)(2,1)S(1)}, u32[]{:S(2)}, u32[]{:S(2)}) collective-permute-start(bf16[256,128]{1,0:T(8,128)(2,1)S(1)} %shard_map.167), channel_id=1, source_target_pairs={{0,1},{1,0},{2,4},{3,5},{4,2},{5,3},{6,8},{7,9},{8,6},{9,7},{10,12... | collective-permute-start | bytes 196616 | tf_op jit(solution)/shard_map/ppermute | solution.py:330
  4.9 3.2 %copy-start.1 = (bf16[2,128,128]{2,1,0:T(8,128)(2,1)S(1)}, bf16[2,128,128]{2,1,0:T(8,128)(2,1)}, u32[]{:S(2)}) copy-start(bf16[2,128,128]{2,1,0:T(8,128)(2,1)} %edge_in.3) | copy-start | bytes 196612
  4.9 3.2 %copy-start.12 = (f32[128]{0:T(128)S(1)}, f32[128]{0:T(128)}, u32[]{:S(2)}) copy-start(f32[128]{0:T(128)} %param.22) | copy-start | bytes 1540
  8.1 2.5 %copy-start.2 = (bf16[2,128,128]{2,1,0:T(8,128)(2,1)S(1)}, bf16[2,128,128]{2,1,0:T(8,128)(2,1)}, u32[]{:S(2)}) copy-start(bf16[2,128,128]{2,1,0:T(8,128)(2,1)} %node_in.1) | copy-start | bytes 196612
  8.1 2.5 %copy-start.6 = (bf16[128,128]{1,0:T(8,128)(2,1)S(1)}, bf16[128,128]{1,0:T(8,128)(2,1)}, u32[]{:S(2)}) copy-start(bf16[128,128]{1,0:T(8,128)(2,1)} %edge_out.1) | copy-start | bytes 98308
  8.1 2.5 %copy-start.7 = (bf16[128,128]{1,0:T(8,128)(2,1)S(1)}, bf16[128,128]{1,0:T(8,128)(2,1)}, u32[]{:S(2)}) copy-start(bf16[128,128]{1,0:T(8,128)(2,1)} %node_out.1) | copy-start | bytes 98308
  8.1 2.5 %copy-start.9 = (bf16[64,128]{1,0:T(8,128)(2,1)S(1)}, bf16[64,128]{1,0:T(8,128)(2,1)}, u32[]{:S(2)}) copy-start(bf16[64,128]{1,0:T(8,128)(2,1)} %state.1) | copy-start | bytes 49156
  8.1 2.5 %copy-start.13 = (f32[128]{0:T(128)S(1)}, f32[128]{0:T(128)}, u32[]{:S(2)}) copy-start(f32[128]{0:T(128)} %param.25) | copy-start | bytes 1540
  8.2 2.5 %copy-start.14 = (f32[128]{0:T(128)S(1)}, f32[128]{0:T(128)}, u32[]{:S(2)}) copy-start(f32[128]{0:T(128)} %param.27) | copy-start | bytes 1540
  13.4 1.3 %collective-permute-start.3 = (bf16[320,128]{1,0:T(8,128)(2,1)S(1)}, bf16[320,128]{1,0:T(8,128)(2,1)S(1)}, u32[]{:S(2)}, u32[]{:S(2)}) collective-permute-start(bf16[320,128]{1,0:T(8,128)(2,1)S(1)} %get-tuple-element.25.sums), channel_id=1, source_target_pairs={{0,1},{1,0},{2,3},{3,2},{4,5},{5,4},{6,7},{7,6},{8,9},{9,8},{10,11... | collective-permute-start | bytes 245768 | tf_op jit(solution)/shard_map/ppermute | solution.py:298
  14.8 4.8 %copy-start.3 = (bf16[2,128,128]{2,1,0:T(8,128)(2,1)S(1)}, bf16[2,128,128]{2,1,0:T(8,128)(2,1)}, u32[]{:S(2)}) copy-start(bf16[2,128,128]{2,1,0:T(8,128)(2,1)} %prolong_in.3) | copy-start | bytes 196612
  14.8 6.7 %copy-start.4 = (bf16[2,128,128]{2,1,0:T(8,128)(2,1)S(1)}, bf16[2,128,128]{2,1,0:T(8,128)(2,1)}, u32[]{:S(2)}) copy-start(bf16[2,128,128]{2,1,0:T(8,128)(2,1)} %coarse_w.1) | copy-start | bytes 196612
  14.8 6.7 %copy-start.8 = (bf16[128,128]{1,0:T(8,128)(2,1)S(1)}, bf16[128,128]{1,0:T(8,128)(2,1)}, u32[]{:S(2)}) copy-start(bf16[128,128]{1,0:T(8,128)(2,1)} %prolong_out.1) | copy-start | bytes 98308
  14.8 6.8 %copy-start.15 = (f32[128]{0:T(128)S(1)}, f32[128]{0:T(128)}, u32[]{:S(2)}) copy-start(f32[128]{0:T(128)} %param.28) | copy-start | bytes 1540
  14.8 6.7 %collective-permute-start.4 = (bf16[256,128]{1,0:T(8,128)(2,1)S(1)}, bf16[256,128]{1,0:T(8,128)(2,1)S(1)}, u32[]{:S(2)}, u32[]{:S(2)}) collective-permute-start(bf16[256,128]{1,0:T(8,128)(2,1)S(1)} %get-tuple-element.28), channel_id=1, source_target_pairs={{0,1},{1,0},{2,4},{3,5},{4,2},{5,3},{6,8},{7,9},{8,6},{9,7},{10,12... | collective-permute-start | bytes 196616 | tf_op jit(solution)/shard_map/ppermute | solution.py:370
  15.1 6.5 %collective-permute-start.5 = (bf16[256,128]{1,0:T(8,128)(2,1)S(1)}, bf16[256,128]{1,0:T(8,128)(2,1)S(1)}, u32[]{:S(2)}, u32[]{:S(2)}) collective-permute-start(bf16[256,128]{1,0:T(8,128)(2,1)S(1)} %get-tuple-element.29), channel_id=1, source_target_pairs={{0,2},{1,3},{2,0},{3,1},{4,6},{5,7},{6,4},{7,5},{8,10},{9,11},{10,... | collective-permute-start | bytes 196616 | tf_op jit(solution)/shard_map/ppermute | solution.py:371
  17.7 3.9 %collective-permute-start.6 = (bf16[64,128]{1,0:T(8,128)(2,1)S(1)}, bf16[64,128]{1,0:T(8,128)(2,1)S(1)}, u32[]{:S(2)}, u32[]{:S(2)}) collective-permute-start(bf16[64,128]{1,0:T(8,128)(2,1)S(1)} %get-tuple-element.30), channel_id=1, source_target_pairs={{0,4},{1,5},{2,6},{3,7},{4,0},{5,1},{6,2},{7,3},{8,12},{9,13},{10,... | collective-permute-start | bytes 49160 | tf_op jit(solution)/shard_map/ppermute | solution.py:372
  19.5 2.0 %collective-permute-start.7 = (bf16[64,128]{1,0:T(8,128)(2,1)S(1)}, bf16[64,128]{1,0:T(8,128)(2,1)S(1)}, u32[]{:S(2)}, u32[]{:S(2)}) collective-permute-start(bf16[64,128]{1,0:T(8,128)(2,1)S(1)} %get-tuple-element.31), channel_id=1, source_target_pairs={{0,1},{1,0},{2,3},{3,2},{4,8},{5,9},{6,10},{7,11},{8,4},{9,5},{10,... | collective-permute-start | bytes 49160 | tf_op jit(solution)/shard_map/ppermute | solution.py:373

commit v6 on v5

--- a/solution.py
+++ b/solution.py
@@ -76,7 +76,7 @@
     boundary[...] = tiles[: boundary.shape[0], :]
 
 
-def local_kernel(n, co_rows, tiles, sources, parents, weights, cols, near, scale, pool, lift):
+def local_kernel(n, co_rows, tiles, sources, parents, weights, cols, near, pieces, scale, pool):
     nodes, width = tiles.shape
     degree = near.shape[0]
     rim = nodes // 4
@@ -104,10 +104,6 @@
     ]
     turned = jnp.concatenate(rows, axis=0).T
     cols[...] = turned
-    scale[...] = turned[:, 4 * degree + 1 : 4 * degree + 2] * jnp.ones((1, width), F32)
-    row = lax.broadcasted_iota(I32, pool.shape, 0).astype(F32).astype(BF16)
-    pool[...] = jnp.where(row == slot.astype(BF16), jnp.ones((), BF16), jnp.zeros((), BF16))
-    lift[...] = one_hot(spread(cols[...], 4 * degree, nodes), 0, 4 * co_rows)
     table = jnp.concatenate([tiles[: 2 * rim, :], tiles[2 * rim :, :]], axis=1)
 
     def step(at, _):
@@ -121,13 +117,17 @@
             for g in group:
                 part = slice((g - k) * BLOCK, (g - k + 1) * BLOCK)
                 of = spread(col, 3 * degree + g, BLOCK)
+                pieces[g, here, :] = of
                 near[g, here, :] = jnp.where(of < jnp.full((), 2, BF16), got[part, :width], got[part, width:])
         return 0
 
     lax.fori_loop(0, nodes // BLOCK, step, 0, unroll=UNROLL)
-
-
-def side_kernel(tiles, around_a, around_s, cols, near, edge_in, edge_bias, edges, picked):
+    scale[...] = turned[:, 4 * degree + 1 : 4 * degree + 2] * jnp.ones((1, width), F32)
+    row = lax.broadcasted_iota(I32, pool.shape, 0).astype(F32).astype(BF16)
+    pool[...] = jnp.where(row == slot.astype(BF16), jnp.ones((), BF16), jnp.zeros((), BF16))
+
+
+def side_kernel(tiles, around_a, around_s, cols, near, pieces, edge_in, edge_bias, edges, picked):
     nodes, width = tiles.shape
     degree = near.shape[0]
     rim = nodes // 4
@@ -143,7 +143,7 @@
             got = mm(ones, table).astype(BF16)
             for g in group:
                 part = slice((g - k) * BLOCK, (g - k + 1) * BLOCK)
-                of = spread(col, 3 * degree + g, BLOCK)
+                of = pieces[g, here, :]
                 value = jnp.where(of < jnp.full((), 6, BF16), got[part, :width], got[part, width:])
                 picked[g // 2, here, g % 2 * width : (g % 2 + 1) * width] = value + near[g, here, :]
         return 0
@@ -189,12 +189,17 @@
     lax.fori_loop(0, nodes // BLOCK, step, 0, unroll=UNROLL)
     node_weights = 0.5 * jnp.concatenate([node_in[0], node_in[1]], axis=0)
     out_twice = jnp.concatenate([edge_out[...], edge_out[...]], axis=0)
+    out_f = node_out[...].astype(F32)
+    centred = split(out_f - jnp.mean(out_f, axis=-1, keepdims=True))
     for first in range(0, nodes, CHUNK):
         here = pl.ds(first, CHUNK)
         aggregate = mm(split(total[here, :]), out_twice).astype(BF16)
         both = jnp.concatenate([tiles[here, :], aggregate], axis=1)
         hidden = silu_of_twice(mm(both, node_weights) + 0.5 * node_bias[...]).astype(BF16)
-        update = normalise(mm(hidden, node_out[...]), node_gain[...])
+        center = mm(hidden, centred)
+        center = center[:, :width] + center[:, width:]
+        spread_of = jnp.mean(center * center, axis=-1, keepdims=True)
+        update = center * lax.rsqrt(spread_of + 1e-05) * node_gain[...]
         mid = (tiles[here, :].astype(F32) + update).astype(BF16)
         fine_mid[here, :] = mid
         weighted[here, :] = (mid.astype(F32) * scale[here, :]).astype(BF16)
@@ -206,7 +211,8 @@
     sums_out[...] = jnp.concatenate([high, low, to_s, to_a, to_b], axis=0)
 
 
-def base_kernel(fine_mid, prolong_in, base):
+def base_kernel(fine_mid, cols, prolong_in, base, lift):
+    lift[...] = one_hot(spread(cols[...], cols.shape[1] - 8, fine_mid.shape[0]), 0, lift.shape[1])
     base[...] = mm(fine_mid[...], 0.5 * prolong_in[0])
 
 
@@ -329,14 +335,14 @@
     around_a = lax.ppermute(boundary, all_tiles, pairs_a)
     around_b = lax.ppermute(boundary, all_tiles, pairs_b)
     around_s = swap(boundary)
-    cols, near, scale, pool, lift = call(
+    cols, near, pieces, scale, pool = call(
         functools.partial(local_kernel, n, co_rows),
         [
             shape((nodes, 40), F32),
             shape((degree, nodes, width), BF16),
+            shape((degree, nodes, width), BF16),
             shape((nodes, width), F32),
             shape((4 * co_rows, nodes), BF16),
-            shape((nodes, 4 * co_rows), BF16),
         ],
         latents, jnp.swapaxes(sources[0, 0], 0, 1), parents[0], restrict_w[0],
         flops=2**33,
@@ -344,7 +350,7 @@
     (edges,) = call(
         side_kernel,
         [shape((degree, nodes, width), F32)],
-        latents, around_a, around_s, cols, near, edge_in, edge_bias[None],
+        latents, around_a, around_s, cols, near, pieces, edge_in, edge_bias[None],
         flops=2**33,
         scratch=[pltpu.VMEM((degree // 2, nodes, 2 * width), BF16)],
     )
@@ -362,7 +368,12 @@
         own, sums, swap(sums),
         flops=2**32,
     )
-    (base,) = call(base_kernel, [shape((nodes, width), F32)], fine_mid, prolong_in, flops=2**29)
+    base, lift = call(
+        base_kernel,
+        [shape((nodes, width), F32), shape((nodes, 4 * co_rows), BF16)],
+        fine_mid, cols, prolong_in,
+        flops=2**29,
+    )
     fine_out, coarse_out = call(
         functools.partial(prolong_kernel, n),
         [shape((nodes, width), BF16), shape((co_rows, width), BF16)],

time: 23.8 us -> 23.4 us (0.983)
  the two profiles are of different devices: /device:TPU:0 before, /device:TPU:20 now
where the time goes in v6:
time: 23.4 us; the launch traced here: 23.2 us
  Pallas kernels  9.75 us (42%)
  starting transfers between devices  6.8 us (29%)
  waiting for transfers between devices  4.79 us (20%)
  local copies, waits for them, and re-layouts  1.02 us (4%)
  between operations  0.87 us (4%)
    pallas_call x7, Pallas kernels, call(): pl.pallas_call(kernel, out_shape=outs, in_specs=[pl.BlockSpec(memory_spac...  9.75 us
    ppermute x1, starting transfers between devices, body(): around_b = lax.ppermute(boundary, all_tiles, pairs_b)  2.53 us
    ppermute x1, waiting for transfers between devices, body(): lax.ppermute(to_first, all_tiles, pairs_first)  1.93 us
    ppermute x1, waiting for transfers between devices, body(): lax.ppermute(to_second, all_tiles, pairs_second)  1.58 us
    ppermute x1, starting transfers between devices, body(): lax.ppermute(to_first, all_tiles, pairs_first)  1.58 us
    ppermute x1, starting transfers between devices, body(): lax.ppermute(to_a, all_tiles, pairs_a)  1.52 us
    ppermute x2, waiting for transfers between devices, swap(): return lax.ppermute(value, 'ty', [(0, 1), (1, 0)])  1.27 us
    unnamed x32, local copies, waits for them, and re-layouts  1.02 us
  transfers between devices with their start and end apart: 8, of which 3 were waited for; matrix products, arithmetic and copies ran while one was open for 0% of the time, Pallas kernels for 23%

profile of v6, /device:TPU:20, one launch (start us, length us, event | category | flops | bytes accessed | tf_op | source)
XLA Modules:
  0.0 23.2 jit_solution(8195302081459642698)
XLA Ops:
  0.6 0.0 copy-start
  0.6 0.9 %copy-done = bf16[1,1,1024,128]{3,2,1,0:T(8,128)(2,1)S(1)} copy-done((bf16[1,1,1024,128]{3,2,1,0:T(8,128)(2,1)S(1)}, bf16[1,1,1024,128]{3,2,1,0:T(8,128)(2,1)}, u32[]{:S(2)}) %copy-start) | copy-done | bytes 262168
  1.6 0.1 collective-permute-start.2
  1.7 0.6 %collective-permute-start.1 = (bf16[256,128]{1,0:T(8,128)(2,1)S(1)}, bf16[256,128]{1,0:T(8,128)(2,1)S(1)}, u32[]{:S(2)}, u32[]{:S(2)}) collective-permute-start(bf16[256,128]{1,0:T(8,128)(2,1)S(1)} %shard_map.167), channel_id=1, source_target_pairs={{0,2},{1,3},{2,0},{3,1},{4,6},{5,7},{6,4},{7,5},{8,10},{9,11},{10,... | collective-permute-start | bytes 196616 | tf_op jit(solution)/shard_map/ppermute | solution.py:335
  2.2 2.5 %collective-permute-start = (bf16[256,128]{1,0:T(8,128)(2,1)S(1)}, bf16[256,128]{1,0:T(8,128)(2,1)S(1)}, u32[]{:S(2)}, u32[]{:S(2)}) collective-permute-start(bf16[256,128]{1,0:T(8,128)(2,1)S(1)} %shard_map.167), channel_id=1, source_target_pairs={{0,1},{1,0},{2,4},{3,5},{4,2},{5,3},{6,8},{7,9},{8,6},{9,7},{10,12... | collective-permute-start | bytes 196616 | tf_op jit(solution)/shard_map/ppermute | solution.py:336
  4.8 0.0 copy-start.12
  4.8 2.8 %shard_map.168 = (f32[1024,40]{1,0:T(8,128)S(1)}, bf16[8,1024,128]{2,1,0:T(8,128)(2,1)S(1)}, bf16[8,1024,128]{2,1,0:T(8,128)(2,1)S(1)}, f32[1024,128]{1,0:T(8,128)S(1)}, bf16[256,1024]{1,0:T(8,128)(2,1)S(1)}) custom-call(bf16[1024,128]{1,0:T(8,128)(2,1)S(1)} %bitcast.12, s32[8,1024]{1,0:T(8,128)S(1)} %bitcast.15, s32[1,1024]{1,0:T(1,128)S(1)} %bitcast.16, ...), custom_call_target="tpu_custom_call" | custom-call | flops 8589934592 | bytes 8589934 | tf_op jit(solution)/shard_map/pallas_call | solution.py:280
  7.6 0.0 collective-permute-done.2.around_s
  7.6 0.0 collective-permute-done.1.around_a
  7.6 0.0 copy-start.2
  7.6 0.0 copy-start.6
  7.7 0.0 copy-start.7
  7.7 0.0 copy-start.9
  7.7 0.0 copy-start.13
  7.7 0.0 copy-start.14
  7.7 2.2 %shard_map.169.near = f32[8,1024,128]{2,1,0:T(8,128)S(1)} custom-call(bf16[1024,128]{1,0:T(8,128)(2,1)S(1)} %bitcast.13, bf16[256,128]{1,0:T(8,128)(2,1)S(1)} %collective-permute-done.1.around_a, bf16[256,128]{1,0:T(8,128)(2,1)S(1)} %collective-permute-done.2.around_s, f32[1024,40]{1,0:T(8,128)S(1)} %get-tuple-element.20.cols, ...), custom_call_target="tpu_custom_call" | custom-call | flops 8589934592 | bytes 8589934 | tf_op jit(solution)/shard_map/pallas_call | solution.py:280
  10.0 0.0 collective-permute-done.around_b
  10.0 2.7 %shard_map.170 = (bf16[1024,128]{1,0:T(8,128)(2,1)S(1)}, f32[64,128]{1,0:T(8,128)S(1)}, bf16[320,128]{1,0:T(8,128)(2,1)S(1)}) custom-call(bf16[1024,128]{1,0:T(8,128)(2,1)S(1)} %bitcast.14, bf16[256,128]{1,0:T(8,128)(2,1)S(1)} %collective-permute-done.around_b, f32[1024,40]{1,0:T(8,128)S(1)} %get-tuple-element.20.cols, f32[8,1024,128]{2,1,0:T(8,128)S(1)} %shard_map.169.near, ...), custom_call_target="tpu_custom_call" | custom-call | flops 8589934592 | bytes 8589934 | tf_op jit(solution)/shard_map/pallas_call | solution.py:280
  12.8 0.1 collective-permute-start.3
  12.8 1.3 %collective-permute-done.3.mate = bf16[320,128]{1,0:T(8,128)(2,1)S(1)} collective-permute-done((bf16[320,128]{1,0:T(8,128)(2,1)S(1)}, bf16[320,128]{1,0:T(8,128)(2,1)S(1)}, u32[]{:S(2)}, u32[]{:S(2)}) %collective-permute-start.3) | collective-permute-done | bytes 81952 | tf_op jit(solution)/shard_map/ppermute | solution.py:304
  14.2 0.5 %collective-permute-start.4 = (bf16[256,128]{1,0:T(8,128)(2,1)S(1)}, bf16[256,128]{1,0:T(8,128)(2,1)S(1)}, u32[]{:S(2)}, u32[]{:S(2)}) collective-permute-start(bf16[256,128]{1,0:T(8,128)(2,1)S(1)} %get-tuple-element.32), channel_id=1, source_target_pairs={{0,1},{1,0},{2,4},{3,5},{4,2},{5,3},{6,8},{7,9},{8,6},{9,7},{10,12... | collective-permute-start | bytes 196616 | tf_op jit(solution)/shard_map/ppermute | solution.py:381
  14.6 1.5 %collective-permute-start.5 = (bf16[256,128]{1,0:T(8,128)(2,1)S(1)}, bf16[256,128]{1,0:T(8,128)(2,1)S(1)}, u32[]{:S(2)}, u32[]{:S(2)}) collective-permute-start(bf16[256,128]{1,0:T(8,128)(2,1)S(1)} %get-tuple-element.33), channel_id=1, source_target_pairs={{0,2},{1,3},{2,0},{3,1},{4,6},{5,7},{6,4},{7,5},{8,10},{9,11},{10,... | collective-permute-start | bytes 196616 | tf_op jit(solution)/shard_map/ppermute | solution.py:382
  16.1 1.6 %collective-permute-start.6 = (bf16[64,128]{1,0:T(8,128)(2,1)S(1)}, bf16[64,128]{1,0:T(8,128)(2,1)S(1)}, u32[]{:S(2)}, u32[]{:S(2)}) collective-permute-start(bf16[64,128]{1,0:T(8,128)(2,1)S(1)} %get-tuple-element.34), channel_id=1, source_target_pairs={{0,4},{1,5},{2,6},{3,7},{4,0},{5,1},{6,2},{7,3},{8,12},{9,13},{10,... | collective-permute-start | bytes 49160 | tf_op jit(solution)/shard_map/ppermute | solution.py:383
  17.7 0.0 collective-permute-start.7
  17.7 0.0 copy-done.3
  17.7 0.2 shard_map.171
  17.9 1.9 %collective-permute-done.6.from_first = bf16[64,128]{1,0:T(8,128)(2,1)S(1)} collective-permute-done((bf16[64,128]{1,0:T(8,128)(2,1)S(1)}, bf16[64,128]{1,0:T(8,128)(2,1)S(1)}, u32[]{:S(2)}, u32[]{:S(2)}) %collective-permute-start.6) | collective-permute-done | bytes 16416 | tf_op jit(solution)/shard_map/ppermute | solution.py:383
  19.9 1.6 %collective-permute-done.7.from_second = bf16[64,128]{1,0:T(8,128)(2,1)S(1)} collective-permute-done((bf16[64,128]{1,0:T(8,128)(2,1)S(1)}, bf16[64,128]{1,0:T(8,128)(2,1)S(1)}, u32[]{:S(2)}, u32[]{:S(2)}) %collective-permute-start.7) | collective-permute-done | bytes 16416 | tf_op jit(solution)/shard_map/ppermute | solution.py:384
  21.5 0.0 collective-permute-done.4.from_b
  21.5 0.0 collective-permute-done.5.from_a
  21.5 0.0 copy-done.8
  21.5 1.7 %shard_map.173 = (bf16[1024,128]{1,0:T(8,128)(2,1)}, bf16[64,128]{1,0:T(8,128)(2,1)}) custom-call(bf16[1024,128]{1,0:T(8,128)(2,1)S(1)} %get-tuple-element.25.fine_mid, f32[1024,128]{1,0:T(8,128)S(1)} %get-tuple-element.26.base, bf16[1024,256]{1,0:T(8,128)(2,1)S(1)} %get-tuple-element.27.lift, f32[64,128]{1,0:T(8,128)S(1)} %get-tuple-element.30.near, ...), custom_call_target="tpu_custom_call" | custom-call | flops 4294967296 | bytes 4294967 | tf_op jit(solution)/shard_map/pallas_call | solution.py:280
  (23 shorter events, 0.1 us)
Async XLA Ops:
  0.6 1.0 %copy-start = (bf16[1,1,1024,128]{3,2,1,0:T(8,128)(2,1)S(1)}, bf16[1,1,1024,128]{3,2,1,0:T(8,128)(2,1)}, u32[]{:S(2)}) copy-start(bf16[1,1,1024,128]{3,2,1,0:T(8,128)(2,1)} %param.16) | copy-start | bytes 786436
  1.6 3.2 %copy-start.5 = (s32[1,1,1024,8]{2,3,1,0:T(8,128)S(1)}, s32[1,1,1024,8]{2,3,1,0:T(8,128)}, u32[]{:S(2)}) copy-start(s32[1,1,1024,8]{2,3,1,0:T(8,128)} %param.17) | copy-start | bytes 98308
  1.6 3.2 %copy-start.10 = (s32[1,1,1024]{2,1,0:T(1,128)S(1)}, s32[1,1,1024]{2,1,0:T(1,128)}, u32[]{:S(2)}) copy-start(s32[1,1,1024]{2,1,0:T(1,128)} %param.18) | copy-start | bytes 12292
  1.6 3.2 %copy-start.11 = (bf16[1,1,1024]{2,1,0:T(2,128)(2,1)S(1)}, bf16[1,1,1024]{2,1,0:T(2,128)(2,1)}, u32[]{:S(2)}) copy-start(bf16[1,1,1024]{2,1,0:T(2,128)(2,1)} %param.19) | copy-start | bytes 6148
  1.6 6.0 %collective-permute-start.2 = (bf16[256,128]{1,0:T(8,128)(2,1)S(1)}, bf16[256,128]{1,0:T(8,128)(2,1)S(1)}, u32[]{:S(2)}, u32[]{:S(2)}) collective-permute-start(bf16[256,128]{1,0:T(8,128)(2,1)S(1)} %shard_map.167), channel_id=1, source_target_pairs={{0,1},{1,0},{2,3},{3,2},{4,5},{5,4},{6,7},{7,6},{8,9},{9,8},{10,11... | collective-permute-start | bytes 196616 | tf_op jit(solution)/shard_map/ppermute | solution.py:304
  1.7 5.9 %collective-permute-start.1 = (bf16[256,128]{1,0:T(8,128)(2,1)S(1)}, bf16[256,128]{1,0:T(8,128)(2,1)S(1)}, u32[]{:S(2)}, u32[]{:S(2)}) collective-permute-start(bf16[256,128]{1,0:T(8,128)(2,1)S(1)} %shard_map.167), channel_id=1, source_target_pairs={{0,2},{1,3},{2,0},{3,1},{4,6},{5,7},{6,4},{7,5},{8,10},{9,11},{10,... | collective-permute-start | bytes 196616 | tf_op jit(solution)/shard_map/ppermute | solution.py:335
  2.2 7.7 %collective-permute-start = (bf16[256,128]{1,0:T(8,128)(2,1)S(1)}, bf16[256,128]{1,0:T(8,128)(2,1)S(1)}, u32[]{:S(2)}, u32[]{:S(2)}) collective-permute-start(bf16[256,128]{1,0:T(8,128)(2,1)S(1)} %shard_map.167), channel_id=1, source_target_pairs={{0,1},{1,0},{2,4},{3,5},{4,2},{5,3},{6,8},{7,9},{8,6},{9,7},{10,12... | collective-permute-start | bytes 196616 | tf_op jit(solution)/shard_map/ppermute | solution.py:336
  4.8 2.8 %copy-start.1 = (bf16[2,128,128]{2,1,0:T(8,128)(2,1)S(1)}, bf16[2,128,128]{2,1,0:T(8,128)(2,1)}, u32[]{:S(2)}) copy-start(bf16[2,128,128]{2,1,0:T(8,128)(2,1)} %edge_in.3) | copy-start | bytes 196612
  4.8 2.8 %copy-start.12 = (f32[128]{0:T(128)S(1)}, f32[128]{0:T(128)}, u32[]{:S(2)}) copy-start(f32[128]{0:T(128)} %param.22) | copy-start | bytes 1540
  7.6 2.3 %copy-start.2 = (bf16[2,128,128]{2,1,0:T(8,128)(2,1)S(1)}, bf16[2,128,128]{2,1,0:T(8,128)(2,1)}, u32[]{:S(2)}) copy-start(bf16[2,128,128]{2,1,0:T(8,128)(2,1)} %node_in.1) | copy-start | bytes 196612
  7.6 2.3 %copy-start.6 = (bf16[128,128]{1,0:T(8,128)(2,1)S(1)}, bf16[128,128]{1,0:T(8,128)(2,1)}, u32[]{:S(2)}) copy-start(bf16[128,128]{1,0:T(8,128)(2,1)} %edge_out.1) | copy-start | bytes 98308
  7.7 2.3 %copy-start.7 = (bf16[128,128]{1,0:T(8,128)(2,1)S(1)}, bf16[128,128]{1,0:T(8,128)(2,1)}, u32[]{:S(2)}) copy-start(bf16[128,128]{1,0:T(8,128)(2,1)} %node_out.1) | copy-start | bytes 98308
  7.7 2.3 %copy-start.9 = (bf16[64,128]{1,0:T(8,128)(2,1)S(1)}, bf16[64,128]{1,0:T(8,128)(2,1)}, u32[]{:S(2)}) copy-start(bf16[64,128]{1,0:T(8,128)(2,1)} %state.1) | copy-start | bytes 49156
  7.7 2.3 %copy-start.13 = (f32[128]{0:T(128)S(1)}, f32[128]{0:T(128)}, u32[]{:S(2)}) copy-start(f32[128]{0:T(128)} %param.25) | copy-start | bytes 1540
  7.7 2.3 %copy-start.14 = (f32[128]{0:T(128)S(1)}, f32[128]{0:T(128)}, u32[]{:S(2)}) copy-start(f32[128]{0:T(128)} %param.27) | copy-start | bytes 1540
  12.8 1.3 %collective-permute-start.3 = (bf16[320,128]{1,0:T(8,128)(2,1)S(1)}, bf16[320,128]{1,0:T(8,128)(2,1)S(1)}, u32[]{:S(2)}, u32[]{:S(2)}) collective-permute-start(bf16[320,128]{1,0:T(8,128)(2,1)S(1)} %get-tuple-element.29.sums), channel_id=1, source_target_pairs={{0,1},{1,0},{2,3},{3,2},{4,5},{5,4},{6,7},{7,6},{8,9},{9,8},{10,11... | collective-permute-start | bytes 245768 | tf_op jit(solution)/shard_map/ppermute | solution.py:304
  14.1 3.6 %copy-start.3 = (bf16[2,128,128]{2,1,0:T(8,128)(2,1)S(1)}, bf16[2,128,128]{2,1,0:T(8,128)(2,1)}, u32[]{:S(2)}) copy-start(bf16[2,128,128]{2,1,0:T(8,128)(2,1)} %prolong_in.3) | copy-start | bytes 196612
  14.1 7.4 %copy-start.4 = (bf16[2,128,128]{2,1,0:T(8,128)(2,1)S(1)}, bf16[2,128,128]{2,1,0:T(8,128)(2,1)}, u32[]{:S(2)}) copy-start(bf16[2,128,128]{2,1,0:T(8,128)(2,1)} %coarse_w.1) | copy-start | bytes 196612
  14.1 7.4 %copy-start.8 = (bf16[128,128]{1,0:T(8,128)(2,1)S(1)}, bf16[128,128]{1,0:T(8,128)(2,1)}, u32[]{:S(2)}) copy-start(bf16[128,128]{1,0:T(8,128)(2,1)} %prolong_out.1) | copy-start | bytes 98308
  14.1 7.4 %copy-start.15 = (f32[128]{0:T(128)S(1)}, f32[128]{0:T(128)}, u32[]{:S(2)}) copy-start(f32[128]{0:T(128)} %param.28) | copy-start | bytes 1540
  14.2 7.3 %collective-permute-start.4 = (bf16[256,128]{1,0:T(8,128)(2,1)S(1)}, bf16[256,128]{1,0:T(8,128)(2,1)S(1)}, u32[]{:S(2)}, u32[]{:S(2)}) collective-permute-start(bf16[256,128]{1,0:T(8,128)(2,1)S(1)} %get-tuple-element.32), channel_id=1, source_target_pairs={{0,1},{1,0},{2,4},{3,5},{4,2},{5,3},{6,8},{7,9},{8,6},{9,7},{10,12... | collective-permute-start | bytes 196616 | tf_op jit(solution)/shard_map/ppermute | solution.py:381
  14.6 6.8 %collective-permute-start.5 = (bf16[256,128]{1,0:T(8,128)(2,1)S(1)}, bf16[256,128]{1,0:T(8,128)(2,1)S(1)}, u32[]{:S(2)}, u32[]{:S(2)}) collective-permute-start(bf16[256,128]{1,0:T(8,128)(2,1)S(1)} %get-tuple-element.33), channel_id=1, source_target_pairs={{0,2},{1,3},{2,0},{3,1},{4,6},{5,7},{6,4},{7,5},{8,10},{9,11},{10,... | collective-permute-start | bytes 196616 | tf_op jit(solution)/shard_map/ppermute | solution.py:382
  16.1 3.7 %collective-permute-start.6 = (bf16[64,128]{1,0:T(8,128)(2,1)S(1)}, bf16[64,128]{1,0:T(8,128)(2,1)S(1)}, u32[]{:S(2)}, u32[]{:S(2)}) collective-permute-start(bf16[64,128]{1,0:T(8,128)(2,1)S(1)} %get-tuple-element.34), channel_id=1, source_target_pairs={{0,4},{1,5},{2,6},{3,7},{4,0},{5,1},{6,2},{7,3},{8,12},{9,13},{10,... | collective-permute-start | bytes 49160 | tf_op jit(solution)/shard_map/ppermute | solution.py:383
  17.7 3.7 %collective-permute-start.7 = (bf16[64,128]{1,0:T(8,128)(2,1)S(1)}, bf16[64,128]{1,0:T(8,128)(2,1)S(1)}, u32[]{:S(2)}, u32[]{:S(2)}) collective-permute-start(bf16[64,128]{1,0:T(8,128)(2,1)S(1)} %get-tuple-element.35), channel_id=1, source_target_pairs={{0,1},{1,0},{2,3},{3,2},{4,8},{5,9},{6,10},{7,11},{8,4},{9,5},{10,... | collective-permute-start | bytes 49160 | tf_op jit(solution)/shard_map/ppermute | solution.py:384

commit v7 on v6

--- a/solution.py
+++ b/solution.py
@@ -95,8 +95,7 @@
     piece_a, piece_b = jnp.where(even, 5, 4), jnp.where(inner, jnp.where(even, 4, 5), -1)
     rows = [
         jnp.where(piece < 4, (index & (2 * rim - 1)) - rim, nowhere).astype(F32),
-        jnp.where((piece == piece_a) | (piece == 7 - j), low, nowhere).astype(F32),
-        jnp.where(piece == piece_b, low, nowhere).astype(F32),
+        jnp.where((piece == piece_a) | (piece == piece_b) | (piece == 7 - j), low, nowhere).astype(F32),
         piece.astype(F32),
         slot,
         weights[...].astype(F32),
@@ -116,77 +115,54 @@
             got = mm(ones, table).astype(BF16)
             for g in group:
                 part = slice((g - k) * BLOCK, (g - k + 1) * BLOCK)
-                of = spread(col, 3 * degree + g, BLOCK)
+                of = spread(col, 2 * degree + g, BLOCK)
                 pieces[g, here, :] = of
                 near[g, here, :] = jnp.where(of < jnp.full((), 2, BF16), got[part, :width], got[part, width:])
         return 0
 
     lax.fori_loop(0, nodes // BLOCK, step, 0, unroll=UNROLL)
-    scale[...] = turned[:, 4 * degree + 1 : 4 * degree + 2] * jnp.ones((1, width), F32)
+    scale[...] = turned[:, 3 * degree + 1 : 3 * degree + 2] * jnp.ones((1, width), F32)
     row = lax.broadcasted_iota(I32, pool.shape, 0).astype(F32).astype(BF16)
     pool[...] = jnp.where(row == slot.astype(BF16), jnp.ones((), BF16), jnp.zeros((), BF16))
 
 
-def side_kernel(tiles, around_a, around_s, cols, near, pieces, edge_in, edge_bias, edges, picked):
+def node_kernel(
+    n, tiles, around_s, around_a, around_b, cols, near, pieces, scale, pool,
+    edge_in, edge_bias, edge_out, node_in, node_bias, node_out, node_gain, state,
+    fine_mid, own, sums_out, total, weighted, picked,
+):
     nodes, width = tiles.shape
     degree = near.shape[0]
     rim = nodes // 4
-    table = jnp.concatenate([around_a[...], around_s[...]], axis=1)
-
-    def step(at, _):
-        first = pl.multiple_of(at * BLOCK, BLOCK)
-        here = pl.ds(first, BLOCK)
+    co_rows = own.shape[0]
+    _, _, even = place(n)
+    got_a, got_b = around_a[...], around_b[...]
+    table = jnp.concatenate([jnp.where(even, got_b, got_a), jnp.where(even, got_a, got_b), around_s[...]], axis=1)
+    for at in range(nodes // BLOCK):
+        here = slice(at * BLOCK, (at + 1) * BLOCK)
         col = cols[here, :]
         for k in range(0, degree, GROUP):
             group = range(k, k + GROUP)
             ones = jnp.concatenate([one_hot(spread(col, degree + g, BLOCK), 0, rim) for g in group], axis=0)
             got = mm(ones, table).astype(BF16)
             for g in group:
-                part = slice((g - k) * BLOCK, (g - k + 1) * BLOCK)
+                part = got[(g - k) * BLOCK : (g - k + 1) * BLOCK]
                 of = pieces[g, here, :]
-                value = jnp.where(of < jnp.full((), 6, BF16), got[part, :width], got[part, width:])
+                value = jnp.where(of < jnp.full((), 5, BF16), part[:, :width], part[:, width : 2 * width])
+                value = jnp.where(of < jnp.full((), 6, BF16), value, part[:, 2 * width :])
                 picked[g // 2, here, g % 2 * width : (g % 2 + 1) * width] = value + near[g, here, :]
-        return 0
-
-    lax.fori_loop(0, nodes // BLOCK, step, 0, unroll=UNROLL)
     project = 0.5 * edge_in[1]
     empty = jnp.zeros_like(project)
     project = jnp.concatenate(
         [jnp.concatenate([project, empty], axis=1), jnp.concatenate([empty, project], axis=1)], axis=0
     )
     dst = mm(tiles[...], 0.5 * edge_in[0]) + 0.5 * edge_bias[...]
+    sums = jnp.zeros((nodes, width), F32)
     for pair in range(degree // 2):
         src = mm(picked[pair], project)
-        edges[2 * pair] = dst + src[:, :width]
-        edges[2 * pair + 1] = dst + src[:, width:]
-
-
-def node_kernel(
-    tiles, around_b, cols, near, scale, pool, edge_in, edge_out, node_in, node_bias, node_out, node_gain, state,
-    fine_mid, own, sums_out, total, weighted,
-):
-    nodes, width = tiles.shape
-    degree = near.shape[0]
-    rim = nodes // 4
-    co_rows = own.shape[0]
-    table = split(mm(around_b[...], 0.5 * edge_in[1]))
-
-    def step(at, _):
-        first = pl.multiple_of(at * BLOCK, BLOCK)
-        here = pl.ds(first, BLOCK)
-        col = cols[here, :]
-        sums = jnp.zeros((BLOCK, width), F32)
-        for k in range(0, degree, GROUP):
-            ones = [one_hot(spread(col, 2 * degree + k + g, BLOCK), 0, rim) for g in range(GROUP)]
-            got = mm(jnp.concatenate(ones, axis=0), table)
-            for g in range(GROUP):
-                part = got[g * BLOCK : (g + 1) * BLOCK]
-                edge = near[k + g, here, :] + (part[:, :width] + part[:, width:])
-                sums = sums + silu_of_twice(edge).astype(BF16).astype(F32)
-        total[here, :] = sums
-        return 0
-
-    lax.fori_loop(0, nodes // BLOCK, step, 0, unroll=UNROLL)
+        for part in (src[:, :width], src[:, width:]):
+            sums = sums + silu_of_twice(dst + part).astype(BF16).astype(F32)
+    total[...] = sums
     node_weights = 0.5 * jnp.concatenate([node_in[0], node_in[1]], axis=0)
     out_twice = jnp.concatenate([edge_out[...], edge_out[...]], axis=0)
     out_f = node_out[...].astype(F32)
@@ -236,7 +212,7 @@
 
 
 def prolong_kernel(
-    n, fine_mid, base, lift, near, mate_near, sums, from_b, from_a, from_first, from_second, coarse_gain, coarse_w,
+    n, fine_mid, base, lift, near, mate_near, sums, from_a, from_first, from_b, from_second, coarse_gain, coarse_w,
     prolong_in, prolong_out, out, coarse_out, ready, coarse_ready, sems,
 ):
     nodes, width = fine_mid.shape
@@ -338,7 +314,7 @@
     cols, near, pieces, scale, pool = call(
         functools.partial(local_kernel, n, co_rows),
         [
-            shape((nodes, 40), F32),
+            shape((nodes, 32), F32),
             shape((degree, nodes, width), BF16),
             shape((degree, nodes, width), BF16),
             shape((nodes, width), F32),
@@ -347,20 +323,17 @@
         latents, jnp.swapaxes(sources[0, 0], 0, 1), parents[0], restrict_w[0],
         flops=2**33,
     )
-    (edges,) = call(
-        side_kernel,
-        [shape((degree, nodes, width), F32)],
-        latents, around_a, around_s, cols, near, pieces, edge_in, edge_bias[None],
+    fine_mid, own, sums = call(
+        functools.partial(node_kernel, n),
+        [shape((nodes, width), BF16), shape((co_rows, width), F32), shape((5 * co_rows, width), BF16)],
+        latents, around_s, around_a, around_b, cols, near, pieces, scale, pool,
+        edge_in, edge_bias[None], edge_out, node_in, node_bias[None], node_out, node_gain[None], coarse_state,
         flops=2**33,
-        scratch=[pltpu.VMEM((degree // 2, nodes, 2 * width), BF16)],
-    )
-    fine_mid, own, sums = call(
-        node_kernel,
-        [shape((nodes, width), BF16), shape((co_rows, width), F32), shape((5 * co_rows, width), BF16)],
-        latents, around_b, cols, edges, scale, pool, edge_in, edge_out, node_in, node_bias[None], node_out, node_gain[None],
-        coarse_state,
-        flops=2**33,
-        scratch=[pltpu.VMEM((nodes, width), F32), pltpu.VMEM((nodes, width), BF16)],
+        scratch=[
+            pltpu.VMEM((nodes, width), F32),
+            pltpu.VMEM((nodes, width), BF16),
+            pltpu.VMEM((degree // 2, nodes, 2 * width), BF16),
+        ],
     )
     near, mate_near, to_a, to_b, to_first, to_second = call(
         functools.partial(share_kernel, n),
@@ -378,9 +351,9 @@
         functools.partial(prolong_kernel, n),
         [shape((nodes, width), BF16), shape((co_rows, width), BF16)],
         fine_mid, base, lift, near, mate_near, sums,
-        lax.ppermute(to_b, all_tiles, pairs_b),
         lax.ppermute(to_a, all_tiles, pairs_a),
         lax.ppermute(to_first, all_tiles, pairs_first),
+        lax.ppermute(to_b, all_tiles, pairs_b),
         lax.ppermute(to_second, all_tiles, pairs_second),
         coarse_gain[None], coarse_w, prolong_in, prolong_out,
         to=pl.ANY,

time: 23.4 us -> 22.8 us (0.974)
  the two profiles are of different devices: /device:TPU:20 before, /device:TPU:0 now
where the time goes in v7:
time: 22.8 us; the launch traced here: 22.7 us
  Pallas kernels  9.01 us (40%)
  starting transfers between devices  8.68 us (38%)
  waiting for transfers between devices  3.12 us (14%)
  local copies, waits for them, and re-layouts  1.02 us (4%)
  between operations  0.86 us (4%)
    pallas_call x6, Pallas kernels, call(): pl.pallas_call(kernel, out_shape=outs, in_specs=[pl.BlockSpec(memory_spac...  9.01 us
    ppermute x1, starting transfers between devices, body(): around_a = lax.ppermute(boundary, all_tiles, pairs_a)  4.03 us
    ppermute x1, waiting for transfers between devices, body(): lax.ppermute(to_first, all_tiles, pairs_first)  2.18 us
    ppermute x1, starting transfers between devices, body(): lax.ppermute(to_first, all_tiles, pairs_first)  2.01 us
    ppermute x1, starting transfers between devices, body(): lax.ppermute(to_a, all_tiles, pairs_a)  1.55 us
    unnamed x32, local copies, waits for them, and re-layouts  1.02 us
    ppermute x2, waiting for transfers between devices, swap(): return lax.ppermute(value, 'ty', [(0, 1), (1, 0)])  0.93 us
    ppermute x2, starting transfers between devices, swap(): return lax.ppermute(value, 'ty', [(0, 1), (1, 0)])  0.56 us
  transfers between devices with their start and end apart: 8, of which 2 were waited for; matrix products, arithmetic and copies ran while one was open for 0% of the time, Pallas kernels for 13%

profile of v7, /device:TPU:0, one launch (start us, length us, event | category | flops | bytes accessed | tf_op | source)
XLA Modules:
  0.0 22.7 jit_solution(13716345345769936422)
XLA Ops:
  0.6 0.9 %copy-done = bf16[1,1,1024,128]{3,2,1,0:T(8,128)(2,1)S(1)} copy-done((bf16[1,1,1024,128]{3,2,1,0:T(8,128)(2,1)S(1)}, bf16[1,1,1024,128]{3,2,1,0:T(8,128)(2,1)}, u32[]{:S(2)}) %copy-start) | copy-done | bytes 262168
  1.6 0.5 %collective-permute-start.2 = (bf16[256,128]{1,0:T(8,128)(2,1)S(1)}, bf16[256,128]{1,0:T(8,128)(2,1)S(1)}, u32[]{:S(2)}, u32[]{:S(2)}) collective-permute-start(bf16[256,128]{1,0:T(8,128)(2,1)S(1)} %shard_map.167), channel_id=1, source_target_pairs={{0,1},{1,0},{2,4},{3,5},{4,2},{5,3},{6,8},{7,9},{8,6},{9,7},{10,12... | collective-permute-start | bytes 196616 | tf_op jit(solution)/shard_map/ppermute | solution.py:312
  2.1 4.0 %collective-permute-start.1 = (bf16[256,128]{1,0:T(8,128)(2,1)S(1)}, bf16[256,128]{1,0:T(8,128)(2,1)S(1)}, u32[]{:S(2)}, u32[]{:S(2)}) collective-permute-start(bf16[256,128]{1,0:T(8,128)(2,1)S(1)} %shard_map.167), channel_id=1, source_target_pairs={{0,2},{1,3},{2,0},{3,1},{4,6},{5,7},{6,4},{7,5},{8,10},{9,11},{10,... | collective-permute-start | bytes 196616 | tf_op jit(solution)/shard_map/ppermute | solution.py:311
  6.1 0.0 collective-permute-start
  6.2 0.0 copy-start.1
  6.2 0.0 copy-start.2
  6.2 0.0 copy-start.6
  6.2 0.0 copy-start.7
  6.2 0.0 copy-start.9
  6.2 0.0 copy-start.12
  6.2 0.0 copy-start.13
  6.3 0.0 copy-start.14
  6.3 2.8 %shard_map.168 = (f32[1024,32]{1,0:T(8,128)S(1)}, bf16[8,1024,128]{2,1,0:T(8,128)(2,1)S(1)}, bf16[8,1024,128]{2,1,0:T(8,128)(2,1)S(1)}, f32[1024,128]{1,0:T(8,128)S(1)}, bf16[256,1024]{1,0:T(8,128)(2,1)S(1)}) custom-call(bf16[1024,128]{1,0:T(8,128)(2,1)S(1)} %bitcast.12, s32[8,1024]{1,0:T(8,128)S(1)} %bitcast.14, s32[1,1024]{1,0:T(1,128)S(1)} %bitcast.15, ...), custom_call_target="tpu_custom_call" | custom-call | flops 8589934592 | bytes 8589934 | tf_op jit(solution)/shard_map/pallas_call | solution.py:256
  9.1 0.0 collective-permute-done.2.around_b
  9.1 0.0 collective-permute-done.1.around_a
  9.1 0.0 collective-permute-done.around_s
  9.2 4.2 %shard_map.169 = (bf16[1024,128]{1,0:T(8,128)(2,1)S(1)}, f32[64,128]{1,0:T(8,128)S(1)}, bf16[320,128]{1,0:T(8,128)(2,1)S(1)}) custom-call(bf16[1024,128]{1,0:T(8,128)(2,1)S(1)} %bitcast.13, bf16[256,128]{1,0:T(8,128)(2,1)S(1)} %collective-permute-done.around_s, bf16[256,128]{1,0:T(8,128)(2,1)S(1)} %collective-permute-done.1.around_a, ...), custom_call_target="tpu_custom_call" | custom-call | flops 8589934592 | bytes 8589934 | tf_op jit(solution)/shard_map/pallas_call | solution.py:256
  13.4 0.6 %collective-permute-start.3 = (bf16[320,128]{1,0:T(8,128)(2,1)S(1)}, bf16[320,128]{1,0:T(8,128)(2,1)S(1)}, u32[]{:S(2)}, u32[]{:S(2)}) collective-permute-start(bf16[320,128]{1,0:T(8,128)(2,1)S(1)} %get-tuple-element.29.sums), channel_id=1, source_target_pairs={{0,1},{1,0},{2,3},{3,2},{4,5},{5,4},{6,7},{7,6},{8,9},{9,8},{10,11... | collective-permute-start | bytes 245768 | tf_op jit(solution)/shard_map/ppermute | solution.py:280
  14.0 0.9 %collective-permute-done.3.mate = bf16[320,128]{1,0:T(8,128)(2,1)S(1)} collective-permute-done((bf16[320,128]{1,0:T(8,128)(2,1)S(1)}, bf16[320,128]{1,0:T(8,128)(2,1)S(1)}, u32[]{:S(2)}, u32[]{:S(2)}) %collective-permute-start.3) | collective-permute-done | bytes 81952 | tf_op jit(solution)/shard_map/ppermute | solution.py:280
  14.9 1.6 %collective-permute-start.4 = (bf16[256,128]{1,0:T(8,128)(2,1)S(1)}, bf16[256,128]{1,0:T(8,128)(2,1)S(1)}, u32[]{:S(2)}, u32[]{:S(2)}) collective-permute-start(bf16[256,128]{1,0:T(8,128)(2,1)S(1)} %get-tuple-element.32), channel_id=1, source_target_pairs={{0,2},{1,3},{2,0},{3,1},{4,6},{5,7},{6,4},{7,5},{8,10},{9,11},{10,... | collective-permute-start | bytes 196616 | tf_op jit(solution)/shard_map/ppermute | solution.py:354
  16.5 0.0 collective-permute-start.6
  16.5 2.0 %collective-permute-start.5 = (bf16[64,128]{1,0:T(8,128)(2,1)S(1)}, bf16[64,128]{1,0:T(8,128)(2,1)S(1)}, u32[]{:S(2)}, u32[]{:S(2)}) collective-permute-start(bf16[64,128]{1,0:T(8,128)(2,1)S(1)} %get-tuple-element.33), channel_id=1, source_target_pairs={{0,4},{1,5},{2,6},{3,7},{4,0},{5,1},{6,2},{7,3},{8,12},{9,13},{10,... | collective-permute-start | bytes 49160 | tf_op jit(solution)/shard_map/ppermute | solution.py:355
  18.5 0.0 collective-permute-start.7
  18.5 0.2 shard_map.170
  18.7 2.2 %collective-permute-done.5.from_first = bf16[64,128]{1,0:T(8,128)(2,1)S(1)} collective-permute-done((bf16[64,128]{1,0:T(8,128)(2,1)S(1)}, bf16[64,128]{1,0:T(8,128)(2,1)S(1)}, u32[]{:S(2)}, u32[]{:S(2)}) %collective-permute-start.5) | collective-permute-done | bytes 16416 | tf_op jit(solution)/shard_map/ppermute | solution.py:355
  20.9 0.0 collective-permute-done.7.from_second
  20.9 0.0 collective-permute-done.4.from_a
  20.9 0.0 collective-permute-done.6.from_b
  20.9 0.0 copy-done.4
  20.9 0.0 copy-done.8
  20.9 0.0 copy-done.15
  21.0 1.7 %shard_map.172 = (bf16[1024,128]{1,0:T(8,128)(2,1)}, bf16[64,128]{1,0:T(8,128)(2,1)}) custom-call(bf16[1024,128]{1,0:T(8,128)(2,1)S(1)} %get-tuple-element.25.fine_mid, f32[1024,128]{1,0:T(8,128)S(1)} %get-tuple-element.26.base, bf16[1024,256]{1,0:T(8,128)(2,1)S(1)} %get-tuple-element.27.lift, f32[64,128]{1,0:T(8,128)S(1)} %get-tuple-element.30.near, ...), custom_call_target="tpu_custom_call" | custom-call | flops 4294967296 | bytes 4294967 | tf_op jit(solution)/shard_map/pallas_call | solution.py:256
  (22 shorter events, 0.1 us)
Async XLA Ops:
  0.6 1.0 %copy-start = (bf16[1,1,1024,128]{3,2,1,0:T(8,128)(2,1)S(1)}, bf16[1,1,1024,128]{3,2,1,0:T(8,128)(2,1)}, u32[]{:S(2)}) copy-start(bf16[1,1,1024,128]{3,2,1,0:T(8,128)(2,1)} %param.16) | copy-start | bytes 786436
  1.6 4.6 %copy-start.5 = (s32[1,1,1024,8]{2,3,1,0:T(8,128)S(1)}, s32[1,1,1024,8]{2,3,1,0:T(8,128)}, u32[]{:S(2)}) copy-start(s32[1,1,1024,8]{2,3,1,0:T(8,128)} %param.17) | copy-start | bytes 98308
  1.6 4.6 %copy-start.10 = (s32[1,1,1024]{2,1,0:T(1,128)S(1)}, s32[1,1,1024]{2,1,0:T(1,128)}, u32[]{:S(2)}) copy-start(s32[1,1,1024]{2,1,0:T(1,128)} %param.18) | copy-start | bytes 12292
  1.6 4.6 %copy-start.11 = (bf16[1,1,1024]{2,1,0:T(2,128)(2,1)S(1)}, bf16[1,1,1024]{2,1,0:T(2,128)(2,1)}, u32[]{:S(2)}) copy-start(bf16[1,1,1024]{2,1,0:T(2,128)(2,1)} %param.19) | copy-start | bytes 6148
  1.6 7.5 %collective-permute-start.2 = (bf16[256,128]{1,0:T(8,128)(2,1)S(1)}, bf16[256,128]{1,0:T(8,128)(2,1)S(1)}, u32[]{:S(2)}, u32[]{:S(2)}) collective-permute-start(bf16[256,128]{1,0:T(8,128)(2,1)S(1)} %shard_map.167), channel_id=1, source_target_pairs={{0,1},{1,0},{2,4},{3,5},{4,2},{5,3},{6,8},{7,9},{8,6},{9,7},{10,12... | collective-permute-start | bytes 196616 | tf_op jit(solution)/shard_map/ppermute | solution.py:312
  2.1 7.0 %collective-permute-start.1 = (bf16[256,128]{1,0:T(8,128)(2,1)S(1)}, bf16[256,128]{1,0:T(8,128)(2,1)S(1)}, u32[]{:S(2)}, u32[]{:S(2)}) collective-permute-start(bf16[256,128]{1,0:T(8,128)(2,1)S(1)} %shard_map.167), channel_id=1, source_target_pairs={{0,2},{1,3},{2,0},{3,1},{4,6},{5,7},{6,4},{7,5},{8,10},{9,11},{10,... | collective-permute-start | bytes 196616 | tf_op jit(solution)/shard_map/ppermute | solution.py:311
  6.1 3.0 %collective-permute-start = (bf16[256,128]{1,0:T(8,128)(2,1)S(1)}, bf16[256,128]{1,0:T(8,128)(2,1)S(1)}, u32[]{:S(2)}, u32[]{:S(2)}) collective-permute-start(bf16[256,128]{1,0:T(8,128)(2,1)S(1)} %shard_map.167), channel_id=1, source_target_pairs={{0,1},{1,0},{2,3},{3,2},{4,5},{5,4},{6,7},{7,6},{8,9},{9,8},{10,11... | collective-permute-start | bytes 196616 | tf_op jit(solution)/shard_map/ppermute | solution.py:280
  6.2 3.0 %copy-start.1 = (bf16[2,128,128]{2,1,0:T(8,128)(2,1)S(1)}, bf16[2,128,128]{2,1,0:T(8,128)(2,1)}, u32[]{:S(2)}) copy-start(bf16[2,128,128]{2,1,0:T(8,128)(2,1)} %edge_in.1) | copy-start | bytes 196612
  6.2 3.0 %copy-start.2 = (bf16[2,128,128]{2,1,0:T(8,128)(2,1)S(1)}, bf16[2,128,128]{2,1,0:T(8,128)(2,1)}, u32[]{:S(2)}) copy-start(bf16[2,128,128]{2,1,0:T(8,128)(2,1)} %node_in.1) | copy-start | bytes 196612
  6.2 3.0 %copy-start.6 = (bf16[128,128]{1,0:T(8,128)(2,1)S(1)}, bf16[128,128]{1,0:T(8,128)(2,1)}, u32[]{:S(2)}) copy-start(bf16[128,128]{1,0:T(8,128)(2,1)} %edge_out.1) | copy-start | bytes 98308
  6.2 3.0 %copy-start.7 = (bf16[128,128]{1,0:T(8,128)(2,1)S(1)}, bf16[128,128]{1,0:T(8,128)(2,1)}, u32[]{:S(2)}) copy-start(bf16[128,128]{1,0:T(8,128)(2,1)} %node_out.1) | copy-start | bytes 98308
  6.2 3.0 %copy-start.9 = (bf16[64,128]{1,0:T(8,128)(2,1)S(1)}, bf16[64,128]{1,0:T(8,128)(2,1)}, u32[]{:S(2)}) copy-start(bf16[64,128]{1,0:T(8,128)(2,1)} %state.1) | copy-start | bytes 49156
  6.2 3.0 %copy-start.12 = (f32[128]{0:T(128)S(1)}, f32[128]{0:T(128)}, u32[]{:S(2)}) copy-start(f32[128]{0:T(128)} %param.22) | copy-start | bytes 1540
  6.2 3.0 %copy-start.13 = (f32[128]{0:T(128)S(1)}, f32[128]{0:T(128)}, u32[]{:S(2)}) copy-start(f32[128]{0:T(128)} %param.25) | copy-start | bytes 1540
  6.3 3.0 %copy-start.14 = (f32[128]{0:T(128)S(1)}, f32[128]{0:T(128)}, u32[]{:S(2)}) copy-start(f32[128]{0:T(128)} %param.27) | copy-start | bytes 1540
  13.4 1.5 %collective-permute-start.3 = (bf16[320,128]{1,0:T(8,128)(2,1)S(1)}, bf16[320,128]{1,0:T(8,128)(2,1)S(1)}, u32[]{:S(2)}, u32[]{:S(2)}) collective-permute-start(bf16[320,128]{1,0:T(8,128)(2,1)S(1)} %get-tuple-element.29.sums), channel_id=1, source_target_pairs={{0,1},{1,0},{2,3},{3,2},{4,5},{5,4},{6,7},{7,6},{8,9},{9,8},{10,11... | collective-permute-start | bytes 245768 | tf_op jit(solution)/shard_map/ppermute | solution.py:280
  14.9 3.6 %copy-start.3 = (bf16[2,128,128]{2,1,0:T(8,128)(2,1)S(1)}, bf16[2,128,128]{2,1,0:T(8,128)(2,1)}, u32[]{:S(2)}) copy-start(bf16[2,128,128]{2,1,0:T(8,128)(2,1)} %prolong_in.3) | copy-start | bytes 196612
  14.9 6.0 %copy-start.4 = (bf16[2,128,128]{2,1,0:T(8,128)(2,1)S(1)}, bf16[2,128,128]{2,1,0:T(8,128)(2,1)}, u32[]{:S(2)}) copy-start(bf16[2,128,128]{2,1,0:T(8,128)(2,1)} %coarse_w.1) | copy-start | bytes 196612
  14.9 6.0 %copy-start.8 = (bf16[128,128]{1,0:T(8,128)(2,1)S(1)}, bf16[128,128]{1,0:T(8,128)(2,1)}, u32[]{:S(2)}) copy-start(bf16[128,128]{1,0:T(8,128)(2,1)} %prolong_out.1) | copy-start | bytes 98308
  14.9 6.1 %copy-start.15 = (f32[128]{0:T(128)S(1)}, f32[128]{0:T(128)}, u32[]{:S(2)}) copy-start(f32[128]{0:T(128)} %param.28) | copy-start | bytes 1540
  14.9 6.0 %collective-permute-start.4 = (bf16[256,128]{1,0:T(8,128)(2,1)S(1)}, bf16[256,128]{1,0:T(8,128)(2,1)S(1)}, u32[]{:S(2)}, u32[]{:S(2)}) collective-permute-start(bf16[256,128]{1,0:T(8,128)(2,1)S(1)} %get-tuple-element.32), channel_id=1, source_target_pairs={{0,2},{1,3},{2,0},{3,1},{4,6},{5,7},{6,4},{7,5},{8,10},{9,11},{10,... | collective-permute-start | bytes 196616 | tf_op jit(solution)/shard_map/ppermute | solution.py:354
  16.5 4.4 %collective-permute-start.6 = (bf16[256,128]{1,0:T(8,128)(2,1)S(1)}, bf16[256,128]{1,0:T(8,128)(2,1)S(1)}, u32[]{:S(2)}, u32[]{:S(2)}) collective-permute-start(bf16[256,128]{1,0:T(8,128)(2,1)S(1)} %get-tuple-element.34), channel_id=1, source_target_pairs={{0,1},{1,0},{2,4},{3,5},{4,2},{5,3},{6,8},{7,9},{8,6},{9,7},{10,12... | collective-permute-start | bytes 196616 | tf_op jit(solution)/shard_map/ppermute | solution.py:356
  16.5 4.4 %collective-permute-start.5 = (bf16[64,128]{1,0:T(8,128)(2,1)S(1)}, bf16[64,128]{1,0:T(8,128)(2,1)S(1)}, u32[]{:S(2)}, u32[]{:S(2)}) collective-permute-start(bf16[64,128]{1,0:T(8,128)(2,1)S(1)} %get-tuple-element.33), channel_id=1, source_target_pairs={{0,4},{1,5},{2,6},{3,7},{4,0},{5,1},{6,2},{7,3},{8,12},{9,13},{10,... | collective-permute-start | bytes 49160 | tf_op jit(solution)/shard_map/ppermute | solution.py:355
  18.5 2.4 %collective-permute-start.7 = (bf16[64,128]{1,0:T(8,128)(2,1)S(1)}, bf16[64,128]{1,0:T(8,128)(2,1)S(1)}, u32[]{:S(2)}, u32[]{:S(2)}) collective-permute-start(bf16[64,128]{1,0:T(8,128)(2,1)S(1)} %get-tuple-element.35), channel_id=1, source_target_pairs={{0,1},{1,0},{2,3},{3,2},{4,8},{5,9},{6,10},{7,11},{8,4},{9,5},{10,... | collective-permute-start | bytes 49160 | tf_op jit(solution)/shard_map/ppermute | solution.py:357
